TPU v7x, 32 devices: a whole 2x2x4 slice. The times are simulated.
32 devices in a mesh: rows: 16 (over z, y, x), tp: 2 (over core).
Axes of the slice: x: 2, y: 2, z: 4, core: 2. Of those that a mesh axis runs over, the one named last changes fastest.
Arguments:
- tokens: bfloat16 [65536, 1024], P(('rows', 'tp')), may hold values from -6 to 6
- segment_ids: int32 [128, 512], P('rows'), may hold values from 0 to 7, never falling along the last dimension, each value on 1 to 256 neighbouring positions
- fill_counts: int32 [128], P('rows'), may hold values from 384 to 512
- qkv_weight: bfloat16 [3, 1024, 1024], P(None, 'rows', 'tp'), may hold values from -0.1875 to 0.1875
- qv_bias: bfloat16 [2, 1024], P(None, 'tp'), may hold values from -3 to 3
- out_weight: bfloat16 [1024, 1024], P('tp', 'rows'), may hold values from -0.75 to 0.75
- out_bias: bfloat16 [1024], replicated, may hold values from -3 to 3
- norm1_gain: bfloat16 [1024], replicated, may hold values from 0.099609375 to 1.8984375
- norm1_bias: bfloat16 [1024], replicated, may hold values from -3 to 3
- in_weight: bfloat16 [1024, 4096], P('rows', 'tp'), may hold values from -0.1875 to 0.1875
- in_bias: bfloat16 [4096], P('tp'), may hold values from -3 to 3
- down_weight: bfloat16 [4096, 1024], P('tp', 'rows'), may hold values from -0.09375 to 0.09375
- down_bias: bfloat16 [1024], replicated, may hold values from -3 to 3
- norm2_gain: bfloat16 [1024], replicated, may hold values from 0.099609375 to 1.8984375
- norm2_bias: bfloat16 [1024], replicated, may hold values from -3 to 3
- cotangent: bfloat16 [65536, 1024], P(('rows', 'tp')), may hold values from -6 to 6
Outputs:
- layer_out: bfloat16 [65536, 1024], P(('rows', 'tp'))
- tokens_grad: bfloat16 [65536, 1024], P(('rows', 'tp'))
- qv_bias_grad: float32 [2, 1024], replicated
- out_bias_grad: float32 [1024], replicated
- norm1_bias_grad: float32 [1024], replicated
- in_bias_grad: float32 [4096], replicated
- down_bias_grad: float32 [1024], replicated
- norm2_bias_grad: float32 [1024], replicated
Inputs may be any that keep to these rules, and one draw needn't show every extreme that they name: `segment_ids`: within a packed row the numbers never fall; each of the 8 documents of a row takes at least one slot and at most half of the 512 slots. Slots from fill_counts on are padding.
All inputs are finite; a program needn't handle non-finite values.
Results may differ from a plain program's by a relative error of at most 0.014.
Values may be sent and summed in bfloat16 or wider, within the bound.
No kernel may reach another device: no remote copies, remote signals or barrier semaphores. Data moves between devices by JAX's collectives and lax.ppermute only.
A program may use at most 256 MiB of HBM per device.

v0:
```python
from functools import partial
import math

import jax
import jax.numpy as jnp
from jax import lax
from jax.sharding import PartitionSpec as P

D = 1024
FF = 4096
HEAD_DIM = 64
SLOTS = 512


EPSILON = 1e-05
MASKED = -1e30


def norm_forward(summed, gain_vec, shift_vec):
    row_mean = jnp.mean(summed, -1, keepdims=True)
    centered = summed - row_mean
    inverse = lax.rsqrt(jnp.mean(centered * centered, -1, keepdims=True) + EPSILON)
    normal = centered * inverse
    return (normal * gain_vec + shift_vec, normal, inverse)


def norm_backward(grad_in, normal, inverse, gain_vec):
    scaled = grad_in * gain_vec
    return inverse * (
        scaled
        - jnp.mean(scaled, -1, keepdims=True)
        - normal * jnp.mean(scaled * normal, -1, keepdims=True)
    )


def allowed_pairs(segment, filled):
    places = lax.iota(jnp.int32, segment.shape[0])
    same_doc = segment[:, None] == segment[None, :]
    live_key = (places[None, :] < filled) | (places[:, None] == places[None, :])
    return same_doc & live_key


def row_scores(queries, key_rows, segment, filled, score_scale):
    scores = (
        jnp.einsum("qhd,khd->hqk", queries, key_rows, preferred_element_type=jnp.float32)
        * score_scale
    )
    return jnp.where(allowed_pairs(segment, filled)[None], scores, MASKED)


def attend_row(operands, score_scale):
    queries, key_rows, value_rows, segment, filled = operands
    scores = row_scores(queries, key_rows, segment, filled, score_scale)
    row_top = jnp.max(scores, -1, keepdims=True)
    exponent = jnp.exp(scores - row_top)
    row_total = jnp.sum(exponent, -1, keepdims=True)
    probs_low = (exponent / row_total).astype(jnp.bfloat16)
    context = jnp.einsum("hqk,khd->qhd", probs_low, value_rows, preferred_element_type=jnp.float32)
    return (context.astype(jnp.bfloat16), row_top[..., 0] + jnp.log(row_total[..., 0]))


def attend_back(operands, score_scale):
    queries, key_rows, value_rows, segment, filled, log_total, context_grad = operands
    scores = row_scores(queries, key_rows, segment, filled, score_scale)
    probs = jnp.exp(scores - log_total[..., None])
    probs_low = probs.astype(jnp.bfloat16)
    probs_grad = jnp.einsum(
        "qhd,khd->hqk", context_grad, value_rows, preferred_element_type=jnp.float32
    )
    value_grad = jnp.einsum(
        "hqk,qhd->khd", probs_low, context_grad, preferred_element_type=jnp.float32
    )
    scores_grad = (probs * (probs_grad - jnp.sum(probs * probs_grad, -1, keepdims=True))).astype(
        jnp.bfloat16
    )
    query_grad = (
        jnp.einsum("hqk,khd->qhd", scores_grad, key_rows, preferred_element_type=jnp.float32)
        * score_scale
    )
    key_grad = (
        jnp.einsum("hqk,qhd->khd", scores_grad, queries, preferred_element_type=jnp.float32)
        * score_scale
    )
    return (
        query_grad.astype(jnp.bfloat16),
        key_grad.astype(jnp.bfloat16),
        value_grad.astype(jnp.bfloat16),
    )


def exact_gelu(values):
    return jax.nn.gelu(values, approximate=False)


def contract_last(left_rows, right_rows):
    return lax.dot_general(
        left_rows, right_rows, (((1,), (1,)), ((), ())), preferred_element_type=jnp.float32
    )


def shards(
    tokens,
    segment_ids,
    fill_counts,
    qkv_weight,
    qv_bias,
    out_weight,
    out_bias,
    norm1_gain,
    norm1_bias,
    in_weight,
    in_bias,
    down_weight,
    down_bias,
    norm2_gain,
    norm2_bias,
    cotangent,
):
    score_scale = 1.0 / math.sqrt(HEAD_DIM)
    frozen = (
        lax.all_gather(qkv_weight, "rows", axis=1, tiled=True),
        lax.all_gather(out_weight, "rows", axis=1, tiled=True),
        lax.all_gather(in_weight, "rows", axis=0, tiled=True),
        lax.all_gather(down_weight, "rows", axis=1, tiled=True),
    )
    qkv_full, out_full, in_full, down_full = frozen
    bias_qv, bias_in = (qv_bias, in_bias)
    segments, fill_rows = (segment_ids, fill_counts)
    gathered = lax.all_gather(tokens, "tp", axis=0, tiled=True)
    column_start = lax.axis_index("tp") * qkv_full.shape[2]
    hidden_start = lax.axis_index("tp") * in_full.shape[1]
    local_width = qkv_full.shape[2]
    heads_here = local_width // HEAD_DIM
    rows_here = segments.shape[0]
    group_rows = gathered.shape[0]
    bias_qv = bias_qv.astype(jnp.float32)

    def by_rows(flat_rows):
        return flat_rows.reshape(rows_here, SLOTS, heads_here, HEAD_DIM)

    queries = (
        jnp.dot(gathered, qkv_full[0], preferred_element_type=jnp.float32) + bias_qv[0]
    ).astype(jnp.bfloat16)
    key_rows = jnp.dot(gathered, qkv_full[1], preferred_element_type=jnp.float32).astype(
        jnp.bfloat16
    )
    value_rows = (
        jnp.dot(gathered, qkv_full[2], preferred_element_type=jnp.float32) + bias_qv[1]
    ).astype(jnp.bfloat16)
    context, log_total = lax.map(
        partial(attend_row, score_scale=score_scale),
        (by_rows(queries), by_rows(key_rows), by_rows(value_rows), segments, fill_rows),
    )
    context = context.reshape(group_rows, local_width)
    attention = lax.psum_scatter(
        jnp.dot(context, out_full, preferred_element_type=jnp.float32),
        "tp",
        scatter_dimension=0,
        tiled=True,
    ) + out_bias.astype(jnp.float32)
    gain_one = norm1_gain.astype(jnp.float32)
    gain_two = norm2_gain.astype(jnp.float32)
    normed, normal_one, inverse_one = norm_forward(
        tokens.astype(jnp.float32) + attention, gain_one, norm1_bias.astype(jnp.float32)
    )
    normed_low = lax.all_gather(normed.astype(jnp.bfloat16), "tp", axis=0, tiled=True)
    inner_act = jnp.dot(normed_low, in_full, preferred_element_type=jnp.float32) + bias_in.astype(
        jnp.float32
    )
    activated = exact_gelu(inner_act).astype(jnp.bfloat16)
    branch = lax.psum_scatter(
        jnp.dot(activated, down_full, preferred_element_type=jnp.float32),
        "tp",
        scatter_dimension=0,
        tiled=True,
    ) + down_bias.astype(jnp.float32)
    final_out, normal_two, inverse_two = norm_forward(
        normed + branch, gain_two, norm2_bias.astype(jnp.float32)
    )
    layer_out = final_out.astype(jnp.bfloat16)
    final_grad = cotangent.astype(jnp.float32)
    sum_two_grad = norm_backward(final_grad, normal_two, inverse_two, gain_two)
    branch_grad = sum_two_grad.astype(jnp.bfloat16)
    act_grad = contract_last(lax.all_gather(branch_grad, "tp", axis=0, tiled=True), down_full)
    slope_grad = jax.vjp(exact_gelu, inner_act)[1](act_grad)[0]
    inner_grad = slope_grad.astype(jnp.bfloat16)
    normed_grad = (
        lax.psum_scatter(contract_last(inner_grad, in_full), "tp", scatter_dimension=0, tiled=True)
        + sum_two_grad
    )
    sum_one_grad = norm_backward(normed_grad, normal_one, inverse_one, gain_one)
    attention_own = sum_one_grad.astype(jnp.bfloat16)
    attention_grad = lax.all_gather(attention_own, "tp", axis=0, tiled=True)
    context_grad = contract_last(attention_grad, out_full).astype(jnp.bfloat16)
    query_grad, key_grad, value_grad = lax.map(
        partial(attend_back, score_scale=score_scale),
        (
            by_rows(queries),
            by_rows(key_rows),
            by_rows(value_rows),
            segments,
            fill_rows,
            log_total,
            by_rows(context_grad),
        ),
    )
    query_grad = query_grad.reshape(group_rows, local_width)
    key_grad = key_grad.reshape(group_rows, local_width)
    value_grad = value_grad.reshape(group_rows, local_width)
    total_term = contract_last(query_grad, qkv_full[0])
    total_term = total_term + contract_last(key_grad, qkv_full[1])
    tokens_grad = (
        lax.psum_scatter(
            (total_term + contract_last(value_grad, qkv_full[2])).astype(jnp.bfloat16),
            "tp",
            scatter_dimension=0,
            tiled=True,
        ).astype(jnp.float32)
        + sum_one_grad
    ).astype(jnp.bfloat16)
    qv_local = jnp.stack(
        [jnp.sum(query_grad, 0, dtype=jnp.float32), jnp.sum(value_grad, 0, dtype=jnp.float32)]
    )
    qv_term = lax.dynamic_update_slice(
        jnp.zeros((2, D), jnp.float32), qv_local, (jnp.int32(0), column_start)
    )
    in_term = lax.dynamic_update_slice(
        jnp.zeros((FF,), jnp.float32), jnp.sum(inner_grad, 0, dtype=jnp.float32), (hidden_start,)
    )
    summed_biases = lax.psum(
        (
            qv_term,
            jnp.sum(attention_own, 0, dtype=jnp.float32),
            jnp.sum(normed_grad, 0),
            in_term,
            jnp.sum(branch_grad, 0, dtype=jnp.float32),
            jnp.sum(final_grad, 0),
        ),
        ("rows", "tp"),
    )
    return (
        layer_out,
        tokens_grad,
        summed_biases[0],
        summed_biases[1],
        summed_biases[2],
        summed_biases[3],
        summed_biases[4],
        summed_biases[5],
    )


def solution(mesh):
    return jax.shard_map(
        shards,
        mesh=mesh,
        in_specs=(
            P(("rows", "tp"), None),
            P("rows", None),
            P("rows"),
            P(None, "rows", "tp"),
            P(None, "tp"),
            P("tp", "rows"),
            P(),
            P(),
            P(),
            P("rows", "tp"),
            P("tp"),
            P("tp", "rows"),
            P(),
            P(),
            P(),
            P(("rows", "tp"), None),
        ),
        out_specs=(P(("rows", "tp"), None), P(("rows", "tp"), None), P(), P(), P(), P(), P(), P()),
        check_vma=False,
    )
```

profile of v0, /device:TPU:0, one launch (start us, length us, event | category | flops | bytes accessed | tf_op | source)
XLA Modules:
  0.0 1106.1 jit_solution(3398719385189300666)
XLA Ops:
  10.2 70.9 %all-gather.11.cloned.1.call-done = bf16[3,1024,512]{2,1,0:T(8,128)(2,1)} async-done(((bf16[3,64,512]{2,1,0:T(8,128)(2,1)}), bf16[3,1024,512]{2,1,0:T(8,128)(2,1)}) %all-gather.11.cloned.1.call-update) | async-done | bytes 3145744 | tf_op jit(solution)/shard_map/all_gather | solution.py:121
  81.1 20.5 %all-gather.9.cloned.1.call-done = bf16[4096,1024]{1,0:T(8,128)(2,1)} async-done(((bf16[2048,1024]{1,0:T(8,128)(2,1)}), bf16[4096,1024]{1,0:T(8,128)(2,1)}) %all-gather.9.cloned.1.call-update) | async-done | bytes 8388624 | tf_op jit(solution)/shard_map/all_gather | solution.py:129
  101.6 10.2 add_convert_fusion.5
  111.8 11.5 %reshape.252 = bf16[8,512,8,64]{3,2,1,0:T(8,128)(2,1)} reshape(bf16[4096,512]{1,0:T(8,128)(2,1)} %add_convert_fusion.5) | data formatting | bytes 8388608 | tf_op jit(solution)/shard_map/reshape | solution.py:139
  123.2 9.9 copy.42
  133.1 9.4 add_convert_fusion.4
  142.6 11.3 %reshape.253 = bf16[8,512,8,64]{3,2,1,0:T(8,128)(2,1)} reshape(bf16[4096,512]{1,0:T(8,128)(2,1)} %add_convert_fusion.4) | data formatting | bytes 8388608 | tf_op jit(solution)/shard_map/reshape | solution.py:139
  153.8 9.7 copy.43
  163.6 9.4 convolution_convert_fusion.1
  173.0 11.2 %reshape.254 = bf16[8,512,8,64]{3,2,1,0:T(8,128)(2,1)} reshape(bf16[4096,512]{1,0:T(8,128)(2,1)} %convolution_convert_fusion.1) | data formatting | bytes 8388608 | tf_op jit(solution)/shard_map/reshape | solution.py:139
  184.2 9.7 copy.44
  196.4 92.6 %while.26 = (s32[]{:T(128)}, bf16[8,512,8,64]{1,3,2,0:T(8,128)(2,1)}, f32[8,8,512]{2,1,0:T(8,128)}, bf16[8,512,8,64]{1,3,2,0:T(8,128)(2,1)}, s32[8,512]{1,0:T(8,...) while((s32[]{:T(128)}, ...), condition=%wide.region_3.4_spmd, body=%wide.region_0.3_spmd.sunk | while | flops 563343872 | bytes 28452464 | solution.py:150
  298.1 12.8 %fusion.89 = f32[4096,1024]{1,0:T(8,128)} fusion(bf16[4096,512]{0,1:T(8,128)(2,1)} %bitcast.171, bf16[512,1024]{0,1:T(8,128)(2,1)} %all-gather.13.cloned.1.call-done), kind=kOutput, calls=%fused_computation.143 | convolution fusion | flops 4294967296 | bytes 22020096 | tf_op jit(solution)/shard_map/dot_general | solution.py:156
  311.6 26.9 %reduce-scatter.5.cloned.1.call-done = f32[2048,1024]{1,0:T(8,128)} async-done(((f32[4096,1024]{1,0:T(8,128)}), f32[2048,1024]{1,0:T(8,128)}) %reduce-scatter.5.cloned.1.call-update) | async-done | bytes 8388624 | tf_op jit(solution)/shard_map/reduce_scatter | solution.py:155
  351.9 67.0 %all-gather.17.cloned.1.call-done = bf16[1024,2048]{1,0:T(8,128)(2,1)} async-done(((bf16[64,2048]{1,0:T(8,128)(2,1)}), bf16[1024,2048]{1,0:T(8,128)(2,1)}) %all-gather.17.cloned.1.call-update) | async-done | bytes 4194320 | tf_op jit(solution)/shard_map/all_gather | solution.py:123
  418.9 20.5 %all-gather.15.cloned.1.call-done = bf16[4096,1024]{1,0:T(8,128)(2,1)} async-done(((bf16[2048,1024]{1,0:T(8,128)(2,1)}), bf16[4096,1024]{1,0:T(8,128)(2,1)}) %all-gather.15.cloned.1.call-update) | async-done | bytes 8388624 | tf_op jit(solution)/shard_map/all_gather | solution.py:166
  439.4 89.2 %fusion.63 = (f32[4096,2048]{1,0:T(8,128)}, f32[4096,2048]{1,0:T(8,128)}) fusion(f32[2048]{0:T(1024)S(1)} %convert_element_type.128, bf16[4096,1024]{1,0:T(8,128)(2,1)} %all-gather.15.cloned.1.call-done, bf16[1024,2048]{1,0:T(8,128)(2,1)} %all-gather.17.cloned.1.call-done), kind=kOutput, calls=%fused_computation.73 | convolution fusion | flops 17708351488 | bytes 79699968 | tf_op jit(solution)/shard_map/dot_general | solution.py:167
  528.6 31.9 %fusion.69 = f32[4096,1024]{1,0:T(8,128)} fusion(bf16[2048,1024]{0,1:T(8,128)(2,1)} %all-gather.19.cloned.1.call-done, f32[4096,2048]{1,0:T(8,128)} %get-tuple-element.220, f32[4096,2048]{1,0:T(8,128)} %get-tuple-element.221, f32[2048]{0:T(1024)S(1)} %convert_element_type.128), kind=kOutput, calls=%fused_computation.90 | convolution fusion | flops 17213423616 | bytes 88088576 | tf_op jit(solution)/shard_map/dot_general | solution.py:172
  561.2 27.0 %reduce-scatter.7.cloned.1.call-done = f32[2048,1024]{1,0:T(8,128)} async-done(((f32[4096,1024]{1,0:T(8,128)}), f32[2048,1024]{1,0:T(8,128)}) %reduce-scatter.7.cloned.1.call-update) | async-done | bytes 8388624 | tf_op jit(solution)/shard_map/reduce_scatter | solution.py:171
  610.5 21.2 %all-gather.21.cloned.1.call-done = bf16[4096,1024]{1,0:T(8,128)(2,1)} async-done(((bf16[2048,1024]{1,0:T(8,128)(2,1)}), bf16[4096,1024]{1,0:T(8,128)(2,1)}) %all-gather.21.cloned.1.call-update) | async-done | bytes 8388624 | tf_op jit(solution)/shard_map/all_gather | solution.py:184
  631.7 42.0 %convert_reduce_fusion = (f32[2048]{0:T(1024)}, bf16[4096,2048]{1,0:T(8,128)(2,1)}) fusion(f32[4096,2048]{1,0:T(8,128)} %get-tuple-element.220, bf16[4096,1024]{1,0:T(8,128)(2,1)} %all-gather.21.cloned.1.call-done, bf16[2048,1024]{0,1:T(8,128)(2,1)} %all-gather.19.cloned.1.call-done, f32[4096,2048]{1,0:T(8,128)} %get-tuple-element.221, ...), kind=kOutput, calls=%fused_computation.74 | convolution fusion | flops 17322473472 | bytes 96485376 | tf_op jit(solution)/shard_map/dot_general | solution.py:96
  673.7 23.5 %fusion.90 = f32[4096,1024]{1,0:T(8,128)} fusion(bf16[4096,2048]{1,0:T(8,128)(2,1)} %get-tuple-element.223, bf16[1024,2048]{1,0:T(8,128)(2,1)} %all-gather.17.cloned.1.call-done), kind=kOutput, calls=%fused_computation.144 | convolution fusion | flops 17179869184 | bytes 37748736 | tf_op jit(solution)/shard_map/dot_general | solution.py:96
  697.9 26.9 %reduce-scatter.9.cloned.1.call-done = f32[2048,1024]{1,0:T(8,128)} async-done(((f32[4096,1024]{1,0:T(8,128)}), f32[2048,1024]{1,0:T(8,128)}) %reduce-scatter.9.cloned.1.call-update) | async-done | bytes 8388624 | tf_op jit(solution)/shard_map/reduce_scatter | solution.py:188
  724.8 14.3 %multiply_reduce_fusion.4 = (f32[2048]{0:T(1024)S(1)}, f32[2048]{0:T(1024)S(1)}, f32[1024]{0:T(1024)}, f32[2048,1024]{1,0:T(8,128)S(1)}, bf16[2048,1024]{1,0:T(8,128)(2,1)}) fusion(f32[1024]{0:T(1024)S(1)} %copy-done.11, f32[2048]{0:T(1024)S(1)} %copy-done.9, f32[2048,1024]{1,0:T(8,128)} %copy-done, f32[2048]{0:T(1024)S(1)} %copy-done.7, ...), kind=kLoop, calls=%fused_computation.120 | loop fusion | flops 39840768 | bytes 42024960 | tf_op jit(solution)/shard_map/reduce_sum | solution.py:31
  739.1 10.2 convert_reduce_fusion.3
  749.4 21.2 %all-gather.23.cloned.1.call-done = bf16[4096,1024]{1,0:T(8,128)(2,1)} async-done(((bf16[2048,1024]{1,0:T(8,128)(2,1)}), bf16[4096,1024]{1,0:T(8,128)(2,1)}) %all-gather.23.cloned.1.call-update) | async-done | bytes 8388624 | tf_op jit(solution)/shard_map/all_gather | solution.py:193
  770.6 9.6 convolution_convert_fusion
  780.2 11.2 %reshape.251 = bf16[8,512,8,64]{3,2,1,0:T(8,128)(2,1)} reshape(bf16[4096,512]{1,0:T(8,128)(2,1)} %convolution_convert_fusion) | data formatting | bytes 8388608 | tf_op jit(solution)/shard_map/reshape | solution.py:139
  791.4 9.7 copy.49
  808.6 177.4 %while.27 = (s32[]{:T(128)}, bf16[8,512,8,64]{1,3,2,0:T(8,128)(2,1)}, bf16[8,512,8,64]{1,3,2,0:T(8,128)(2,1)}, bf16[8,512,8,64]{1,3,2,0:T(8,128)(2,1)}, bf16[8,5...) while((s32[]{:T(128)}, ...), condition=%wide.region_17.18_spmd, body=%wide.region_15.17_spmd.sunk | while | flops 1375990272 | bytes 69333128 | solution.py:195
  1024.0 18.2 %add_convert_fusion.1 = bf16[4096,1024]{1,0:T(8,128)(2,1)} fusion(f32[4096,1024]{1,0:T(8,128)} %fusion.79, f32[4096,1024]{1,0:T(8,128)} %fusion.80, bf16[4096,512]{0,1:T(8,128)(2,1)} %bitcast.164, bf16[3,1024,512]{2,1,0:T(8,128)(2,1)S(1)} %copy-done.5), kind=kOutput, calls=%fused_computation.91 | convolution fusion | flops 4307550208 | bytes 47185920 | tf_op jit(solution)/shard_map/dot_general | solution.py:96
  1049.1 41.8 %all-reduce = (f32[2,1024]{1,0:T(2,128)}, f32[1024]{0:T(1024)}, f32[1024]{0:T(1024)}, f32[4096]{0:T(1024)}, f32[1024]{0:T(1024)}, /*index=5*/f32[1024]{0:T(1024)}) all-reduce(f32[2,1024]{1,0:T(2,128)S(1)} %maximum_dynamic-update-slice_fusion, f32[1024]{0:T(1024)S(1)} %copy-done.16, ...), channel_id=1, replica_groups=mesh['rows'=16,'tp'=2] {'rows','tp'}, use_global_device_ids=true, to_apply=%region_21.22 | all-reduce | flops 10240 | bytes 81920 | tf_op jit(solution)/shard_map/psum | solution.py:230
  (283 shorter events, 381.1 us)
Async XLA Ops:
  7.2 73.9 %all-gather.11.cloned.1.call-start = ((), (), s32[]{:S(2)}) async-start(), calls=%async_computation.5 | async-start | bytes 3342336 | tf_op jit(solution)/shard_map/all_gather | solution.py:121
  7.9 93.7 %all-gather.9.cloned.1.call-start = ((), (), s32[]{:S(2)}) async-start(), calls=%async_computation.4 | async-start | bytes 12582912 | tf_op jit(solution)/shard_map/all_gather | solution.py:129
  8.6 289.4 %all-gather.13.cloned.1.call-start = ((), (), s32[]{:S(2)}) async-start(), calls=%async_computation.6 | async-start | bytes 1114112 | tf_op jit(solution)/shard_map/all_gather | solution.py:122
  9.4 329.2 %reduce-scatter.5.cloned.1.call-start = ((), (), s32[]{:S(2)}) async-start(), calls=%async_computation.7 | async-start | bytes 25165824 | tf_op jit(solution)/shard_map/reduce_scatter | solution.py:155
  123.2 9.9 copy-start.4
  184.2 12.3 %copy-start.27 = (s32[8]{0:T(128)S(1)}, s32[8]{0:T(128)}, u32[]{:S(2)}) copy-start(s32[8]{0:T(128)} %param.22) | copy-start | bytes 100
  310.9 108.0 %all-gather.17.cloned.1.call-start = ((), (), s32[]{:S(2)}) async-start(), calls=%async_computation.9 | async-start | bytes 4456448 | tf_op jit(solution)/shard_map/all_gather | solution.py:123
  311.5 127.9 %all-gather.15.cloned.1.call-start = ((), (), s32[]{:S(2)}) async-start(), calls=%async_computation.8 | async-start | bytes 12582912 | tf_op jit(solution)/shard_map/all_gather | solution.py:166
  311.6 34.0 %copy-start.10 = (f32[1024]{0:T(1024)}, f32[1024]{0:T(1024)S(1)}, u32[]{:S(2)}) copy-start(f32[1024]{0:T(1024)S(1)} %convert_element_type.125) | copy-start | bytes 12292
  311.6 34.0 %copy-start.12 = (f32[1024]{0:T(1024)}, f32[1024]{0:T(1024)S(1)}, u32[]{:S(2)}) copy-start(f32[1024]{0:T(1024)S(1)} %convert_element_type.126) | copy-start | bytes 12292
  344.3 3.3 copy-start.6
  348.2 3.6 copy-start.19
  351.1 177.6 %all-gather.19.cloned.1.call-start = ((), (), s32[]{:S(2)}) async-start(), calls=%async_computation.10 | async-start | bytes 4456448 | tf_op jit(solution)/shard_map/all_gather | solution.py:124
  351.8 236.4 %reduce-scatter.7.cloned.1.call-start = ((), (), s32[]{:S(2)}) async-start(), calls=%async_computation.11 | async-start | bytes 25165824 | tf_op jit(solution)/shard_map/reduce_scatter | solution.py:171
  560.5 27.7 %copy-start.7 = (f32[2048]{0:T(1024)S(1)}, f32[2048]{0:T(1024)}, u32[]{:S(2)}) copy-start(f32[2048]{0:T(1024)} %copy-done.6) | copy-start | bytes 24580
  560.5 27.7 %copy-start.9 = (f32[2048]{0:T(1024)S(1)}, f32[2048]{0:T(1024)}, u32[]{:S(2)}) copy-start(f32[2048]{0:T(1024)} %copy-done.8) | copy-start | bytes 24580
  560.6 27.6 %copy-start.11 = (f32[1024]{0:T(1024)S(1)}, f32[1024]{0:T(1024)}, u32[]{:S(2)}) copy-start(f32[1024]{0:T(1024)} %copy-done.10) | copy-start | bytes 12292
  560.6 27.6 %copy-start.13 = (f32[1024]{0:T(1024)S(1)}, f32[1024]{0:T(1024)}, u32[]{:S(2)}) copy-start(f32[1024]{0:T(1024)} %copy-done.12) | copy-start | bytes 12292
  560.6 71.1 %all-gather.21.cloned.1.call-start = ((), (), s32[]{:S(2)}) async-start(), calls=%async_computation.12 | async-start | bytes 12582912 | tf_op jit(solution)/shard_map/all_gather | solution.py:184
  595.3 10.3 copy-start.1
  595.3 5.2 copy-start.3
  610.4 114.4 %reduce-scatter.9.cloned.1.call-start = ((), (), s32[]{:S(2)}) async-start(), calls=%async_computation.13 | async-start | bytes 25165824 | tf_op jit(solution)/shard_map/reduce_scatter | solution.py:188
  697.2 73.4 %all-gather.23.cloned.1.call-start = ((), (), s32[]{:S(2)}) async-start(), calls=%async_computation.14 | async-start | bytes 12582912 | tf_op jit(solution)/shard_map/all_gather | solution.py:193
  739.1 31.5 %copy-start.26 = (bf16[512,1024]{0,1:T(8,128)(2,1)S(1)}, bf16[512,1024]{0,1:T(8,128)(2,1)}, u32[]{:S(2)}) copy-start(bf16[512,1024]{0,1:T(8,128)(2,1)} %all-gather.13.cloned.1.call-done) | copy-start | bytes 3145732
  749.4 341.5 %reduce-scatter.11.cloned.1.call-start = ((), (), s32[]{:S(2)}) async-start(), calls=%async_computation.15 | async-start | bytes 12582912 | tf_op jit(solution)/shard_map/reduce_scatter | solution.py:213
  801.1 7.5 copy-start.28
  986.0 7.1 copy-start.2
  998.0 9.6 copy-start.5
  1042.2 6.8 copy-start.14
  1042.2 6.9 copy-start.15
  1042.2 6.9 copy-start.16
  1042.3 6.9 copy-start.17
  (9 other events, 8.7 us)
Sparse Core Ops, SparseCore 0:
  10.8 70.2 all-gather.10
  82.6 18.9 all-gather.8
  104.4 56.4 all-gather.12
  311.0 27.4 reduce-scatter.4
  341.5 77.3 all-gather.16
  420.9 18.4 all-gather.14
  442.6 77.2 all-gather.18
  560.7 27.4 reduce-scatter.6
  610.5 21.0 all-gather.20
  697.3 27.4 reduce-scatter.8
  749.5 21.0 all-gather.22
  1042.4 18.0 reduce-scatter.10
where the time goes:
time: 1120 us; the launch traced here: 1110 us
  matrix products  461 us (41%)
  waiting for transfers between devices  306 us (27%)
  local copies, waits for them, and re-layouts  161 us (14%)
  other arithmetic  120 us (11%)
  blocking collectives  41.8 us (4%)
  between operations  14.8 us (1%)
    dot_general x6, matrix products, contract_last(): lax.dot_general(left_rows, right_rows, (((1,), (1,)), ((), ())), preferre...  110 us
    dot_general x1, matrix products, shards(): jnp.dot(normed_low, in_full, preferred_element_type=jnp.float32)  89.2 us
    all_gather x1, waiting for transfers between devices, shards(): lax.all_gather(qkv_weight, 'rows', axis=1, tiled=True)  70.9 us
    all_gather x1, waiting for transfers between devices, shards(): lax.all_gather(in_weight, 'rows', axis=0, tiled=True)  67 us
    reshape x4, local copies, waits for them, and re-layouts, by_rows(): return flat_rows.reshape(rows_here, SLOTS, heads_here, HEAD_DIM)  45.2 us
    psum x1, blocking collectives, shards(): lax.psum((qv_term, jnp.sum(attention_own, 0, dtype=jnp.float32), jnp.sum(...  41.8 us
    dot_general x16, matrix products, row_scores(): jnp.einsum('qhd,khd->hqk', queries, key_rows, preferred_element_type=jnp....  41.5 us
    while x4, local copies, waits for them, and re-layouts, shards(): lax.map(partial(attend_row, score_scale=score_scale), (by_rows(queries),...  34.1 us
  transfers between devices with their start and end apart: 12, of which 9 were waited for; matrix products, arithmetic and copies ran while one was open for 27% of the time, Pallas kernels for 0%

commit v1 on v0

v1 whole, which is shorter than its diff:
```python
import math

import jax
import jax.numpy as jnp
from jax import lax
from jax.experimental import pallas as pl
from jax.experimental.pallas import tpu as pltpu
from jax.sharding import PartitionSpec as P

D = 1024
FF = 4096
HEADS = 16
HEAD_DIM = 64
SLOTS = 512
GROUP = 4
WIDE = GROUP * HEAD_DIM
PAIR = 2 * HEAD_DIM
GROUPS = HEADS // GROUP
TILE = 256
HIDDEN = 512
EPSILON = 1e-05
MASKED = -1e30
SCALE = 1.0 / math.sqrt(HEAD_DIM)
VMEM_BYTES = 60 * 2**20

NN = (((1,), (0,)), ((), ()))
NT = (((1,), (1,)), ((), ()))


def mul(left, right, dims=NN):
    return lax.dot_general(left, right, dims, preferred_element_type=jnp.float32)


def low(values):
    return values.astype(jnp.bfloat16)


def wide(values):
    return values.astype(jnp.float32)


def norm_forward(summed, gain_vec, shift_vec):
    row_mean = jnp.mean(summed, -1, keepdims=True)
    centered = summed - row_mean
    inverse = lax.rsqrt(jnp.mean(centered * centered, -1, keepdims=True) + EPSILON)
    normal = centered * inverse
    return (normal * gain_vec + shift_vec, normal, inverse)


def norm_backward(grad_in, normal, inverse, gain_vec):
    scaled = grad_in * gain_vec
    return inverse * (
        scaled
        - jnp.mean(scaled, -1, keepdims=True)
        - normal * jnp.mean(scaled * normal, -1, keepdims=True)
    )


def mask_bias(seg_col, seg_row, filled):
    keys = lax.broadcasted_iota(jnp.int32, (SLOTS, SLOTS), 0)
    places = lax.broadcasted_iota(jnp.int32, (SLOTS, SLOTS), 1)
    allowed = (seg_col == seg_row) & ((keys < filled) | (keys == places))
    return jnp.where(allowed, 0.0, MASKED)


def half_rows(rows, head):
    zeros = jnp.zeros((HEAD_DIM, rows.shape[1]), rows.dtype)
    return jnp.concatenate([rows, zeros] if head % 2 == 0 else [zeros, rows], 0)


def attend_kernel(fill_ref, x_ref, segc_ref, segr_ref, w_ref, b_ref, qkv_ref, ctx_ref, lse_ref, bias_ref):
    row = pl.program_id(0)

    @pl.when(pl.program_id(1) == 0)
    def _():
        bias_ref[...] = mask_bias(segc_ref[0], segr_ref[0], fill_ref[row])

    x = x_ref[...]
    weight = [w_ref[:, 0, i].reshape(D, WIDE) for i in range(3)]
    q = low(mul(x, weight[0]) + b_ref[0:1, :])
    k = low(mul(x, weight[1]))
    v = low(mul(x, weight[2]) + b_ref[1:2, :])
    qkv_ref[0] = q
    qkv_ref[1] = k
    qkv_ref[2] = v
    q_t = (q * jnp.bfloat16(SCALE)).T
    v_t = v.T
    ones = jnp.ones((HEAD_DIM, SLOTS), jnp.bfloat16)
    context = []
    for head in range(GROUP):
        own = slice(head * HEAD_DIM, (head + 1) * HEAD_DIM)
        pair = slice(head // 2 * PAIR, (head // 2 + 1) * PAIR)
        scores = mul(k[:, pair], half_rows(q_t[own], head)) + bias_ref[...]
        top = jnp.max(scores, 0, keepdims=True)
        probs = low(jnp.exp(scores - top))
        out = mul(jnp.concatenate([v_t[own], ones], 0), probs)
        total = out[HEAD_DIM : HEAD_DIM + 1]
        context.append(low(out[:HEAD_DIM] / total))
        lse_ref[0, 0, head : head + 1, :] = top + jnp.log(total)
    ctx_ref[...] = jnp.concatenate(context, 0).T


def attend_back_kernel(
    fill_ref, qkv_ref, ctx_ref, dctx_ref, lse_ref, segc_ref, segr_ref, w_ref, sum_ref, out_ref, qvb_ref, bias_ref, acc_ref
):
    row = pl.program_id(0)
    group = pl.program_id(1)

    @pl.when(group == 0)
    def _():
        bias_ref[...] = mask_bias(segc_ref[0], segr_ref[0], fill_ref[row])
        acc_ref[...] = wide(sum_ref[...])

    @pl.when((group == 0) & (row == 0))
    def _():
        qvb_ref[...] = jnp.zeros_like(qvb_ref)

    q = qkv_ref[0]
    k = qkv_ref[1]
    v = qkv_ref[2]
    d_out = dctx_ref[...]
    product = wide(d_out) * wide(ctx_ref[...])
    high = low(product)
    rest = low(product - wide(high))
    picks = lax.broadcasted_iota(jnp.int32, (16, WIDE), 1) // HEAD_DIM
    picks = low(jnp.where(picks == lax.broadcasted_iota(jnp.int32, (16, WIDE), 0), 1.0, 0.0))
    delta = mul(picks, high, NT) + mul(picks, rest, NT)
    q_t = (q * jnp.bfloat16(SCALE)).T
    k_t = k.T
    d_out_t = d_out.T
    d_q, d_k, d_v = [], [], []
    for head in range(GROUP):
        own = slice(head * HEAD_DIM, (head + 1) * HEAD_DIM)
        pair = slice(head // 2 * PAIR, (head // 2 + 1) * PAIR)
        scores = mul(k[:, pair], half_rows(q_t[own], head)) + bias_ref[...]
        probs = jnp.exp(scores - lse_ref[0, 0, head : head + 1, :])
        probs_grad = mul(v[:, pair], half_rows(d_out_t[own], head))
        scores_grad = low(probs * (probs_grad - delta[head : head + 1]))
        probs_low = low(probs)
        d_v.append(low(mul(d_out_t[own], probs_low, NT)))
        d_k.append(low(mul(q_t[own], scores_grad, NT)))
        d_q.append(low(mul(k_t[own], scores_grad) * SCALE))
    d_q = jnp.concatenate(d_q, 0).T
    d_k = jnp.concatenate(d_k, 0).T
    d_v = jnp.concatenate(d_v, 0).T
    columns = pl.ds(pl.multiple_of(group * WIDE, WIDE), WIDE)
    qvb_ref[0:1, columns] += jnp.sum(wide(d_q), 0, keepdims=True)
    qvb_ref[1:2, columns] += jnp.sum(wide(d_v), 0, keepdims=True)
    total = acc_ref[...]
    for i, grad in enumerate((d_q, d_k, d_v)):
        total = total + mul(grad, w_ref[:, 0, i].reshape(D, WIDE), NT)
    acc_ref[...] = total

    @pl.when(group == GROUPS - 1)
    def _():
        out_ref[...] = low(total)


def gelu_and_slope(v):
    phi = 0.5 * (1.0 + lax.erf(v * math.sqrt(0.5)))
    bell = jnp.exp(-0.5 * v * v) * (1.0 / math.sqrt(2.0 * math.pi))
    return v * phi, phi + v * bell


def feed_kernel(
    x_ref, ctx_ref, ct_ref, wo_ref, wi_ref, wd_ref, vec_ref, bi_ref,
    out_ref, dctx_ref, sum_ref, vecg_ref, big_ref, slope_ref,
):
    @pl.when(pl.program_id(0) == 0)
    def _():
        vecg_ref[...] = jnp.zeros_like(vecg_ref)
        big_ref[...] = jnp.zeros_like(big_ref)

    out_bias, gain_one, bias_one, down_bias, gain_two, bias_two = [vec_ref[i : i + 1, :] for i in range(6)]
    half = D // 2
    hidden = FF // 2
    ctx = ctx_ref[...]
    out_w = [wo_ref[:, t].reshape(D, half) for t in range(2)]
    attention = mul(ctx[:, :half], out_w[0], NT) + mul(ctx[:, half:], out_w[1], NT) + out_bias
    normed, normal_one, inverse_one = norm_forward(wide(x_ref[...]) + attention, gain_one, bias_one)
    normed_low = low(normed)
    branch = normed + down_bias
    chunks = [(t, c) for t in range(2) for c in range(hidden // HIDDEN)]
    for t, c in chunks:
        part = slice(c * HIDDEN, (c + 1) * HIDDEN)
        flat = slice(t * hidden + c * HIDDEN, t * hidden + (c + 1) * HIDDEN)
        inner = mul(normed_low, wi_ref[:, t, :, part].reshape(D, HIDDEN)) + bi_ref[0:1, flat]
        act, slope = gelu_and_slope(inner)
        slope_ref[:, flat] = low(slope)
        branch = branch + mul(low(act), wd_ref[:, t, :, part].reshape(D, HIDDEN), NT)
    final, normal_two, inverse_two = norm_forward(branch, gain_two, bias_two)
    out_ref[...] = low(final)
    final_grad = wide(ct_ref[...])
    sum_two = norm_backward(final_grad, normal_two, inverse_two, gain_two)
    branch_grad = low(sum_two)
    normed_grad = sum_two
    for t, c in chunks:
        part = slice(c * HIDDEN, (c + 1) * HIDDEN)
        flat = slice(t * hidden + c * HIDDEN, t * hidden + (c + 1) * HIDDEN)
        act_grad = mul(branch_grad, wd_ref[:, t, :, part].reshape(D, HIDDEN))
        inner_grad = low(act_grad * wide(slope_ref[:, flat]))
        big_ref[0:1, flat] += jnp.sum(wide(inner_grad), 0, keepdims=True)
        normed_grad = normed_grad + mul(inner_grad, wi_ref[:, t, :, part].reshape(D, HIDDEN), NT)
    sum_one = low(norm_backward(normed_grad, normal_one, inverse_one, gain_one))
    sum_ref[...] = sum_one
    for t in range(2):
        dctx_ref[:, t * half : (t + 1) * half] = low(mul(sum_one, out_w[t]))
    sums = (wide(sum_one), normed_grad, wide(branch_grad), final_grad)
    for i, term in enumerate(sums):
        vecg_ref[i : i + 1, :] += jnp.sum(term, 0, keepdims=True)


def params(grid_rank):
    return pltpu.CompilerParams(
        dimension_semantics=("arbitrary",) * grid_rank, vmem_limit_bytes=VMEM_BYTES
    )


def attend(tokens, seg_col, seg_row, fills, w_qkv, b_qv):
    rows = tokens.shape[0] // SLOTS
    n = w_qkv.shape[0]
    chunk = w_qkv.shape[3]
    return pl.pallas_call(
        attend_kernel,
        grid=(rows, GROUPS),
        in_specs=[
            pl.BlockSpec(memory_space=pltpu.SMEM),
            pl.BlockSpec((SLOTS, D), lambda r, g: (r, 0)),
            pl.BlockSpec((1, SLOTS, 1), lambda r, g: (r, 0, 0)),
            pl.BlockSpec((1, 1, SLOTS), lambda r, g: (r, 0, 0)),
            pl.BlockSpec((n, 1, 3, chunk, WIDE), lambda r, g: (0, g // 2, 0, 0, g % 2)),
            pl.BlockSpec((2, WIDE), lambda r, g: (0, g)),
        ],
        out_specs=[
            pl.BlockSpec((3, SLOTS, WIDE), lambda r, g: (0, r, g)),
            pl.BlockSpec((SLOTS, WIDE), lambda r, g: (r, g)),
            pl.BlockSpec((1, 1, GROUP, SLOTS), lambda r, g: (r, g, 0, 0)),
        ],
        out_shape=[
            jax.ShapeDtypeStruct((3, rows * SLOTS, D), jnp.bfloat16),
            jax.ShapeDtypeStruct((rows * SLOTS, D), jnp.bfloat16),
            jax.ShapeDtypeStruct((rows, GROUPS, GROUP, SLOTS), jnp.float32),
        ],
        scratch_shapes=[pltpu.VMEM((SLOTS, SLOTS), jnp.float32)],
        compiler_params=params(2),
        name="attend",
    )(fills, tokens, seg_col, seg_row, w_qkv, b_qv)


def attend_back(qkv, context, context_grad, lse, seg_col, seg_row, fills, w_qkv, sum_one):
    rows = context.shape[0] // SLOTS
    n = w_qkv.shape[0]
    chunk = w_qkv.shape[3]
    return pl.pallas_call(
        attend_back_kernel,
        grid=(rows, GROUPS),
        in_specs=[
            pl.BlockSpec(memory_space=pltpu.SMEM),
            pl.BlockSpec((3, SLOTS, WIDE), lambda r, g: (0, r, g)),
            pl.BlockSpec((SLOTS, WIDE), lambda r, g: (r, g)),
            pl.BlockSpec((SLOTS, WIDE), lambda r, g: (r, g)),
            pl.BlockSpec((1, 1, GROUP, SLOTS), lambda r, g: (r, g, 0, 0)),
            pl.BlockSpec((1, SLOTS, 1), lambda r, g: (r, 0, 0)),
            pl.BlockSpec((1, 1, SLOTS), lambda r, g: (r, 0, 0)),
            pl.BlockSpec((n, 1, 3, chunk, WIDE), lambda r, g: (0, g // 2, 0, 0, g % 2)),
            pl.BlockSpec((SLOTS, D), lambda r, g: (r, 0)),
        ],
        out_specs=[
            pl.BlockSpec((SLOTS, D), lambda r, g: (r, 0)),
            pl.BlockSpec((8, D), lambda r, g: (0, 0)),
        ],
        out_shape=[
            jax.ShapeDtypeStruct((rows * SLOTS, D), jnp.bfloat16),
            jax.ShapeDtypeStruct((8, D), jnp.float32),
        ],
        scratch_shapes=[
            pltpu.VMEM((SLOTS, SLOTS), jnp.float32),
            pltpu.VMEM((SLOTS, D), jnp.float32),
        ],
        compiler_params=params(2),
        name="attend_back",
    )(fills, qkv, context, context_grad, lse, seg_col, seg_row, w_qkv, sum_one)


def feed(tokens, context, cotangent, w_out, w_in, w_down, vectors, in_bias):
    count = tokens.shape[0]
    tile = pl.BlockSpec((TILE, D), lambda i: (i, 0))

    def whole(array):
        return pl.BlockSpec(array.shape, lambda i: (0,) * array.ndim, pipeline_mode=pl.Buffered(1))

    return pl.pallas_call(
        feed_kernel,
        grid=(count // TILE,),
        in_specs=[tile, tile, tile] + [whole(a) for a in (w_out, w_in, w_down, vectors, in_bias)],
        out_specs=[
            tile,
            tile,
            tile,
            pl.BlockSpec((8, D), lambda i: (0, 0)),
            pl.BlockSpec((8, FF), lambda i: (0, 0)),
        ],
        out_shape=[
            jax.ShapeDtypeStruct((count, D), jnp.bfloat16),
            jax.ShapeDtypeStruct((count, D), jnp.bfloat16),
            jax.ShapeDtypeStruct((count, D), jnp.bfloat16),
            jax.ShapeDtypeStruct((8, D), jnp.float32),
            jax.ShapeDtypeStruct((8, FF), jnp.float32),
        ],
        scratch_shapes=[pltpu.VMEM((TILE, FF), jnp.bfloat16)],
        compiler_params=params(1),
        name="feed",
    )(tokens, context, cotangent, w_out, w_in, w_down, vectors, in_bias)


def layer(tokens, cotangent, segments, fills, w_qkv, w_out, w_in, w_down, b_qv, vectors, in_bias):
    seg_col = segments[:, :, None]
    seg_row = segments[:, None, :]
    qkv, context, lse = attend(tokens, seg_col, seg_row, fills, w_qkv, b_qv)
    layer_out, context_grad, sum_one, vec_grads, in_grads = feed(
        tokens, context, cotangent, w_out, w_in, w_down, vectors, in_bias
    )
    tokens_grad, qv_grads = attend_back(
        qkv, context, context_grad, lse, seg_col, seg_row, fills, w_qkv, sum_one
    )
    return layer_out, tokens_grad, qv_grads, vec_grads, in_grads


def shards(
    tokens,
    segment_ids,
    fill_counts,
    qkv_weight,
    qv_bias,
    out_weight,
    out_bias,
    norm1_gain,
    norm1_bias,
    in_weight,
    in_bias,
    down_weight,
    down_bias,
    norm2_gain,
    norm2_bias,
    cotangent,
):
    n = lax.axis_size("rows")
    core = lax.axis_index("tp")
    rows_here = tokens.shape[0] // SLOTS
    segments = lax.dynamic_slice_in_dim(segment_ids, core * rows_here, rows_here, 0)
    fills = lax.dynamic_slice_in_dim(fill_counts, core * rows_here, rows_here, 0)

    def gather(shard):
        whole = lax.all_gather(shard, ("rows", "tp"), axis=0, tiled=False)
        return whole.reshape((n, 2) + shard.shape)

    w_qkv = gather(qkv_weight)
    w_out = gather(out_weight.T)
    w_in = gather(in_weight)
    w_down = gather(down_weight.T)

    own = jnp.concatenate([qv_bias.reshape(-1), in_bias])
    other = lax.ppermute(own, "tp", [(0, 1), (1, 0)])
    both = jnp.where(core == 0, jnp.stack([own, other]), jnp.stack([other, own])).astype(jnp.float32)
    width = qv_bias.shape[1]
    b_qv = both[:, : 2 * width].reshape(2, 2, width).transpose(1, 0, 2).reshape(2, 2 * width)
    b_in = both[:, 2 * width :].reshape(1, -1)
    vectors = wide(
        jnp.stack([out_bias, norm1_gain, norm1_bias, down_bias, norm2_gain, norm2_bias, out_bias, out_bias])
    )
    layer_out, tokens_grad, qv_grads, vec_grads, in_grads = layer(
        tokens, cotangent, segments, fills, w_qkv, w_out, w_in, w_down, b_qv, vectors, b_in
    )
    qv, vec, hid = lax.psum((qv_grads[:2], vec_grads[:4], in_grads[0]), ("rows", "tp"))
    return (layer_out, tokens_grad, qv, vec[0], vec[1], hid, vec[2], vec[3])


def solution(mesh):
    return jax.shard_map(
        shards,
        mesh=mesh,
        in_specs=(
            P(("rows", "tp"), None),
            P("rows", None),
            P("rows"),
            P(None, "rows", "tp"),
            P(None, "tp"),
            P("tp", "rows"),
            P(),
            P(),
            P(),
            P("rows", "tp"),
            P("tp"),
            P("tp", "rows"),
            P(),
            P(),
            P(),
            P(("rows", "tp"), None),
        ),
        out_specs=(P(("rows", "tp"), None), P(("rows", "tp"), None), P(), P(), P(), P(), P(), P()),
        check_vma=False,
    )
```

time: 1120 us -> 535 us (0.48); the launches traced: 1110 us -> 534 us
  matrix products: 461 us -> 0 us
  Pallas kernels: 0 us -> 239 us
  local copies, waits for them, and re-layouts: 161 us -> 12.3 us
  other arithmetic: 120 us -> 0.68 us
  waiting for transfers between devices: 306 us -> 228 us
    dot_general x68 -> x0, matrix products: 461 us -> none  [the longest x6 110 us: contract_last(): lax.dot_general(left_rows, right_rows, (((1,), (1,)), ((), ())), preferre...]
    pallas_call x0 -> x3, Pallas kernels: none -> 239 us  [the longest x1 116 us: feed(): pl.pallas_call(feed_kernel, grid=(count // TILE,), in_specs=[tile, tile,...]
    reduce_scatter x4 -> x0, waiting for transfers between devices: 80.8 us -> none  [the longest x1 27 us: shards(): lax.psum_scatter(jnp.dot(activated, down_full, preferred_element_type=jnp...]
    reduce_sum x18 -> x0, other arithmetic: 69 us -> none  [the longest x2 19.4 us: norm_backward(): jnp.mean(scaled, -1, keepdims=True)]
    while x8 -> x0, local copies, waits for them, and re-layouts: 56.5 us -> none  [the longest x4 34.1 us: shards(): lax.map(partial(attend_row, score_scale=score_scale), (by_rows(queries),...]
    reshape x4 -> x0, local copies, waits for them, and re-layouts: 45.2 us -> none  [by_rows(): return flat_rows.reshape(rows_here, SLOTS, heads_here, HEAD_DIM)]
    convert_element_type x17 -> x2, other arithmetic: 32.2 us -> 0.68 us  [the longest x1 0.62 us: wide(): return values.astype(jnp.float32)]
    unnamed x62 -> x11, local copies, waits for them, and re-layouts: 21.6 us -> 1.94 us
  transfers between devices with their start and end apart: 12 -> 5, of which waited for: 9 -> 4; matrix products, arithmetic and copies ran while one was open for 27% -> 2% of each run, Pallas kernels for 0% -> 10%
where the time goes in v1:
time: 535 us; the launch traced here: 534 us
  Pallas kernels  239 us (45%)
  waiting for transfers between devices  228 us (43%)
  blocking collectives  40.4 us (8%)
  between operations  13.9 us (3%)
  local copies, waits for them, and re-layouts  12.3 us (2%)
    all_gather x4, waiting for transfers between devices, gather(): whole = lax.all_gather(shard, ('rows', 'tp'), axis=0, tiled=False)  225 us
    pallas_call x1, Pallas kernels, feed(): pl.pallas_call(feed_kernel, grid=(count // TILE,), in_specs=[tile, tile,...  116 us
    pallas_call x1, Pallas kernels, attend_back(): pl.pallas_call(attend_back_kernel, grid=(rows, GROUPS), in_specs=[pl.Bloc...  69.5 us
    pallas_call x1, Pallas kernels, attend(): pl.pallas_call(attend_kernel, grid=(rows, GROUPS), in_specs=[pl.BlockSpec...  52.7 us
    psum x1, blocking collectives, shards(): lax.psum((qv_grads[:2], vec_grads[:4], in_grads[0]), ('rows', 'tp'))  40.4 us
  transfers between devices with their start and end apart: 5, of which 4 were waited for; matrix products, arithmetic and copies ran while one was open for 2% of the time, Pallas kernels for 10%

profile of v1, /device:TPU:0, one launch (start us, length us, event | category | flops | bytes accessed | tf_op | source)
XLA Modules:
  0.0 534.1 jit_solution(8670739017576843680)
XLA Ops:
  7.2 0.7 all-gather.9.cloned.1.call-update
  8.0 0.7 all-gather.11.cloned.1.call-update
  8.7 0.7 all-gather.13.cloned.1.call-update
  9.4 0.5 all-gather.15.cloned.1.call-update
  10.0 0.7 copy.31
  10.7 0.7 constant_dynamic-update-slice_fusion
  11.4 0.5 collective-permute-start
  11.9 1.2 dynamic_slice.6.fill_ref
  13.1 0.7 stack.41
  13.8 0.7 stack.42
  14.5 0.7 stack.43
  15.2 0.7 stack.44
  15.8 0.7 stack.45
  16.5 0.7 stack.46
  17.2 0.6 broadcast_in_dim.7.segr_ref
  17.8 0.1 stack.47
  17.9 0.6 convert_element_type.7.vec_ref
  18.5 1.4 copy.29.segc_ref
  19.9 0.1 fusion
  20.0 0.6 copy.33
  20.6 0.6 copy.32
  21.2 61.9 %all-gather.9.cloned.1.call-done = bf16[96,64,512]{2,1,0:T(8,128)(2,1)} async-done(((bf16[3,64,512]{2,1,0:T(8,128)(2,1)}), bf16[96,64,512]{2,1,0:T(8,128)(2,1)}) %all-gather.9.cloned.1.call-update) | async-done | bytes 6291472 | tf_op jit(solution)/shard_map/all_gather | solution.py:354
  83.1 52.7 %attend.1 = (bf16[3,2048,1024]{2,1,0:T(8,128)(2,1)}, bf16[2048,1024]{1,0:T(8,128)(2,1)}, f32[4,4,4,512]{3,2,1,0:T(4,128)}) custom-call(s32[4]{0:T(128)} %dynamic_slice.6.fill_ref, bf16[2048,1024]{1,0:T(8,128)(2,1)} %x_ref.3, s32[4,512,1]{2,1,0:T(8,128)} %copy.29.segc_ref, s32[4,1,512]{2,1,0:T(1,128)} %broadcast_in_dim.7.segr_ref, ...), custom_call_target="tpu_custom_call" | custom-call | tf_op jit(solution)/shard_map/attend/pallas_call | solution.py:223
  135.8 5.1 all-gather.11.cloned.1.call-done
  140.9 79.2 %all-gather.13.cloned.1.call-done = bf16[2048,2048]{1,0:T(8,128)(2,1)} async-done(((bf16[64,2048]{1,0:T(8,128)(2,1)}), bf16[2048,2048]{1,0:T(8,128)(2,1)}) %all-gather.13.cloned.1.call-update) | async-done | bytes 8388624 | tf_op jit(solution)/shard_map/all_gather | solution.py:354
  220.1 78.8 %all-gather.15.cloned.1.call-done = bf16[2048,2048]{1,0:T(8,128)(2,1)} async-done(((bf16[64,2048]{1,0:T(8,128)(2,1)}), bf16[2048,2048]{1,0:T(8,128)(2,1)}) %all-gather.15.cloned.1.call-update) | async-done | bytes 8388624 | tf_op jit(solution)/shard_map/all_gather | solution.py:354
  298.9 116.4 %feed.1 = (bf16[2048,1024]{1,0:T(8,128)(2,1)}, bf16[2048,1024]{1,0:T(8,128)(2,1)}, bf16[2048,1024]{1,0:T(8,128)(2,1)}, f32[8,1024]{1,0:T(8,128)}, f32[8,4096]{1,0:T(8,128)}) custom-call(bf16[2048,1024]{1,0:T(8,128)(2,1)} %x_ref.3, bf16[2048,1024]{1,0:T(8,128)(2,1)} %get-tuple-element.18.ctx_ref, bf16[2048,1024]{1,0:T(8,128)(2,1)} %ct_ref.1, ...), custom_call_target="tpu_custom_call" | custom-call | tf_op jit(solution)/shard_map/feed/pallas_call | solution.py:292
  415.3 69.5 %attend_back.1 = (bf16[2048,1024]{1,0:T(8,128)(2,1)}, f32[8,1024]{1,0:T(8,128)}) custom-call(s32[4]{0:T(128)} %dynamic_slice.6.fill_ref, bf16[3,2048,1024]{2,1,0:T(8,128)(2,1)} %get-tuple-element.20.qkv_ref, bf16[2048,1024]{1,0:T(8,128)(2,1)} %get-tuple-element.18.ctx_ref, bf16[2048,1024]{1,0:T(8,128)(2,1)} %get-tuple-element.21.dctx_ref, ...), custom_call_target="tpu_custom_call" | custom-call | tf_op jit(solution)/shard_map/attend_back/pallas_call | solution.py:254
  484.8 0.8 slice.29
  485.6 0.9 slice.33
  486.5 40.4 %all-reduce = (f32[2,1024]{1,0:T(2,128)}, f32[4,1024]{1,0:T(4,128)S(1)}, f32[4096]{0:T(1024)}) all-reduce(f32[2,1024]{1,0:T(2,128)S(1)} %slice.29, f32[4,1024]{1,0:T(4,128)S(1)} %slice.30, f32[4096]{0:T(1024)S(1)} %bitcast.32), channel_id=1, replica_groups=mesh['rows'=16,'tp'=2] {'rows','tp'}, use_global_device_ids=true, to_apply=%region_0.1 | all-reduce | flops 10240 | bytes 81920 | tf_op jit(solution)/shard_map/psum | solution.py:374
  526.9 0.6 fusion.1
  (19 shorter events, 0.2 us)
Async XLA Ops:
  7.2 4.6 copy-start
  7.2 75.9 %all-gather.9.cloned.1.call-start = ((), (), s32[]{:S(2)}) async-start(), calls=%async_computation | async-start | bytes 6488064 | tf_op jit(solution)/shard_map/all_gather | solution.py:354
  7.9 133.0 %all-gather.11.cloned.1.call-start = ((), (), s32[]{:S(2)}) async-start(), calls=%async_computation.1 | async-start | bytes 2162688 | tf_op jit(solution)/shard_map/all_gather | solution.py:354
  8.7 211.4 %all-gather.13.cloned.1.call-start = ((), (), s32[]{:S(2)}) async-start(), calls=%async_computation.2 | async-start | bytes 8650752 | tf_op jit(solution)/shard_map/all_gather | solution.py:354
  9.4 289.5 %all-gather.15.cloned.1.call-start = ((), (), s32[]{:S(2)}) async-start(), calls=%async_computation.3 | async-start | bytes 8650752 | tf_op jit(solution)/shard_map/all_gather | solution.py:354
  11.4 8.5 %collective-permute-start = (bf16[3072]{0:T(1024)(128)(2,1)S(1)}, bf16[3072]{0:T(1024)(128)(2,1)S(1)}, u32[]{:S(2)}, u32[]{:S(2)}) collective-permute-start(bf16[3072]{0:T(1024)(128)(2,1)S(1)} %constant_dynamic-update-slice_fusion), channel_id=1, source_target_pairs={{0,1},{1,0},{2,3},{3,2},{4,5},{5,4},{6,7},{7,6},{8,9},{9,8},{10,11... | collective-permute-start | bytes 18440 | tf_op jit(solution)/shard_map/ppermute | solution.py:363
  415.3 70.3 %copy-start.2 = (f32[8,1024]{1,0:T(8,128)S(1)}, f32[8,1024]{1,0:T(8,128)}, u32[]{:S(2)}) copy-start(f32[8,1024]{1,0:T(8,128)} %get-tuple-element.26) | copy-start | bytes 98308
  415.3 112.3 %copy-start.1 = (s32[8,512]{1,0:T(8,128)S(1)}, s32[8,512]{1,0:T(8,128)}, u32[]{:S(2)}) copy-start(s32[8,512]{1,0:T(8,128)} %param.17) | copy-start | bytes 49156
Sparse Core Ops, SparseCore 0:
  10.9 72.1 all-gather.8
  86.0 54.8 all-gather.10
  143.8 76.2 all-gather.12
  222.8 76.0 all-gather.14

commit v2 on v1

v2 whole, which is shorter than its diff:
```python
from functools import partial
import math

import jax
import jax.numpy as jnp
from jax import lax
from jax.experimental import pallas as pl
from jax.experimental.pallas import tpu as pltpu
from jax.sharding import PartitionSpec as P

D = 1024
FF = 4096
HEADS = 16
HEAD_DIM = 64
SLOTS = 512
GROUP = 4
WIDE = GROUP * HEAD_DIM
PAIR = 2 * HEAD_DIM
GROUPS = HEADS // GROUP
TILE = 256
HIDDEN = 512
EPSILON = 1e-05
MASKED = -1e30
SCALE = 1.0 / math.sqrt(HEAD_DIM)
VMEM_BYTES = 60 * 2**20

NN = (((1,), (0,)), ((), ()))
NT = (((1,), (1,)), ((), ()))


def mul(left, right, dims=NN):
    return lax.dot_general(left, right, dims, preferred_element_type=jnp.float32)


def low(values):
    return values.astype(jnp.bfloat16)


def wide(values):
    return values.astype(jnp.float32)


def norm_forward(summed, gain_vec, shift_vec):
    row_mean = jnp.mean(summed, -1, keepdims=True)
    centered = summed - row_mean
    inverse = lax.rsqrt(jnp.mean(centered * centered, -1, keepdims=True) + EPSILON)
    normal = centered * inverse
    return (normal * gain_vec + shift_vec, normal, inverse)


def norm_backward(grad_in, normal, inverse, gain_vec):
    scaled = grad_in * gain_vec
    return inverse * (
        scaled
        - jnp.mean(scaled, -1, keepdims=True)
        - normal * jnp.mean(scaled * normal, -1, keepdims=True)
    )


def mask_bias(seg_col, seg_row, filled):
    keys = lax.broadcasted_iota(jnp.int32, (SLOTS, SLOTS), 0)
    places = lax.broadcasted_iota(jnp.int32, (SLOTS, SLOTS), 1)
    allowed = (seg_col == seg_row) & ((keys < filled) | (keys == places))
    return jnp.where(allowed, 0.0, MASKED)


def half_rows(rows, head):
    zeros = jnp.zeros((HEAD_DIM, rows.shape[1]), rows.dtype)
    return jnp.concatenate([rows, zeros] if head % 2 == 0 else [zeros, rows], 0)


def fetch(refs, scratch, sem, columns=None):
    copies = []
    half = len(refs) // 2
    for i, ref in enumerate(refs):
        size = ref.shape[0]
        if columns is not None:
            ref = ref.at[:, :, :, columns]
        target = scratch.at[i // half, pl.ds(i % half * size, size)]
        copies.append(pltpu.make_async_copy(ref, target, sem.at[i]))
        copies[-1].start()
    return copies


def set_weight(w_ref, slot_ref, other, part, columns=slice(None)):
    parts = [w_ref[slot_ref[other, c], part, :, columns] for c in range(w_ref.shape[0])]
    return jnp.concatenate(parts, 0)


def columns_of(w_ref, slot_ref, other, columns):
    there = w_ref.at[other]
    return jnp.concatenate([there[slot_ref[other, c], :, columns] for c in range(there.shape[0])], 0)


def attend_kernel(step, count, fill_ref, slot_ref, x_ref, segc_ref, segr_ref, b_ref, *rest):
    qkv_ref, ctx_ref, lse_ref, w_ref, sem = rest[-5:]

    @pl.when(pl.program_id(0) == 0)
    def _():
        copies = []
        for i, ref in enumerate(rest[:count]):
            size = ref.shape[0]
            source = ref.at[:, :, :, pl.ds(step % 2 * WIDE, WIDE)]
            copies.append(pltpu.make_async_copy(source, w_ref.at[pl.ds(i * size, size)], sem.at[i]))
            copies[-1].start()
        for copy in copies:
            copy.wait()

    x = x_ref[...]
    weight = [set_weight(w_ref, slot_ref, step // 2, i) for i in range(3)]
    bias = mask_bias(segc_ref[0], segr_ref[0], fill_ref[pl.program_id(0)])
    q = low(mul(x, weight[0]) + b_ref[0:1, :])
    k = low(mul(x, weight[1]))
    v = low(mul(x, weight[2]) + b_ref[1:2, :])
    qkv_ref[0] = q
    qkv_ref[1] = k
    qkv_ref[2] = v
    q_t = (q * jnp.bfloat16(SCALE)).T
    v_t = v.T
    ones = jnp.ones((HEAD_DIM, SLOTS), jnp.bfloat16)
    context = []
    for head in range(GROUP):
        own = slice(head * HEAD_DIM, (head + 1) * HEAD_DIM)
        pair = slice(head // 2 * PAIR, (head // 2 + 1) * PAIR)
        scores = mul(k[:, pair], half_rows(q_t[own], head)) + bias
        top = jnp.max(scores, 0, keepdims=True)
        probs = low(jnp.exp(scores - top))
        out = mul(jnp.concatenate([v_t[own], ones], 0), probs)
        total = out[HEAD_DIM : HEAD_DIM + 1]
        context.append(low(out[:HEAD_DIM] / total))
        lse_ref[0, 0, head : head + 1, :] = top + jnp.log(total)
    ctx_ref[...] = jnp.concatenate(context, 0).T


def attend_back_kernel(
    count, fill_ref, slot_ref, qkv_ref, ctx_ref, dctx_ref, lse_ref, segc_ref, segr_ref, *rest
):
    sum_ref, out_ref, qvb_ref, bias_ref, acc_ref, w_ref, sem = rest[-7:]
    row = pl.program_id(0)
    group = pl.program_id(1)

    @pl.when(group == 0)
    def _():
        bias_ref[...] = mask_bias(segc_ref[0], segr_ref[0], fill_ref[row])
        acc_ref[...] = wide(sum_ref[...])

    @pl.when((group == 0) & (row == 0))
    def _():
        qvb_ref[...] = jnp.zeros_like(qvb_ref)
        for copy in fetch(rest[:count], w_ref, sem):
            copy.wait()

    q = qkv_ref[0]
    k = qkv_ref[1]
    v = qkv_ref[2]
    d_out = dctx_ref[...]
    product = wide(d_out) * wide(ctx_ref[...])
    high = low(product)
    rest = low(product - wide(high))
    picks = lax.broadcasted_iota(jnp.int32, (16, WIDE), 1) // HEAD_DIM
    picks = low(jnp.where(picks == lax.broadcasted_iota(jnp.int32, (16, WIDE), 0), 1.0, 0.0))
    delta = mul(picks, high, NT) + mul(picks, rest, NT)
    q_t = (q * jnp.bfloat16(SCALE)).T
    k_t = k.T
    d_out_t = d_out.T
    d_q, d_k, d_v = [], [], []
    for head in range(GROUP):
        own = slice(head * HEAD_DIM, (head + 1) * HEAD_DIM)
        pair = slice(head // 2 * PAIR, (head // 2 + 1) * PAIR)
        scores = mul(k[:, pair], half_rows(q_t[own], head)) + bias_ref[...]
        probs = jnp.exp(scores - lse_ref[0, 0, head : head + 1, :])
        probs_grad = mul(v[:, pair], half_rows(d_out_t[own], head))
        scores_grad = low(probs * (probs_grad - delta[head : head + 1]))
        probs_low = low(probs)
        d_v.append(low(mul(d_out_t[own], probs_low, NT)))
        d_k.append(low(mul(q_t[own], scores_grad, NT)))
        d_q.append(low(mul(k_t[own], scores_grad) * SCALE))
    d_q = jnp.concatenate(d_q, 0).T
    d_k = jnp.concatenate(d_k, 0).T
    d_v = jnp.concatenate(d_v, 0).T
    columns = pl.ds(pl.multiple_of(group * WIDE, WIDE), WIDE)
    qvb_ref[0:1, columns] += jnp.sum(wide(d_q), 0, keepdims=True)
    qvb_ref[1:2, columns] += jnp.sum(wide(d_v), 0, keepdims=True)
    half_set = pl.ds(pl.multiple_of(group % 2 * WIDE, WIDE), WIDE)
    total = acc_ref[...]
    for i, grad in enumerate((d_q, d_k, d_v)):
        weight = set_weight(w_ref.at[group // 2], slot_ref, group // 2, i, half_set)
        total = total + mul(grad, weight, NT)
    acc_ref[...] = total

    @pl.when(group == GROUPS - 1)
    def _():
        out_ref[...] = low(total)


def gelu_and_slope(v):
    phi = 0.5 * (1.0 + lax.erf(v * math.sqrt(0.5)))
    bell = jnp.exp(-0.5 * v * v) * (1.0 / math.sqrt(2.0 * math.pi))
    return v * phi, phi + v * bell


FLAT = 1024
PIECES = 2 * FLAT // HIDDEN


def piece_weight(first_ref, late_ref, slot_ref, piece, down):
    ref, width = (first_ref, FLAT) if piece < PIECES else (late_ref, FF // 2 - FLAT)
    other, start = divmod(piece % PIECES * HIDDEN, width)
    return columns_of(ref, slot_ref, other, pl.ds(down * width + start, HIDDEN))


def out_columns(first_ref, slot_ref, group):
    return columns_of(first_ref, slot_ref, group // 2, pl.ds(2 * FLAT + group % 2 * WIDE, WIDE))


def vectors_of(vec_ref):
    return [vec_ref[i : i + 1, :] for i in range(6)]


def front_kernel(count, slot_ref, x_ref, ctx_ref, vec_ref, bi_ref, *rest):
    normal_ref, inv_ref, branch_ref, slope_ref, first_ref, sem = rest[-6:]

    @pl.when(pl.program_id(0) == 0)
    def _():
        for copy in fetch(rest[:count], first_ref, sem):
            copy.wait()

    out_bias, gain_one, bias_one, down_bias, _, _ = vectors_of(vec_ref)
    ctx = ctx_ref[...]
    attention = out_bias
    for group in range(GROUPS):
        columns = slice(group * WIDE, (group + 1) * WIDE)
        attention = attention + mul(ctx[:, columns], out_columns(first_ref, slot_ref, group), NT)
    normed, normal_one, inverse_one = norm_forward(wide(x_ref[...]) + attention, gain_one, bias_one)
    normal_ref[...] = normal_one
    inv_ref[...] = jnp.broadcast_to(inverse_one, inv_ref.shape)
    normed_low = low(normed)
    branch = normed + down_bias
    for piece in range(PIECES):
        flat = slice(piece * HIDDEN, (piece + 1) * HIDDEN)
        inner = mul(normed_low, piece_weight(first_ref, None, slot_ref, piece, 0)) + bi_ref[0:1, flat]
        act, slope = gelu_and_slope(inner)
        slope_ref[:, flat] = low(slope)
        branch = branch + mul(low(act), piece_weight(first_ref, None, slot_ref, piece, 1), NT)
    branch_ref[...] = branch


def back_kernel(
    counts, slot_ref, normal_ref, inv_ref, branch_ref, slope_ref, ct_ref, vec_ref, bi_ref, *rest
):
    out_ref, dctx_ref, sum_ref, vecg_ref, big_ref, keep_ref, first_ref, first_sem, late_ref, late_sem = rest[-10:]

    @pl.when(pl.program_id(0) == 0)
    def _():
        vecg_ref[...] = jnp.zeros_like(vecg_ref)
        big_ref[...] = jnp.zeros_like(big_ref)
        late = fetch(rest[counts[0] : sum(counts)], late_ref, late_sem)
        for copy in late + fetch(rest[: counts[0]], first_ref, first_sem):
            copy.wait()

    _, gain_one, bias_one, _, gain_two, bias_two = vectors_of(vec_ref)
    weight = partial(piece_weight, first_ref, late_ref, slot_ref)
    normal_one = normal_ref[...]
    inverse_one = inv_ref[:, 0:1]
    normed_low = low(normal_one * gain_one + bias_one)
    branch = branch_ref[...]
    for piece in range(PIECES, FF // HIDDEN):
        flat = slice(piece * HIDDEN, (piece + 1) * HIDDEN)
        inner = mul(normed_low, weight(piece, 0)) + bi_ref[0:1, flat]
        act, slope = gelu_and_slope(inner)
        keep_ref[:, (piece - PIECES) * HIDDEN : (piece - PIECES + 1) * HIDDEN] = low(slope)
        branch = branch + mul(low(act), weight(piece, 1), NT)
    final, normal_two, inverse_two = norm_forward(branch, gain_two, bias_two)
    out_ref[...] = low(final)
    final_grad = wide(ct_ref[...])
    sum_two = norm_backward(final_grad, normal_two, inverse_two, gain_two)
    branch_grad = low(sum_two)
    normed_grad = sum_two
    for piece in range(FF // HIDDEN):
        flat = slice(piece * HIDDEN, (piece + 1) * HIDDEN)
        if piece < PIECES:
            slope = slope_ref[:, flat]
        else:
            slope = keep_ref[:, (piece - PIECES) * HIDDEN : (piece - PIECES + 1) * HIDDEN]
        inner_grad = low(mul(branch_grad, weight(piece, 1)) * wide(slope))
        big_ref[0:1, flat] += jnp.sum(wide(inner_grad), 0, keepdims=True)
        normed_grad = normed_grad + mul(inner_grad, weight(piece, 0), NT)
    sum_one = low(norm_backward(normed_grad, normal_one, inverse_one, gain_one))
    sum_ref[...] = sum_one
    for group in range(GROUPS):
        columns = slice(group * WIDE, (group + 1) * WIDE)
        dctx_ref[:, columns] = low(mul(sum_one, out_columns(first_ref, slot_ref, group)))
    sums = (wide(sum_one), normed_grad, wide(branch_grad), final_grad)
    for i, term in enumerate(sums):
        vecg_ref[i : i + 1, :] += jnp.sum(term, 0, keepdims=True)


def params(grid_rank):
    return pltpu.CompilerParams(
        dimension_semantics=("arbitrary",) * grid_rank, vmem_limit_bytes=VMEM_BYTES
    )


def cost(flops, moved):
    return pl.CostEstimate(flops=int(flops), bytes_accessed=int(moved), transcendentals=0)


SCALARS = pl.BlockSpec(memory_space=pltpu.SMEM)
ANYWHERE = pl.BlockSpec(memory_space=pl.ANY)


def whole(array):
    return pl.BlockSpec(array.shape, lambda *_: (0,) * array.ndim, pipeline_mode=pl.Buffered(1))


def slot_scratch(pieces):
    half = len(pieces) // 2
    n = sum(w.shape[0] for w in pieces[:half])
    return [
        pltpu.VMEM((2, n) + pieces[0].shape[1:], pieces[0].dtype),
        pltpu.SemaphoreType.DMA((len(pieces),)),
    ]


def attend(step, earlier, tokens, seg_col, seg_row, fills, slots, pieces, bias):
    rows = tokens.shape[0] // SLOTS
    return pl.pallas_call(
        partial(attend_kernel, step, len(pieces)),
        grid=(rows,),
        in_specs=[
            SCALARS,
            SCALARS,
            pl.BlockSpec((SLOTS, D), lambda r: (r, 0)),
            pl.BlockSpec((1, SLOTS, 1), lambda r: (r, 0, 0)),
            pl.BlockSpec((1, 1, SLOTS), lambda r: (r, 0, 0)),
            whole(bias),
        ]
        + [ANYWHERE] * (len(pieces) + len(earlier)),
        out_specs=[
            pl.BlockSpec((3, SLOTS, WIDE), lambda r: (0, r, step)),
            pl.BlockSpec((SLOTS, WIDE), lambda r: (r, step)),
            pl.BlockSpec((1, 1, GROUP, SLOTS), lambda r: (r, step, 0, 0)),
        ],
        out_shape=[
            jax.ShapeDtypeStruct((3, rows * SLOTS, D), jnp.bfloat16),
            jax.ShapeDtypeStruct((rows * SLOTS, D), jnp.bfloat16),
            jax.ShapeDtypeStruct((rows, GROUPS, GROUP, SLOTS), jnp.float32),
        ],
        scratch_shapes=[
            pltpu.VMEM((sum(w.shape[0] for w in pieces),) + pieces[0].shape[1:3] + (WIDE,), jnp.bfloat16),
            pltpu.SemaphoreType.DMA((len(pieces),)),
        ],
        input_output_aliases={6 + len(pieces) + i: i for i in range(len(earlier))},
        compiler_params=params(1),
        cost_estimate=cost(15e9, 10e6),
        name="attend",
    )(fills, slots, tokens, seg_col, seg_row, bias, *pieces, *earlier)


def attend_back(qkv, context, context_grad, lse, seg_col, seg_row, fills, slots, weights, sum_one):
    rows = context.shape[0] // SLOTS
    return pl.pallas_call(
        partial(attend_back_kernel, len(weights)),
        grid=(rows, GROUPS),
        in_specs=[
            SCALARS,
            SCALARS,
            pl.BlockSpec((3, SLOTS, WIDE), lambda r, g: (0, r, g)),
            pl.BlockSpec((SLOTS, WIDE), lambda r, g: (r, g)),
            pl.BlockSpec((SLOTS, WIDE), lambda r, g: (r, g)),
            pl.BlockSpec((1, 1, GROUP, SLOTS), lambda r, g: (r, g, 0, 0)),
            pl.BlockSpec((1, SLOTS, 1), lambda r, g: (r, 0, 0)),
            pl.BlockSpec((1, 1, SLOTS), lambda r, g: (r, 0, 0)),
        ]
        + [ANYWHERE] * len(weights)
        + [pl.BlockSpec((SLOTS, D), lambda r, g: (r, 0))],
        out_specs=[
            pl.BlockSpec((SLOTS, D), lambda r, g: (r, 0)),
            pl.BlockSpec((8, D), lambda r, g: (0, 0)),
        ],
        out_shape=[
            jax.ShapeDtypeStruct((rows * SLOTS, D), jnp.bfloat16),
            jax.ShapeDtypeStruct((8, D), jnp.float32),
        ],
        scratch_shapes=[
            pltpu.VMEM((SLOTS, SLOTS), jnp.float32),
            pltpu.VMEM((SLOTS, D), jnp.float32),
        ]
        + slot_scratch(weights),
        compiler_params=params(2),
        cost_estimate=cost(50e9, 30e6),
        name="attend_back",
    )(fills, slots, qkv, context, context_grad, lse, seg_col, seg_row, *weights, sum_one)


def tiles(width):
    return pl.BlockSpec((TILE, width), lambda i: (i, 0))


def feed_front(slots, tokens, context, first, vectors, in_bias):
    count = tokens.shape[0]
    return pl.pallas_call(
        partial(front_kernel, len(first)),
        grid=(count // TILE,),
        in_specs=[SCALARS, tiles(D), tiles(D), whole(vectors), whole(in_bias)] + [ANYWHERE] * len(first),
        out_specs=[tiles(D), tiles(128), tiles(D), tiles(2 * FLAT)],
        out_shape=[
            jax.ShapeDtypeStruct((count, D), jnp.float32),
            jax.ShapeDtypeStruct((count, 128), jnp.float32),
            jax.ShapeDtypeStruct((count, D), jnp.float32),
            jax.ShapeDtypeStruct((count, 2 * FLAT), jnp.bfloat16),
        ],
        scratch_shapes=slot_scratch(first),
        compiler_params=params(1),
        cost_estimate=cost(25e9, 30e6),
        name="feed_front",
    )(slots, tokens, context, vectors, in_bias, *first)


def feed_back(slots, front, cotangent, first, late, vectors, in_bias):
    count = cotangent.shape[0]
    return pl.pallas_call(
        partial(back_kernel, (len(first), len(late))),
        grid=(count // TILE,),
        in_specs=[SCALARS, tiles(D), tiles(128), tiles(D), tiles(2 * FLAT), tiles(D), whole(vectors), whole(in_bias)]
        + [ANYWHERE] * (len(first) + len(late)),
        out_specs=[
            tiles(D),
            tiles(D),
            tiles(D),
            pl.BlockSpec((8, D), lambda i: (0, 0)),
            pl.BlockSpec((8, FF), lambda i: (0, 0)),
        ],
        out_shape=[
            jax.ShapeDtypeStruct((count, D), jnp.bfloat16),
            jax.ShapeDtypeStruct((count, D), jnp.bfloat16),
            jax.ShapeDtypeStruct((count, D), jnp.bfloat16),
            jax.ShapeDtypeStruct((8, D), jnp.float32),
            jax.ShapeDtypeStruct((8, FF), jnp.float32),
        ],
        scratch_shapes=[pltpu.VMEM((TILE, FF - 2 * FLAT), jnp.bfloat16)] + slot_scratch(first) + slot_scratch(late),
        compiler_params=params(1),
        cost_estimate=cost(75e9, 40e6),
        name="feed_back",
    )(slots, *front, cotangent, vectors, in_bias, *first, *late)


def stage_bits(n):
    bits = n.bit_length() - 1
    in_z = -(-bits // 3)
    in_y = -(-(bits - in_z) // 2)
    in_x = bits - in_z - in_y
    x = list(range(in_x))
    y = list(range(in_x, in_x + in_y))
    z = list(range(in_x + in_y, bits))
    return z + y + x, z[::-1] + x + y


def partner(block, n, stage):
    bits = [order[stage] for order in stage_bits(n)]
    pairs = [(2 * i + core, 2 * (i ^ (1 << bits[core])) + core) for i in range(n) for core in range(2)]
    return lax.ppermute(block, ("rows", "tp"), pairs)


def joined(*blocks):
    return jnp.concatenate(blocks, 0)


def swap_cores(block):
    return lax.ppermute(block, "tp", [(0, 1), (1, 0)])


def after(value, *earlier):
    return lax.optimization_barrier((value, earlier))[0]


def together(*values):
    return lax.optimization_barrier(values)


def slot_table(n):
    apart = jnp.arange(n, dtype=jnp.int32) ^ lax.axis_index("rows")
    tables = []
    for order in stage_bits(n):
        tables.append(sum(((apart >> bit) & 1) << place for place, bit in enumerate(order)))
    core = lax.axis_index("tp")
    return jnp.where(core == 0, jnp.stack(tables), jnp.stack(tables[::-1]))


def sum_over_all(values, n):
    values = values + swap_cores(values)
    step = 1
    while step < n:
        values = values + lax.ppermute(values, "rows", [(i, i ^ step) for i in range(n)])
        step *= 2
    return values


def shards(
    tokens,
    segment_ids,
    fill_counts,
    qkv_weight,
    qv_bias,
    out_weight,
    out_bias,
    norm1_gain,
    norm1_bias,
    in_weight,
    in_bias,
    down_weight,
    down_bias,
    norm2_gain,
    norm2_bias,
    cotangent,
):
    n = lax.axis_size("rows")
    core = lax.axis_index("tp")
    rows_here = tokens.shape[0] // SLOTS
    down_t = down_weight.T
    width = qv_bias.shape[1]

    last = n.bit_length() - 2

    def spread(blocks, stages):
        for stage in stages:
            blocks = blocks + [partner(block, n, stage) for block in blocks]
        return blocks

    middle = range(2, last)
    q = qkv_weight[None]
    q = joined(q, partner(q, n, 0))
    q = joined(q, partner(q, n, 1))
    first = jnp.concatenate([in_weight[:, :FLAT], down_t[:, :FLAT], out_weight.T], 1)[None]
    q, first = together(q, first)
    q_own = spread([q], middle)
    first = joined(first, partner(first, n, 0))
    segments = lax.dynamic_slice_in_dim(segment_ids, core * rows_here, rows_here, 0)
    fills = lax.dynamic_slice_in_dim(fill_counts, core * rows_here, rows_here, 0)
    seg_col = segments[:, :, None]
    seg_row = segments[:, None, :]
    slots = slot_table(n)
    own = jnp.concatenate([qv_bias.reshape(-1), in_bias])
    other = swap_cores(own)
    by_distance = [wide(b) for b in (own, other)]
    b_qv = [b[: 2 * width].reshape(2, width) for b in by_distance]
    b_in = [b[2 * width :] for b in by_distance]
    b_hidden = jnp.concatenate([b_in[0][:FLAT], b_in[1][:FLAT], b_in[0][FLAT:], b_in[1][FLAT:]]).reshape(1, -1)
    vectors = wide(
        jnp.concatenate([out_bias, norm1_gain, norm1_bias, down_bias, norm2_gain, norm2_bias, out_bias, out_bias])
    ).reshape(8, D)
    small = (seg_col, seg_row, fills, slots, b_qv, b_hidden, vectors)
    q_own, first, small = together(q_own, first, small)
    seg_col, seg_row, fills, slots, b_qv, b_hidden, vectors = small
    q_own = spread(q_own, [last])
    first_got = partner(first, n, 1)

    def run(step, earlier):
        bias = b_qv[step // 2][:, step % 2 * WIDE : (step % 2 + 1) * WIDE]
        pieces = q_others if step >= 2 else q_own
        return attend(step, earlier, tokens, seg_col, seg_row, fills, slots, pieces, bias)

    late = jnp.concatenate([in_weight[:, FLAT:], down_t[:, FLAT:]], 1)[None]
    q_own, first_got, late = together(q_own, first_got, late)
    first = joined(first, first_got)
    q_others = [swap_cores(w) for w in q_own]
    first_own = spread([first], middle)
    late_got = partner(late, n, 0)
    results = run(0, ())
    results, first_own, late_got, q_others = together(results, first_own, late_got, q_others)
    late = joined(late, late_got)
    first_own = spread(first_own, [last])
    late_got = partner(late, n, 1)
    results = run(1, results)
    results = run(2, results)
    results, first_own, late_got = together(results, first_own, late_got)
    late = joined(late, late_got)
    first_others = [swap_cores(w) for w in first_own]
    late_own = spread([late], middle)
    results = run(3, results)
    results, late_own = together(results, late_own)
    late_own = spread(late_own, [last])

    qkv, context, lse = results
    first = first_own + first_others
    front = feed_front(slots, tokens, context, first, vectors, b_hidden)
    front, late_own = together(front, late_own)
    late = late_own + [swap_cores(w) for w in late_own]
    layer_out, context_grad, sum_one, vec_grads, in_grads = feed_back(
        slots, front, cotangent, first, late, vectors, b_hidden
    )
    hidden = in_grads[0].reshape(2, 2, FF // 4)
    hidden = jnp.where(core == 0, hidden, hidden[:, ::-1]).transpose(1, 0, 2)
    early = jnp.concatenate([vec_grads[:4].reshape(-1), hidden.reshape(-1)])
    early = jnp.sum(lax.all_gather(early, ("rows", "tp"), axis=0), 0)
    vec = early[: 4 * D].reshape(4, D)

    tokens_grad, qv_grads = attend_back(
        qkv, context, context_grad, lse, seg_col, seg_row, fills, slots, q_own + q_others, sum_one
    )
    qv = qv_grads[:2].reshape(2, 2, D // 2)
    qv = jnp.where(core == 0, qv, qv[:, ::-1]).reshape(2, D)
    qv = sum_over_all(qv, n)
    return (layer_out, tokens_grad, qv, vec[0], vec[1], early[4 * D :], vec[2], vec[3])


def solution(mesh):
    return jax.shard_map(
        shards,
        mesh=mesh,
        in_specs=(
            P(("rows", "tp"), None),
            P("rows", None),
            P("rows"),
            P(None, "rows", "tp"),
            P(None, "tp"),
            P("tp", "rows"),
            P(),
            P(),
            P(),
            P("rows", "tp"),
            P("tp"),
            P("tp", "rows"),
            P(),
            P(),
            P(),
            P(("rows", "tp"), None),
        ),
        out_specs=(P(("rows", "tp"), None), P(("rows", "tp"), None), P(), P(), P(), P(), P(), P()),
        check_vma=False,
    )
```

time: 535 us -> 389 us (0.73)
  waiting for transfers between devices: 228 us -> 54.4 us
  blocking collectives: 40.4 us -> 0 us
  starting transfers between devices: 0.6 us -> 30 us
  Pallas kernels: 239 us -> 262 us
  local copies, waits for them, and re-layouts: 12.3 us -> 21.7 us
    all_gather x4 -> x1, waiting for transfers between devices: 225 us -> 0.01 us  [shards(): early = jnp.sum(lax.all_gather(early, ('rows', 'tp'), axis=0), 0)]
    ppermute x1 -> x33, waiting for transfers between devices: 0.01 us -> 54.4 us  [the longest x15 38.6 us: partner(): return lax.ppermute(block, ('rows', 'tp'), pairs)]
    psum x1 -> x0, blocking collectives: 40.4 us -> none  [shards(): lax.psum((qv_grads[:2], vec_grads[:4], in_grads[0]), ('rows', 'tp'))]
    ppermute x1 -> x33, starting transfers between devices: 0.45 us -> 30 us  [the longest x15 19.2 us: partner(): return lax.ppermute(block, ('rows', 'tp'), pairs)]
    pallas_call x3 -> x7, Pallas kernels: 239 us -> 262 us  [the longest x1 87.7 us: feed_back(): pl.pallas_call(partial(back_kernel, (len(first), len(late))), grid=(count...]
    unnamed x11 -> x40, local copies, waits for them, and re-layouts: 1.94 us -> 9.39 us
  transfers between devices with their start and end apart: 5 -> 34, of which waited for: 4 -> 13; matrix products, arithmetic and copies ran while one was open for 2% -> 5% of each run, Pallas kernels for 10% -> 45%
where the time goes in v2:
time: 389 us; the launch traced here: 388 us
  Pallas kernels  262 us (67%)
  waiting for transfers between devices  54.4 us (14%)
  starting transfers between devices  30 us (8%)
  local copies, waits for them, and re-layouts  21.7 us (6%)
  between operations  14.5 us (4%)
  other arithmetic  5.51 us (1%)
    pallas_call x1, Pallas kernels, feed_back(): pl.pallas_call(partial(back_kernel, (len(first), len(late))), grid=(count...  87.7 us
    pallas_call x1, Pallas kernels, attend_back(): pl.pallas_call(partial(attend_back_kernel, len(weights)), grid=(rows, GRO...  71.4 us
    pallas_call x4, Pallas kernels, attend(): pl.pallas_call(partial(attend_kernel, step, len(pieces)), grid=(rows,), i...  63 us
    pallas_call x1, Pallas kernels, feed_front(): pl.pallas_call(partial(front_kernel, len(first)), grid=(count // TILE,),...  39.6 us
    ppermute x15, waiting for transfers between devices, partner(): return lax.ppermute(block, ('rows', 'tp'), pairs)  38.6 us
    ppermute x15, starting transfers between devices, partner(): return lax.ppermute(block, ('rows', 'tp'), pairs)  19.2 us
    unnamed x40, local copies, waits for them, and re-layouts  9.39 us
    ppermute x4, waiting for transfers between devices, sum_over_all(): lax.ppermute(values, 'rows', [(i, i ^ step) for i in range(n)])  8.63 us
  transfers between devices with their start and end apart: 34, of which 13 were waited for; matrix products, arithmetic and copies ran while one was open for 5% of the time, Pallas kernels for 45%

profile of v2, /device:TPU:0, one launch (start us, length us, event | category | flops | bytes accessed | tf_op | source)
XLA Modules:
  0.0 387.9 jit_solution(4477715020032479323)
XLA Ops:
  9.1 2.6 collective-permute-start
  19.3 2.7 collective-permute-start.1
  22.9 9.4 %collective-permute-done.1 = bf16[2,3,64,512]{3,2,1,0:T(8,128)(2,1)S(1)} collective-permute-done((bf16[2,3,64,512]{3,2,1,0:T(8,128)(2,1)S(1)}, bf16[2,3,64,512]{3,2,1,0:T(8,128)(2,1)S(1)}, u32[]{:S(2)}, u32[]{:S(2)}) %collective-permute-start.1) | collective-permute-done | bytes 393248 | tf_op jit(solution)/shard_map/ppermute | solution.py:462
  33.3 1.6 collective-permute-start.2
  38.4 8.6 %collective-permute-done.3 = bf16[1,64,2560]{2,1,0:T(8,128)(2,1)S(1)} collective-permute-done((bf16[1,64,2560]{2,1,0:T(8,128)(2,1)S(1)}, bf16[1,64,2560]{2,1,0:T(8,128)(2,1)S(1)}, u32[]{:S(2)}, u32[]{:S(2)}) %collective-permute-start.3) | collective-permute-done | bytes 327712 | tf_op jit(solution)/shard_map/ppermute | solution.py:462
  47.1 1.5 collective-permute-start.7
  48.6 1.5 collective-permute-start.5
  51.2 1.4 copy.50.segc_ref
  54.0 11.6 %collective-permute-done.7 = bf16[2,64,2560]{2,1,0:T(8,128)(2,1)S(1)} collective-permute-done((bf16[2,64,2560]{2,1,0:T(8,128)(2,1)S(1)}, bf16[2,64,2560]{2,1,0:T(8,128)(2,1)S(1)}, u32[]{:S(2)}, u32[]{:S(2)}) %collective-permute-start.7) | collective-permute-done | bytes 655392 | tf_op jit(solution)/shard_map/ppermute | solution.py:462
  65.7 3.5 collective-permute-done.6.rest_3_
  69.1 2.5 collective-permute-start.9
  73.5 4.0 %collective-permute-done.9 = bf16[1,64,2048]{2,1,0:T(8,128)(2,1)S(1)} collective-permute-done((bf16[1,64,2048]{2,1,0:T(8,128)(2,1)S(1)}, bf16[1,64,2048]{2,1,0:T(8,128)(2,1)S(1)}, u32[]{:S(2)}, u32[]{:S(2)}) %collective-permute-start.9) | collective-permute-done | bytes 262176 | tf_op jit(solution)/shard_map/ppermute | solution.py:462
  78.2 15.8 %attend.4 = (bf16[3,2048,1024]{2,1,0:T(8,128)(2,1)}, bf16[2048,1024]{1,0:T(8,128)(2,1)}, f32[4,4,4,512]{3,2,1,0:T(4,128)}) custom-call(s32[4]{0:T(128)} %dynamic_slice.7.fill_ref, s32[2,16]{1,0:T(2,128)} %add_select_fusion.slot_ref, bf16[2048,1024]{1,0:T(8,128)(2,1)} %x_ref.9, s32[4,512,1]{2,1,0:T(8,128)} %copy.50.segc_ref, ...), custom_call_target="tpu_custom_call" | custom-call | flops 15000000512 | bytes 10000000 | tf_op jit(solution)/shard_map/attend/pallas_call | solution.py:327
  94.1 1.4 collective-permute-done.8.rest_1_
  95.6 1.3 collective-permute-start.14
  97.7 15.7 %attend.5 = (bf16[3,2048,1024]{2,1,0:T(8,128)(2,1)}, bf16[2048,1024]{1,0:T(8,128)(2,1)}, f32[4,4,4,512]{3,2,1,0:T(4,128)}) custom-call(s32[4]{0:T(128)} %dynamic_slice.7.fill_ref, s32[2,16]{1,0:T(2,128)} %add_select_fusion.slot_ref, bf16[2048,1024]{1,0:T(8,128)(2,1)} %x_ref.9, ...), custom_call_target="tpu_custom_call", output_to_operand_aliasing={{0}: (10, {}), {1}: (11, {}), {2}: (12, {})} | custom-call | flops 15000000512 | bytes 10000000 | tf_op jit(solution)/shard_map/attend/pallas_call | solution.py:327
  113.5 15.8 %attend.6 = (bf16[3,2048,1024]{2,1,0:T(8,128)(2,1)}, bf16[2048,1024]{1,0:T(8,128)(2,1)}, f32[4,4,4,512]{3,2,1,0:T(4,128)}) custom-call(s32[4]{0:T(128)} %dynamic_slice.7.fill_ref, s32[2,16]{1,0:T(2,128)} %add_select_fusion.slot_ref, bf16[2048,1024]{1,0:T(8,128)(2,1)} %x_ref.9, ...), custom_call_target="tpu_custom_call", output_to_operand_aliasing={{0}: (10, {}), {1}: (11, {}), {2}: (12, {})} | custom-call | flops 15000000512 | bytes 10000000 | tf_op jit(solution)/shard_map/attend/pallas_call | solution.py:327
  131.4 15.8 %attend.7 = (bf16[3,2048,1024]{2,1,0:T(8,128)(2,1)}, bf16[2048,1024]{1,0:T(8,128)(2,1)}, f32[4,4,4,512]{3,2,1,0:T(4,128)}) custom-call(s32[4]{0:T(128)} %dynamic_slice.7.fill_ref, s32[2,16]{1,0:T(2,128)} %add_select_fusion.slot_ref, bf16[2048,1024]{1,0:T(8,128)(2,1)} %x_ref.9, ...), custom_call_target="tpu_custom_call", output_to_operand_aliasing={{0}: (10, {}), {1}: (11, {}), {2}: (12, {})} | custom-call | flops 15000000512 | bytes 10000000 | tf_op jit(solution)/shard_map/attend/pallas_call | solution.py:327
  147.2 1.2 collective-permute-start.22
  149.4 39.6 %feed_front.1 = (f32[2048,1024]{1,0:T(8,128)}, f32[2048,128]{1,0:T(8,128)}, f32[2048,1024]{1,0:T(8,128)}, bf16[2048,2048]{1,0:T(8,128)(2,1)}) custom-call(s32[2,16]{1,0:T(2,128)} %add_select_fusion.slot_ref, bf16[2048,1024]{1,0:T(8,128)(2,1)} %x_ref.9, bf16[2048,1024]{1,0:T(8,128)(2,1)} %get-tuple-element.124.ctx_ref, f32[8,1024]{1,0:T(8,128)} %reshape.143.vec_ref, ...), custom_call_target="tpu_custom_call" | custom-call | flops 24999999488 | bytes 30000000 | tf_op jit(solution)/shard_map/feed_front/pallas_call | solution.py:402
  190.2 1.6 collective-permute-done.24.rest_12_
  191.8 4.5 %collective-permute-done.25.rest_13_ = bf16[4,64,2048]{2,1,0:T(8,128)(2,1)S(1)} collective-permute-done((bf16[4,64,2048]{2,1,0:T(8,128)(2,1)S(1)}, bf16[4,64,2048]{2,1,0:T(8,128)(2,1)S(1)}, u32[]{:S(2)}, u32[]{:S(2)}) %collective-permute-start.25) | collective-permute-done | bytes 1048608 | tf_op jit(solution)/shard_map/ppermute | solution.py:470
  198.3 87.7 %feed_back.1 = (bf16[2048,1024]{1,0:T(8,128)(2,1)}, bf16[2048,1024]{1,0:T(8,128)(2,1)}, bf16[2048,1024]{1,0:T(8,128)(2,1)}, f32[8,1024]{1,0:T(8,128)}, f32[8,4096]{1,0:T(8,128)}) custom-call(s32[2,16]{1,0:T(2,128)} %add_select_fusion.slot_ref, f32[2048,1024]{1,0:T(8,128)} %get-tuple-element.137.normal_ref, f32[2048,128]{1,0:T(8,128)} %get-tuple-element.138.inv_ref, ...), custom_call_target="tpu_custom_call" | custom-call | flops 74999996416 | bytes 40000000 | tf_op jit(solution)/shard_map/feed_back/pallas_call | solution.py:422
  288.4 71.4 %attend_back.1 = (bf16[2048,1024]{1,0:T(8,128)(2,1)}, f32[8,1024]{1,0:T(8,128)}) custom-call(s32[4]{0:T(128)} %dynamic_slice.7.fill_ref, s32[2,16]{1,0:T(2,128)} %add_select_fusion.slot_ref, bf16[3,2048,1024]{2,1,0:T(8,128)(2,1)} %get-tuple-element.146.qkv_ref, bf16[2048,1024]{1,0:T(8,128)(2,1)} %get-tuple-element.124.ctx_ref, ...), custom_call_target="tpu_custom_call" | custom-call | flops 49999998976 | bytes 30000000 | tf_op jit(solution)/shard_map/attend_back/pallas_call | solution.py:362
  363.1 2.6 collective-permute-done.29
  365.7 1.1 collective-permute-start.30
  366.9 2.5 collective-permute-done.30
  369.4 2.1 collective-permute-start.31
  371.5 1.6 collective-permute-done.31
  373.2 2.6 collective-permute-start.32
  375.8 1.9 collective-permute-done.32
  378.3 1.4 reshape.144
  (128 shorter events, 34.9 us)
Async XLA Ops:
  7.2 371.1 %all-gather.3.cloned.1.call-start = ((), (), s32[]{:S(2)}) async-start(), calls=%async_computation | async-start | bytes 1081344 | tf_op jit(solution)/shard_map/all_gather | solution.py:595
  8.6 29.1 %collective-permute-start.4 = (bf16[3072]{0:T(1024)(128)(2,1)S(1)}, bf16[3072]{0:T(1024)(128)(2,1)S(1)}, u32[]{:S(2)}, u32[]{:S(2)}) collective-permute-start(bf16[3072]{0:T(1024)(128)(2,1)S(1)} %constant_dynamic-update-slice_fusion.7), channel_id=1, source_target_pairs={{0,1},{1,0},{2,3},{3,2},{4,5},{5,4},{6,7},{7,6},{8,9},{9,8},{10,11... | collective-permute-start | bytes 18440 | tf_op jit(solution)/shard_map/ppermute | solution.py:470
  9.1 9.3 %collective-permute-start = (bf16[1,3,64,512]{3,2,1,0:T(8,128)(2,1)}, bf16[1,3,64,512]{3,2,1,0:T(8,128)(2,1)S(1)}, u32[]{:S(2)}, u32[]{:S(2)}) collective-permute-start(bf16[1,3,64,512]{3,2,1,0:T(8,128)(2,1)} %bitcast.24), channel_id=1, source_target_pairs={{0,8},{1,17},{2,10},{3,19},{4,12},{5,21},{6,14},{7,23},{8,0},{9,25... | collective-permute-start | bytes 589832 | tf_op jit(solution)/shard_map/ppermute | solution.py:462
  19.3 13.0 %collective-permute-start.1 = (bf16[2,3,64,512]{3,2,1,0:T(8,128)(2,1)S(1)}, bf16[2,3,64,512]{3,2,1,0:T(8,128)(2,1)S(1)}, u32[]{:S(2)}, u32[]{:S(2)}) collective-permute-start(bf16[2,3,64,512]{3,2,1,0:T(8,128)(2,1)S(1)} %pad_maximum_fusion.3), channel_id=1, source_target_pairs={{0,16},{1,9},{2,18},{3,11},{4,20},{5,13},{6,22},{7,15},{8,24},{9,1... | collective-permute-start | bytes 1179656 | tf_op jit(solution)/shard_map/ppermute | solution.py:462
  33.3 13.8 %collective-permute-start.2 = (bf16[4,3,64,512]{3,2,1,0:T(8,128)(2,1)S(1)}, bf16[4,3,64,512]{3,2,1,0:T(8,128)(2,1)}, u32[]{:S(2)}, u32[]{:S(2)}) collective-permute-start(bf16[4,3,64,512]{3,2,1,0:T(8,128)(2,1)S(1)} %pad_maximum_fusion.rest_0_), channel_id=1, source_target_pairs={{0,4},{1,3},{2,6},{3,1},{4,0},{5,7},{6,2},{7,5},{8,12},{9,11},{10,... | collective-permute-start | bytes 2359304 | tf_op jit(solution)/shard_map/ppermute | solution.py:462
  37.3 9.7 %collective-permute-start.3 = (bf16[1,64,2560]{2,1,0:T(8,128)(2,1)S(1)}, bf16[1,64,2560]{2,1,0:T(8,128)(2,1)S(1)}, u32[]{:S(2)}, u32[]{:S(2)}) collective-permute-start(bf16[1,64,2560]{2,1,0:T(8,128)(2,1)S(1)} %maximum_bitcast_fusion), channel_id=1, source_target_pairs={{0,8},{1,17},{2,10},{3,19},{4,12},{5,21},{6,14},{7,23},{8,0},{9,25... | collective-permute-start | bytes 983048 | tf_op jit(solution)/shard_map/ppermute | solution.py:462
  47.1 18.6 %collective-permute-start.7 = (bf16[2,64,2560]{2,1,0:T(8,128)(2,1)S(1)}, bf16[2,64,2560]{2,1,0:T(8,128)(2,1)S(1)}, u32[]{:S(2)}, u32[]{:S(2)}) collective-permute-start(bf16[2,64,2560]{2,1,0:T(8,128)(2,1)S(1)} %pad_maximum_fusion.1), channel_id=1, source_target_pairs={{0,16},{1,9},{2,18},{3,11},{4,20},{5,13},{6,22},{7,15},{8,24},{9,1... | collective-permute-start | bytes 1966088 | tf_op jit(solution)/shard_map/ppermute | solution.py:462
  48.6 17.1 %collective-permute-start.5 = (bf16[4,3,64,512]{3,2,1,0:T(8,128)(2,1)S(1)}, bf16[4,3,64,512]{3,2,1,0:T(8,128)(2,1)}, u32[]{:S(2)}, u32[]{:S(2)}) collective-permute-start(bf16[4,3,64,512]{3,2,1,0:T(8,128)(2,1)S(1)} %pad_maximum_fusion.rest_0_), channel_id=1, source_target_pairs={{0,2},{1,5},{2,0},{3,7},{4,6},{5,1},{6,4},{7,3},{8,10},{9,13},{10,... | collective-permute-start | bytes 2359304 | tf_op jit(solution)/shard_map/ppermute | solution.py:462
  50.1 19.0 %collective-permute-start.6 = (bf16[4,3,64,512]{3,2,1,0:T(8,128)(2,1)}, bf16[4,3,64,512]{3,2,1,0:T(8,128)(2,1)}, u32[]{:S(2)}, u32[]{:S(2)}) collective-permute-start(bf16[4,3,64,512]{3,2,1,0:T(8,128)(2,1)} %collective-permute-done.2.rest_1_), channel_id=1, source_target_pairs={{0,2},{1,5},{2,0},{3,7},{4,6},{5,1},{6,4},{7,3},{8,10},{9,13},{10,... | collective-permute-start | bytes 2359304 | tf_op jit(solution)/shard_map/ppermute | solution.py:462
  69.1 8.4 %collective-permute-start.9 = (bf16[1,64,2048]{2,1,0:T(8,128)(2,1)S(1)}, bf16[1,64,2048]{2,1,0:T(8,128)(2,1)S(1)}, u32[]{:S(2)}, u32[]{:S(2)}) collective-permute-start(bf16[1,64,2048]{2,1,0:T(8,128)(2,1)S(1)} %maximum_bitcast_fusion.1), channel_id=1, source_target_pairs={{0,8},{1,17},{2,10},{3,19},{4,12},{5,21},{6,14},{7,23},{8,0},{9,25... | collective-permute-start | bytes 786440 | tf_op jit(solution)/shard_map/ppermute | solution.py:462
  71.6 22.4 %collective-permute-start.10 = (bf16[4,3,64,512]{3,2,1,0:T(8,128)(2,1)S(1)}, bf16[4,3,64,512]{3,2,1,0:T(8,128)(2,1)S(1)}, u32[]{:S(2)}, u32[]{:S(2)}) collective-permute-start(bf16[4,3,64,512]{3,2,1,0:T(8,128)(2,1)S(1)} %pad_maximum_fusion.rest_0_), channel_id=1, source_target_pairs={{0,1},{1,0},{2,3},{3,2},{4,5},{5,4},{6,7},{7,6},{8,9},{9,8},{10,11... | collective-permute-start | bytes 2359304 | tf_op jit(solution)/shard_map/ppermute | solution.py:470
  71.6 22.5 %collective-permute-start.11 = (bf16[4,3,64,512]{3,2,1,0:T(8,128)(2,1)}, bf16[4,3,64,512]{3,2,1,0:T(8,128)(2,1)}, u32[]{:S(2)}, u32[]{:S(2)}) collective-permute-start(bf16[4,3,64,512]{3,2,1,0:T(8,128)(2,1)} %collective-permute-done.2.rest_1_), channel_id=1, source_target_pairs={{0,1},{1,0},{2,3},{3,2},{4,5},{5,4},{6,7},{7,6},{8,9},{9,8},{10,11... | collective-permute-start | bytes 2359304 | tf_op jit(solution)/shard_map/ppermute | solution.py:470
  72.1 22.0 %collective-permute-start.12 = (bf16[4,3,64,512]{3,2,1,0:T(8,128)(2,1)}, bf16[4,3,64,512]{3,2,1,0:T(8,128)(2,1)}, u32[]{:S(2)}, u32[]{:S(2)}) collective-permute-start(bf16[4,3,64,512]{3,2,1,0:T(8,128)(2,1)} %collective-permute-done.5.rest_2_), channel_id=1, source_target_pairs={{0,1},{1,0},{2,3},{3,2},{4,5},{5,4},{6,7},{7,6},{8,9},{9,8},{10,11... | collective-permute-start | bytes 2359304 | tf_op jit(solution)/shard_map/ppermute | solution.py:470
  72.1 22.0 %collective-permute-start.13 = (bf16[4,3,64,512]{3,2,1,0:T(8,128)(2,1)}, bf16[4,3,64,512]{3,2,1,0:T(8,128)(2,1)}, u32[]{:S(2)}, u32[]{:S(2)}) collective-permute-start(bf16[4,3,64,512]{3,2,1,0:T(8,128)(2,1)} %collective-permute-done.6.rest_3_), channel_id=1, source_target_pairs={{0,1},{1,0},{2,3},{3,2},{4,5},{5,4},{6,7},{7,6},{8,9},{9,8},{10,11... | collective-permute-start | bytes 2359304 | tf_op jit(solution)/shard_map/ppermute | solution.py:470
  77.6 17.9 %collective-permute-start.8 = (bf16[4,64,2560]{2,1,0:T(8,128)(2,1)}, bf16[4,64,2560]{2,1,0:T(8,128)(2,1)}, u32[]{:S(2)}, u32[]{:S(2)}) collective-permute-start(bf16[4,64,2560]{2,1,0:T(8,128)(2,1)} %constant_dynamic-update-slice_fusion.2.rest_0_), channel_id=1, source_target_pairs={{0,4},{1,3},{2,6},{3,1},{4,0},{5,7},{6,2},{7,5},{8,12},{9,11},{10,... | collective-permute-start | bytes 3932168 | tf_op jit(solution)/shard_map/ppermute | solution.py:462
  95.5 33.7 %collective-permute-start.16 = (bf16[2,64,2048]{2,1,0:T(8,128)(2,1)S(1)}, bf16[2,64,2048]{2,1,0:T(8,128)(2,1)S(1)}, u32[]{:S(2)}, u32[]{:S(2)}) collective-permute-start(bf16[2,64,2048]{2,1,0:T(8,128)(2,1)S(1)} %pad_maximum_fusion.2), channel_id=1, source_target_pairs={{0,16},{1,9},{2,18},{3,11},{4,20},{5,13},{6,22},{7,15},{8,24},{9,1... | collective-permute-start | bytes 1572872 | tf_op jit(solution)/shard_map/ppermute | solution.py:462
  95.6 33.7 %collective-permute-start.14 = (bf16[4,64,2560]{2,1,0:T(8,128)(2,1)}, bf16[4,64,2560]{2,1,0:T(8,128)(2,1)}, u32[]{:S(2)}, u32[]{:S(2)}) collective-permute-start(bf16[4,64,2560]{2,1,0:T(8,128)(2,1)} %constant_dynamic-update-slice_fusion.2.rest_0_), channel_id=1, source_target_pairs={{0,2},{1,5},{2,0},{3,7},{4,6},{5,1},{6,4},{7,3},{8,10},{9,13},{10,... | collective-permute-start | bytes 3932168 | tf_op jit(solution)/shard_map/ppermute | solution.py:462
  96.9 32.4 %collective-permute-start.15 = (bf16[4,64,2560]{2,1,0:T(8,128)(2,1)}, bf16[4,64,2560]{2,1,0:T(8,128)(2,1)}, u32[]{:S(2)}, u32[]{:S(2)}) collective-permute-start(bf16[4,64,2560]{2,1,0:T(8,128)(2,1)} %collective-permute-done.8.rest_1_), channel_id=1, source_target_pairs={{0,2},{1,5},{2,0},{3,7},{4,6},{5,1},{6,4},{7,3},{8,10},{9,13},{10,... | collective-permute-start | bytes 3932168 | tf_op jit(solution)/shard_map/ppermute | solution.py:462
  129.4 17.8 %collective-permute-start.17 = (bf16[4,64,2048]{2,1,0:T(8,128)(2,1)S(1)}, bf16[4,64,2048]{2,1,0:T(8,128)(2,1)S(1)}, u32[]{:S(2)}, u32[]{:S(2)}) collective-permute-start(bf16[4,64,2048]{2,1,0:T(8,128)(2,1)S(1)} %constant_dynamic-update-slice_fusion.4.rest_8_), channel_id=1, source_target_pairs={{0,4},{1,3},{2,6},{3,1},{4,0},{5,7},{6,2},{7,5},{8,12},{9,11},{10,... | collective-permute-start | bytes 3145736 | tf_op jit(solution)/shard_map/ppermute | solution.py:462
  130.4 18.0 %collective-permute-start.18 = (bf16[4,64,2560]{2,1,0:T(8,128)(2,1)}, bf16[4,64,2560]{2,1,0:T(8,128)(2,1)S(1)}, u32[]{:S(2)}, u32[]{:S(2)}) collective-permute-start(bf16[4,64,2560]{2,1,0:T(8,128)(2,1)} %constant_dynamic-update-slice_fusion.2.rest_0_), channel_id=1, source_target_pairs={{0,1},{1,0},{2,3},{3,2},{4,5},{5,4},{6,7},{7,6},{8,9},{9,8},{10,11... | collective-permute-start | bytes 3932168 | tf_op jit(solution)/shard_map/ppermute | solution.py:470
  130.4 18.9 %collective-permute-start.19 = (bf16[4,64,2560]{2,1,0:T(8,128)(2,1)}, bf16[4,64,2560]{2,1,0:T(8,128)(2,1)}, u32[]{:S(2)}, u32[]{:S(2)}) collective-permute-start(bf16[4,64,2560]{2,1,0:T(8,128)(2,1)} %collective-permute-done.8.rest_1_), channel_id=1, source_target_pairs={{0,1},{1,0},{2,3},{3,2},{4,5},{5,4},{6,7},{7,6},{8,9},{9,8},{10,11... | collective-permute-start | bytes 3932168 | tf_op jit(solution)/shard_map/ppermute | solution.py:470
  130.9 18.4 %collective-permute-start.20 = (bf16[4,64,2560]{2,1,0:T(8,128)(2,1)}, bf16[4,64,2560]{2,1,0:T(8,128)(2,1)}, u32[]{:S(2)}, u32[]{:S(2)}) collective-permute-start(bf16[4,64,2560]{2,1,0:T(8,128)(2,1)} %collective-permute-done.14.rest_2_), channel_id=1, source_target_pairs={{0,1},{1,0},{2,3},{3,2},{4,5},{5,4},{6,7},{7,6},{8,9},{9,8},{10,11... | collective-permute-start | bytes 3932168 | tf_op jit(solution)/shard_map/ppermute | solution.py:470
  130.9 18.4 %collective-permute-start.21 = (bf16[4,64,2560]{2,1,0:T(8,128)(2,1)}, bf16[4,64,2560]{2,1,0:T(8,128)(2,1)}, u32[]{:S(2)}, u32[]{:S(2)}) collective-permute-start(bf16[4,64,2560]{2,1,0:T(8,128)(2,1)} %collective-permute-done.15.rest_3_), channel_id=1, source_target_pairs={{0,1},{1,0},{2,3},{3,2},{4,5},{5,4},{6,7},{7,6},{8,9},{9,8},{10,11... | collective-permute-start | bytes 3932168 | tf_op jit(solution)/shard_map/ppermute | solution.py:470
  147.2 41.9 %collective-permute-start.22 = (bf16[4,64,2048]{2,1,0:T(8,128)(2,1)S(1)}, bf16[4,64,2048]{2,1,0:T(8,128)(2,1)}, u32[]{:S(2)}, u32[]{:S(2)}) collective-permute-start(bf16[4,64,2048]{2,1,0:T(8,128)(2,1)S(1)} %constant_dynamic-update-slice_fusion.4.rest_8_), channel_id=1, source_target_pairs={{0,2},{1,5},{2,0},{3,7},{4,6},{5,1},{6,4},{7,3},{8,10},{9,13},{10,... | collective-permute-start | bytes 3145736 | tf_op jit(solution)/shard_map/ppermute | solution.py:462
  148.3 40.7 %collective-permute-start.23 = (bf16[4,64,2048]{2,1,0:T(8,128)(2,1)S(1)}, bf16[4,64,2048]{2,1,0:T(8,128)(2,1)}, u32[]{:S(2)}, u32[]{:S(2)}) collective-permute-start(bf16[4,64,2048]{2,1,0:T(8,128)(2,1)S(1)} %collective-permute-done.17.rest_9_), channel_id=1, source_target_pairs={{0,2},{1,5},{2,0},{3,7},{4,6},{5,1},{6,4},{7,3},{8,10},{9,13},{10,... | collective-permute-start | bytes 3145736 | tf_op jit(solution)/shard_map/ppermute | solution.py:462
  189.2 7.1 %collective-permute-start.25 = (bf16[4,64,2048]{2,1,0:T(8,128)(2,1)S(1)}, bf16[4,64,2048]{2,1,0:T(8,128)(2,1)S(1)}, u32[]{:S(2)}, u32[]{:S(2)}) collective-permute-start(bf16[4,64,2048]{2,1,0:T(8,128)(2,1)S(1)} %collective-permute-done.17.rest_9_), channel_id=1, source_target_pairs={{0,1},{1,0},{2,3},{3,2},{4,5},{5,4},{6,7},{7,6},{8,9},{9,8},{10,11... | collective-permute-start | bytes 3145736 | tf_op jit(solution)/shard_map/ppermute | solution.py:470
  189.7 7.7 %collective-permute-start.26 = (bf16[4,64,2048]{2,1,0:T(8,128)(2,1)}, bf16[4,64,2048]{2,1,0:T(8,128)(2,1)S(1)}, u32[]{:S(2)}, u32[]{:S(2)}) collective-permute-start(bf16[4,64,2048]{2,1,0:T(8,128)(2,1)} %collective-permute-done.22.rest_10_), channel_id=1, source_target_pairs={{0,1},{1,0},{2,3},{3,2},{4,5},{5,4},{6,7},{7,6},{8,9},{9,8},{10,11... | collective-permute-start | bytes 3145736 | tf_op jit(solution)/shard_map/ppermute | solution.py:470
  189.7 8.6 %collective-permute-start.27 = (bf16[4,64,2048]{2,1,0:T(8,128)(2,1)}, bf16[4,64,2048]{2,1,0:T(8,128)(2,1)}, u32[]{:S(2)}, u32[]{:S(2)}) collective-permute-start(bf16[4,64,2048]{2,1,0:T(8,128)(2,1)} %collective-permute-done.23.rest_11_), channel_id=1, source_target_pairs={{0,1},{1,0},{2,3},{3,2},{4,5},{5,4},{6,7},{7,6},{8,9},{9,8},{10,11... | collective-permute-start | bytes 3145736 | tf_op jit(solution)/shard_map/ppermute | solution.py:470
  362.1 3.7 collective-permute-start.29
  365.7 3.7 collective-permute-start.30
  369.4 3.8 collective-permute-start.31
  373.2 4.5 %collective-permute-start.32 = (f32[2,1024]{1,0:T(2,128)S(1)}, f32[2,1024]{1,0:T(2,128)S(1)}, u32[]{:S(2)}, u32[]{:S(2)}) collective-permute-start(f32[2,1024]{1,0:T(2,128)S(1)} %add.89), channel_id=1, source_target_pairs={{0,16},{2,18},{4,20},{6,22},{8,24},{10,26},{12,28},{14,30},{16,0},... | collective-permute-start | bytes 24584 | tf_op jit(solution)/shard_map/ppermute | solution.py:494
  (14 other events, 315.4 us)
Sparse Core Ops, SparseCore 0:
  288.5 53.5 all-gather.2

commit v3 on v2

--- a/solution.py
+++ b/solution.py
@@ -18,7 +18,8 @@
 PAIR = 2 * HEAD_DIM
 GROUPS = HEADS // GROUP
 TILE = 256
-HIDDEN = 512
+HIDDEN = 1024
+STRIP = 32
 EPSILON = 1e-05
 MASKED = -1e30
 SCALE = 1.0 / math.sqrt(HEAD_DIM)
@@ -26,6 +27,7 @@
 
 NN = (((1,), (0,)), ((), ()))
 NT = (((1,), (1,)), ((), ()))
+TT = (((0,), (1,)), ((), ()))
 
 
 def mul(left, right, dims=NN):
@@ -69,17 +71,33 @@
     return jnp.concatenate([rows, zeros] if head % 2 == 0 else [zeros, rows], 0)
 
 
-def fetch(refs, scratch, sem, columns=None):
+def fetch(refs, scratch, sem, columns=None, start=True):
     copies = []
     half = len(refs) // 2
     for i, ref in enumerate(refs):
         size = ref.shape[0]
+        target = scratch.at[i // half, pl.ds(i % half * size, size)]
         if columns is not None:
-            ref = ref.at[:, :, :, columns]
-        target = scratch.at[i // half, pl.ds(i % half * size, size)]
+            ref, target = ref.at[:, :, columns], target.at[:, :, columns]
         copies.append(pltpu.make_async_copy(ref, target, sem.at[i]))
-        copies[-1].start()
+        if start:
+            copies[-1].start()
     return copies
+
+
+def first_or_later(step, body):
+    @pl.when(step == 0)
+    def _():
+        body(True)
+
+    @pl.when(step != 0)
+    def _():
+        body(False)
+
+
+def wait_all(copies):
+    for copy in copies:
+        copy.wait()
 
 
 def set_weight(w_ref, slot_ref, other, part, columns=slice(None)):
@@ -93,7 +111,7 @@
 
 
 def attend_kernel(step, count, fill_ref, slot_ref, x_ref, segc_ref, segr_ref, b_ref, *rest):
-    qkv_ref, ctx_ref, lse_ref, w_ref, sem = rest[-5:]
+    qk_ref, kv_ref, ctx_ref, lse_ref, w_ref, sem = rest[-6:]
 
     @pl.when(pl.program_id(0) == 0)
     def _():
@@ -112,29 +130,39 @@
     q = low(mul(x, weight[0]) + b_ref[0:1, :])
     k = low(mul(x, weight[1]))
     v = low(mul(x, weight[2]) + b_ref[1:2, :])
-    qkv_ref[0] = q
-    qkv_ref[1] = k
-    qkv_ref[2] = v
     q_t = (q * jnp.bfloat16(SCALE)).T
     v_t = v.T
+    qk_ref[0, 0] = q_t
+    qk_ref[1, 0] = k.T
+    kv_ref[0] = k
+    kv_ref[1] = v
     ones = jnp.ones((HEAD_DIM, SLOTS), jnp.bfloat16)
-    context = []
-    for head in range(GROUP):
+
+    def score(head):
         own = slice(head * HEAD_DIM, (head + 1) * HEAD_DIM)
         pair = slice(head // 2 * PAIR, (head // 2 + 1) * PAIR)
-        scores = mul(k[:, pair], half_rows(q_t[own], head)) + bias
-        top = jnp.max(scores, 0, keepdims=True)
-        probs = low(jnp.exp(scores - top))
+        return mul(k[:, pair], half_rows(q_t[own], head)) + bias
+
+    def finish(head, top, probs):
+        own = slice(head * HEAD_DIM, (head + 1) * HEAD_DIM)
         out = mul(jnp.concatenate([v_t[own], ones], 0), probs)
         total = out[HEAD_DIM : HEAD_DIM + 1]
-        context.append(low(out[:HEAD_DIM] / total))
+        ctx_ref[0, own] = low(out[:HEAD_DIM] / total)
         lse_ref[0, 0, head : head + 1, :] = top + jnp.log(total)
-    ctx_ref[...] = jnp.concatenate(context, 0).T
-
-
-def attend_back_kernel(
-    count, fill_ref, slot_ref, qkv_ref, ctx_ref, dctx_ref, lse_ref, segc_ref, segr_ref, *rest
-):
+
+    scores = score(0)
+    done = None
+    for head in range(GROUP):
+        following = score(head + 1) if head + 1 < GROUP else None
+        if done is not None:
+            finish(head - 1, *done)
+        top = jnp.max(scores, 0, keepdims=True)
+        done = top, low(jnp.exp(scores - top))
+        scores = following
+    finish(GROUP - 1, *done)
+
+
+def attend_back_kernel(count, fill_ref, slot_ref, qk_ref, kv_ref, dctx_ref, delta_ref, lse_ref, segc_ref, segr_ref, *rest):
     sum_ref, out_ref, qvb_ref, bias_ref, acc_ref, w_ref, sem = rest[-7:]
     row = pl.program_id(0)
     group = pl.program_id(1)
@@ -144,53 +172,42 @@
         bias_ref[...] = mask_bias(segc_ref[0], segr_ref[0], fill_ref[row])
         acc_ref[...] = wide(sum_ref[...])
 
-    @pl.when((group == 0) & (row == 0))
-    def _():
-        qvb_ref[...] = jnp.zeros_like(qvb_ref)
-        for copy in fetch(rest[:count], w_ref, sem):
-            copy.wait()
-
-    q = qkv_ref[0]
-    k = qkv_ref[1]
-    v = qkv_ref[2]
-    d_out = dctx_ref[...]
-    product = wide(d_out) * wide(ctx_ref[...])
-    high = low(product)
-    rest = low(product - wide(high))
-    picks = lax.broadcasted_iota(jnp.int32, (16, WIDE), 1) // HEAD_DIM
-    picks = low(jnp.where(picks == lax.broadcasted_iota(jnp.int32, (16, WIDE), 0), 1.0, 0.0))
-    delta = mul(picks, high, NT) + mul(picks, rest, NT)
-    q_t = (q * jnp.bfloat16(SCALE)).T
-    k_t = k.T
-    d_out_t = d_out.T
-    d_q, d_k, d_v = [], [], []
-    for head in range(GROUP):
-        own = slice(head * HEAD_DIM, (head + 1) * HEAD_DIM)
-        pair = slice(head // 2 * PAIR, (head // 2 + 1) * PAIR)
-        scores = mul(k[:, pair], half_rows(q_t[own], head)) + bias_ref[...]
-        probs = jnp.exp(scores - lse_ref[0, 0, head : head + 1, :])
-        probs_grad = mul(v[:, pair], half_rows(d_out_t[own], head))
-        scores_grad = low(probs * (probs_grad - delta[head : head + 1]))
-        probs_low = low(probs)
-        d_v.append(low(mul(d_out_t[own], probs_low, NT)))
-        d_k.append(low(mul(q_t[own], scores_grad, NT)))
-        d_q.append(low(mul(k_t[own], scores_grad) * SCALE))
-    d_q = jnp.concatenate(d_q, 0).T
-    d_k = jnp.concatenate(d_k, 0).T
-    d_v = jnp.concatenate(d_v, 0).T
-    columns = pl.ds(pl.multiple_of(group * WIDE, WIDE), WIDE)
-    qvb_ref[0:1, columns] += jnp.sum(wide(d_q), 0, keepdims=True)
-    qvb_ref[1:2, columns] += jnp.sum(wide(d_v), 0, keepdims=True)
-    half_set = pl.ds(pl.multiple_of(group % 2 * WIDE, WIDE), WIDE)
-    total = acc_ref[...]
-    for i, grad in enumerate((d_q, d_k, d_v)):
-        weight = set_weight(w_ref.at[group // 2], slot_ref, group // 2, i, half_set)
-        total = total + mul(grad, weight, NT)
-    acc_ref[...] = total
+    def body(arriving):
+        if arriving:
+            qvb_ref[...] = jnp.zeros_like(qvb_ref)
+            fetch(rest[:count], w_ref, sem)
+        d_q, d_k, d_v = [], [], []
+        for head in range(GROUP):
+            own = slice(head * HEAD_DIM, (head + 1) * HEAD_DIM)
+            pair = slice(head // 2 * PAIR, (head // 2 + 1) * PAIR)
+            q_t, k_t, d_out_t = qk_ref[0, 0, own], qk_ref[1, 0, own], dctx_ref[0, own]
+            scores = mul(kv_ref[0, :, pair], half_rows(q_t, head)) + bias_ref[...]
+            probs = jnp.exp(scores - lse_ref[0, 0, head : head + 1, :])
+            probs_grad = mul(kv_ref[1, :, pair], half_rows(d_out_t, head))
+            scores_grad = low(probs * (probs_grad - delta_ref[0, 0, head : head + 1, :]))
+            probs_low = low(probs)
+            d_v.append(low(mul(d_out_t, probs_low, NT)))
+            d_k.append(low(mul(q_t, scores_grad, NT)))
+            d_q.append(low(mul(k_t, scores_grad) * SCALE))
+        if arriving:
+            wait_all(fetch(rest[:count], w_ref, sem, start=False))
+        ones = jnp.ones((16, SLOTS), jnp.bfloat16)
+        columns = pl.ds(pl.multiple_of(group * WIDE, WIDE), WIDE)
+        half_set = pl.ds(pl.multiple_of(group % 2 * WIDE, WIDE), WIDE)
+        total = acc_ref[...]
+        for i, grad in enumerate((d_q, d_k, d_v)):
+            grad = jnp.concatenate(grad, 0)
+            weight = set_weight(w_ref.at[group // 2], slot_ref, group // 2, i, half_set)
+            total = total + mul(grad, weight, TT)
+            if i != 1:
+                qvb_ref[i // 2 : i // 2 + 1, columns] += mul(ones, grad, NT)[0:1]
+        acc_ref[...] = total
+
+    first_or_later(row * GROUPS + group, body)
 
     @pl.when(group == GROUPS - 1)
     def _():
-        out_ref[...] = low(total)
+        out_ref[...] = low(acc_ref[...])
 
 
 def gelu_and_slope(v):
@@ -218,24 +235,29 @@
 
 
 def front_kernel(count, slot_ref, x_ref, ctx_ref, vec_ref, bi_ref, *rest):
-    normal_ref, inv_ref, branch_ref, slope_ref, first_ref, sem = rest[-6:]
+    normal_ref, inv_ref, branch_ref, slope_ref, low_ref, first_ref, sem = rest[-7:]
+
 
     @pl.when(pl.program_id(0) == 0)
     def _():
-        for copy in fetch(rest[:count], first_ref, sem):
-            copy.wait()
+        wait_all(fetch(rest[:count], first_ref, sem))
 
     out_bias, gain_one, bias_one, down_bias, _, _ = vectors_of(vec_ref)
-    ctx = ctx_ref[...]
     attention = out_bias
     for group in range(GROUPS):
-        columns = slice(group * WIDE, (group + 1) * WIDE)
-        attention = attention + mul(ctx[:, columns], out_columns(first_ref, slot_ref, group), NT)
-    normed, normal_one, inverse_one = norm_forward(wide(x_ref[...]) + attention, gain_one, bias_one)
-    normal_ref[...] = normal_one
-    inv_ref[...] = jnp.broadcast_to(inverse_one, inv_ref.shape)
-    normed_low = low(normed)
-    branch = normed + down_bias
+        part = slice(group * WIDE, (group + 1) * WIDE)
+        attention = attention + mul(ctx_ref[0, part], out_columns(first_ref, slot_ref, group), TT)
+    branch_ref[...] = attention
+    for start in range(0, TILE, STRIP):
+        rows = slice(start, start + STRIP)
+        normed, normal_one, inverse_one = norm_forward(wide(x_ref[rows]) + branch_ref[rows], gain_one, bias_one)
+        normal_ref[rows] = normal_one
+        inv_ref[rows] = jnp.broadcast_to(inverse_one, (STRIP, 128))
+        low_ref[rows] = low(normed)
+        branch_ref[rows] = normed + down_bias
+    normed_low = low_ref[...]
+    branch = branch_ref[...]
+
     for piece in range(PIECES):
         flat = slice(piece * HIDDEN, (piece + 1) * HIDDEN)
         inner = mul(normed_low, piece_weight(first_ref, None, slot_ref, piece, 0)) + bi_ref[0:1, flat]
@@ -246,23 +268,29 @@
 
 
 def back_kernel(
-    counts, slot_ref, normal_ref, inv_ref, branch_ref, slope_ref, ct_ref, vec_ref, bi_ref, *rest
+    counts, slot_ref, normal_ref, inv_ref, branch_ref, slope_ref, ct_ref, ctx_ref, vec_ref, bi_ref, *rest
 ):
-    out_ref, dctx_ref, sum_ref, vecg_ref, big_ref, keep_ref, first_ref, first_sem, late_ref, late_sem = rest[-10:]
+    out_ref, dctx_ref, delta_ref, sum_ref, vecg_ref, big_ref, keep_ref, acc_ref, low_ref, first_ref, first_sem, late_ref, late_sem = rest[-13:]
+
 
     @pl.when(pl.program_id(0) == 0)
     def _():
         vecg_ref[...] = jnp.zeros_like(vecg_ref)
         big_ref[...] = jnp.zeros_like(big_ref)
         late = fetch(rest[counts[0] : sum(counts)], late_ref, late_sem)
-        for copy in late + fetch(rest[: counts[0]], first_ref, first_sem):
-            copy.wait()
+        wait_all(late + fetch(rest[: counts[0]], first_ref, first_sem))
 
     _, gain_one, bias_one, _, gain_two, bias_two = vectors_of(vec_ref)
     weight = partial(piece_weight, first_ref, late_ref, slot_ref)
-    normal_one = normal_ref[...]
-    inverse_one = inv_ref[:, 0:1]
-    normed_low = low(normal_one * gain_one + bias_one)
+    strips = [slice(start, start + STRIP) for start in range(0, TILE, STRIP)]
+
+    def add(total, term):
+        term = jnp.sum(term.reshape(STRIP // 8, 8, D), 0)
+        return term if total is None else total + term
+
+    for rows in strips:
+        low_ref[rows] = low(normal_ref[rows] * gain_one + bias_one)
+    normed_low = low_ref[...]
     branch = branch_ref[...]
     for piece in range(PIECES, FF // HIDDEN):
         flat = slice(piece * HIDDEN, (piece + 1) * HIDDEN)
@@ -270,12 +298,19 @@
         act, slope = gelu_and_slope(inner)
         keep_ref[:, (piece - PIECES) * HIDDEN : (piece - PIECES + 1) * HIDDEN] = low(slope)
         branch = branch + mul(low(act), weight(piece, 1), NT)
-    final, normal_two, inverse_two = norm_forward(branch, gain_two, bias_two)
-    out_ref[...] = low(final)
-    final_grad = wide(ct_ref[...])
-    sum_two = norm_backward(final_grad, normal_two, inverse_two, gain_two)
-    branch_grad = low(sum_two)
-    normed_grad = sum_two
+    acc_ref[...] = branch
+    sums = [None] * 4
+    for rows in strips:
+        final, normal_two, inverse_two = norm_forward(acc_ref[rows], gain_two, bias_two)
+        out_ref[rows] = low(final)
+        final_grad = wide(ct_ref[rows])
+        sum_two = norm_backward(final_grad, normal_two, inverse_two, gain_two)
+        acc_ref[rows] = sum_two
+        low_ref[rows] = low(sum_two)
+        sums[2] = add(sums[2], wide(low(sum_two)))
+        sums[3] = add(sums[3], final_grad)
+    branch_grad = low_ref[...]
+    normed_grad = acc_ref[...]
     for piece in range(FF // HIDDEN):
         flat = slice(piece * HIDDEN, (piece + 1) * HIDDEN)
         if piece < PIECES:
@@ -285,12 +320,22 @@
         inner_grad = low(mul(branch_grad, weight(piece, 1)) * wide(slope))
         big_ref[0:1, flat] += jnp.sum(wide(inner_grad), 0, keepdims=True)
         normed_grad = normed_grad + mul(inner_grad, weight(piece, 0), NT)
-    sum_one = low(norm_backward(normed_grad, normal_one, inverse_one, gain_one))
-    sum_ref[...] = sum_one
+    acc_ref[...] = normed_grad
+    for rows in strips:
+        normed_grad = acc_ref[rows]
+        sum_one = low(norm_backward(normed_grad, normal_ref[rows], inv_ref[rows, 0:1], gain_one))
+        sum_ref[rows] = sum_one
+        sums[0] = add(sums[0], wide(sum_one))
+        sums[1] = add(sums[1], normed_grad)
+    sum_one = sum_ref[...]
     for group in range(GROUPS):
-        columns = slice(group * WIDE, (group + 1) * WIDE)
-        dctx_ref[:, columns] = low(mul(sum_one, out_columns(first_ref, slot_ref, group)))
-    sums = (wide(sum_one), normed_grad, wide(branch_grad), final_grad)
+        part = slice(group * WIDE, (group + 1) * WIDE)
+        context_grad = low(mul(sum_one, out_columns(first_ref, slot_ref, group))).T
+        dctx_ref[0, part] = context_grad
+        product = wide(context_grad) * wide(ctx_ref[0, part])
+        for head in range(GROUP):
+            own = slice(head * HEAD_DIM, (head + 1) * HEAD_DIM)
+            delta_ref[0, group, head : head + 1, :] = jnp.sum(product[own], 0, keepdims=True)
     for i, term in enumerate(sums):
         vecg_ref[i : i + 1, :] += jnp.sum(term, 0, keepdims=True)
 
@@ -337,13 +382,15 @@
         ]
         + [ANYWHERE] * (len(pieces) + len(earlier)),
         out_specs=[
-            pl.BlockSpec((3, SLOTS, WIDE), lambda r: (0, r, step)),
-            pl.BlockSpec((SLOTS, WIDE), lambda r: (r, step)),
+            pl.BlockSpec((2, 1, WIDE, SLOTS), lambda r: (0, r, step, 0)),
+            pl.BlockSpec((2, SLOTS, WIDE), lambda r: (0, r, step)),
+            pl.BlockSpec((1, WIDE, SLOTS), lambda r: (r, step, 0)),
             pl.BlockSpec((1, 1, GROUP, SLOTS), lambda r: (r, step, 0, 0)),
         ],
         out_shape=[
-            jax.ShapeDtypeStruct((3, rows * SLOTS, D), jnp.bfloat16),
-            jax.ShapeDtypeStruct((rows * SLOTS, D), jnp.bfloat16),
+            jax.ShapeDtypeStruct((2, rows, D, SLOTS), jnp.bfloat16),
+            jax.ShapeDtypeStruct((2, rows * SLOTS, D), jnp.bfloat16),
+            jax.ShapeDtypeStruct((rows, D, SLOTS), jnp.bfloat16),
             jax.ShapeDtypeStruct((rows, GROUPS, GROUP, SLOTS), jnp.float32),
         ],
         scratch_shapes=[
@@ -357,17 +404,18 @@
     )(fills, slots, tokens, seg_col, seg_row, bias, *pieces, *earlier)
 
 
-def attend_back(qkv, context, context_grad, lse, seg_col, seg_row, fills, slots, weights, sum_one):
-    rows = context.shape[0] // SLOTS
+def attend_back(qk, kv, context_grad, delta, lse, seg_col, seg_row, fills, slots, weights, sum_one):
+    rows = kv.shape[1] // SLOTS
     return pl.pallas_call(
         partial(attend_back_kernel, len(weights)),
         grid=(rows, GROUPS),
         in_specs=[
             SCALARS,
             SCALARS,
-            pl.BlockSpec((3, SLOTS, WIDE), lambda r, g: (0, r, g)),
-            pl.BlockSpec((SLOTS, WIDE), lambda r, g: (r, g)),
-            pl.BlockSpec((SLOTS, WIDE), lambda r, g: (r, g)),
+            pl.BlockSpec((2, 1, WIDE, SLOTS), lambda r, g: (0, r, g, 0)),
+            pl.BlockSpec((2, SLOTS, WIDE), lambda r, g: (0, r, g)),
+            pl.BlockSpec((1, WIDE, SLOTS), lambda r, g: (r, g, 0)),
+            pl.BlockSpec((1, 1, GROUP, SLOTS), lambda r, g: (r, g, 0, 0)),
             pl.BlockSpec((1, 1, GROUP, SLOTS), lambda r, g: (r, g, 0, 0)),
             pl.BlockSpec((1, SLOTS, 1), lambda r, g: (r, 0, 0)),
             pl.BlockSpec((1, 1, SLOTS), lambda r, g: (r, 0, 0)),
@@ -390,11 +438,15 @@
         compiler_params=params(2),
         cost_estimate=cost(50e9, 30e6),
         name="attend_back",
-    )(fills, slots, qkv, context, context_grad, lse, seg_col, seg_row, *weights, sum_one)
+    )(fills, slots, qk, kv, context_grad, delta, lse, seg_col, seg_row, *weights, sum_one)
 
 
 def tiles(width):
     return pl.BlockSpec((TILE, width), lambda i: (i, 0))
+
+
+PER_ROW = SLOTS // TILE
+ROWS_T = pl.BlockSpec((1, D, TILE), lambda i: (i // PER_ROW, 0, i % PER_ROW))
 
 
 def feed_front(slots, tokens, context, first, vectors, in_bias):
@@ -402,7 +454,7 @@
     return pl.pallas_call(
         partial(front_kernel, len(first)),
         grid=(count // TILE,),
-        in_specs=[SCALARS, tiles(D), tiles(D), whole(vectors), whole(in_bias)] + [ANYWHERE] * len(first),
+        in_specs=[SCALARS, tiles(D), ROWS_T, whole(vectors), whole(in_bias)] + [ANYWHERE] * len(first),
         out_specs=[tiles(D), tiles(128), tiles(D), tiles(2 * FLAT)],
         out_shape=[
             jax.ShapeDtypeStruct((count, D), jnp.float32),
@@ -410,39 +462,47 @@
             jax.ShapeDtypeStruct((count, D), jnp.float32),
             jax.ShapeDtypeStruct((count, 2 * FLAT), jnp.bfloat16),
         ],
-        scratch_shapes=slot_scratch(first),
+        scratch_shapes=[pltpu.VMEM((TILE, D), jnp.bfloat16)] + slot_scratch(first),
         compiler_params=params(1),
         cost_estimate=cost(25e9, 30e6),
         name="feed_front",
     )(slots, tokens, context, vectors, in_bias, *first)
 
 
-def feed_back(slots, front, cotangent, first, late, vectors, in_bias):
+def feed_back(slots, front, cotangent, context, first, late, vectors, in_bias):
     count = cotangent.shape[0]
     return pl.pallas_call(
         partial(back_kernel, (len(first), len(late))),
         grid=(count // TILE,),
-        in_specs=[SCALARS, tiles(D), tiles(128), tiles(D), tiles(2 * FLAT), tiles(D), whole(vectors), whole(in_bias)]
+        in_specs=[SCALARS, tiles(D), tiles(128), tiles(D), tiles(2 * FLAT), tiles(D), ROWS_T, whole(vectors), whole(in_bias)]
         + [ANYWHERE] * (len(first) + len(late)),
         out_specs=[
             tiles(D),
-            tiles(D),
+            ROWS_T,
+            pl.BlockSpec((1, GROUPS, GROUP, TILE), lambda i: (i // PER_ROW, 0, 0, i % PER_ROW)),
             tiles(D),
             pl.BlockSpec((8, D), lambda i: (0, 0)),
             pl.BlockSpec((8, FF), lambda i: (0, 0)),
         ],
         out_shape=[
             jax.ShapeDtypeStruct((count, D), jnp.bfloat16),
-            jax.ShapeDtypeStruct((count, D), jnp.bfloat16),
+            jax.ShapeDtypeStruct((count // SLOTS, D, SLOTS), jnp.bfloat16),
+            jax.ShapeDtypeStruct((count // SLOTS, GROUPS, GROUP, SLOTS), jnp.float32),
             jax.ShapeDtypeStruct((count, D), jnp.bfloat16),
             jax.ShapeDtypeStruct((8, D), jnp.float32),
             jax.ShapeDtypeStruct((8, FF), jnp.float32),
         ],
-        scratch_shapes=[pltpu.VMEM((TILE, FF - 2 * FLAT), jnp.bfloat16)] + slot_scratch(first) + slot_scratch(late),
+        scratch_shapes=[
+            pltpu.VMEM((TILE, FF - 2 * FLAT), jnp.bfloat16),
+            pltpu.VMEM((TILE, D), jnp.float32),
+            pltpu.VMEM((TILE, D), jnp.bfloat16),
+        ]
+        + slot_scratch(first)
+        + slot_scratch(late),
         compiler_params=params(1),
         cost_estimate=cost(75e9, 40e6),
         name="feed_back",
-    )(slots, *front, cotangent, vectors, in_bias, *first, *late)
+    )(slots, *front, cotangent, context, vectors, in_bias, *first, *late)
 
 
 def stage_bits(n):
@@ -581,13 +641,13 @@
     results, late_own = together(results, late_own)
     late_own = spread(late_own, [last])
 
-    qkv, context, lse = results
+    qk, kv, context, lse = results
     first = first_own + first_others
     front = feed_front(slots, tokens, context, first, vectors, b_hidden)
     front, late_own = together(front, late_own)
     late = late_own + [swap_cores(w) for w in late_own]
-    layer_out, context_grad, sum_one, vec_grads, in_grads = feed_back(
-        slots, front, cotangent, first, late, vectors, b_hidden
+    layer_out, context_grad, delta, sum_one, vec_grads, in_grads = feed_back(
+        slots, front, cotangent, context, first, late, vectors, b_hidden
     )
     hidden = in_grads[0].reshape(2, 2, FF // 4)
     hidden = jnp.where(core == 0, hidden, hidden[:, ::-1]).transpose(1, 0, 2)
@@ -596,7 +656,7 @@
     vec = early[: 4 * D].reshape(4, D)
 
     tokens_grad, qv_grads = attend_back(
-        qkv, context, context_grad, lse, seg_col, seg_row, fills, slots, q_own + q_others, sum_one
+        qk, kv, context_grad, delta, lse, seg_col, seg_row, fills, slots, q_own + q_others, sum_one
     )
     qv = qv_grads[:2].reshape(2, 2, D // 2)
     qv = jnp.where(core == 0, qv, qv[:, ::-1]).reshape(2, D)

time: 389 us -> 373 us (0.959)
  Pallas kernels: 262 us -> 239 us
    pallas_call x4, Pallas kernels: 63 us -> 55.4 us  [attend(): pl.pallas_call(partial(attend_kernel, step, len(pieces)), grid=(rows,), i...]
    pallas_call x1, Pallas kernels: 87.7 us -> 81.3 us  [feed_back(): pl.pallas_call(partial(back_kernel, (len(first), len(late))), grid=(count...]
    pallas_call x1, Pallas kernels: 71.4 us -> 66.3 us  [attend_back(): pl.pallas_call(partial(attend_back_kernel, len(weights)), grid=(rows, GRO...]
    ppermute x15, waiting for transfers between devices: 38.6 us -> 43.7 us  [partner(): return lax.ppermute(block, ('rows', 'tp'), pairs)]
  transfers between devices with their start and end apart: 34 -> 34, of which waited for: 13 -> 14; matrix products, arithmetic and copies ran while one was open for 5% -> 5% of each run, Pallas kernels for 45% -> 42%
where the time goes in v3:
time: 373 us; the launch traced here: 372 us
  Pallas kernels  239 us (64%)
  waiting for transfers between devices  58.2 us (16%)
  starting transfers between devices  31.9 us (9%)
  local copies, waits for them, and re-layouts  22.6 us (6%)
  between operations  14.5 us (4%)
  other arithmetic  5.49 us (1%)
    pallas_call x1, Pallas kernels, feed_back(): pl.pallas_call(partial(back_kernel, (len(first), len(late))), grid=(count...  81.3 us
    pallas_call x1, Pallas kernels, attend_back(): pl.pallas_call(partial(attend_back_kernel, len(weights)), grid=(rows, GRO...  66.3 us
    pallas_call x4, Pallas kernels, attend(): pl.pallas_call(partial(attend_kernel, step, len(pieces)), grid=(rows,), i...  55.4 us
    ppermute x15, waiting for transfers between devices, partner(): return lax.ppermute(block, ('rows', 'tp'), pairs)  43.7 us
    pallas_call x1, Pallas kernels, feed_front(): pl.pallas_call(partial(front_kernel, len(first)), grid=(count // TILE,),...  36 us
    ppermute x15, starting transfers between devices, partner(): return lax.ppermute(block, ('rows', 'tp'), pairs)  18.8 us
    unnamed x40, local copies, waits for them, and re-layouts  10.2 us
    ppermute x4, starting transfers between devices, sum_over_all(): lax.ppermute(values, 'rows', [(i, i ^ step) for i in range(n)])  9.24 us
  transfers between devices with their start and end apart: 34, of which 14 were waited for; matrix products, arithmetic and copies ran while one was open for 5% of the time, Pallas kernels for 42%

profile of v3, /device:TPU:0, one launch (start us, length us, event | category | flops | bytes accessed | tf_op | source)
XLA Modules:
  0.0 371.6 jit_solution(7014637754457193640)
XLA Ops:
  9.1 2.6 collective-permute-start
  19.3 2.7 collective-permute-start.1
  22.9 9.4 %collective-permute-done.1 = bf16[2,3,64,512]{3,2,1,0:T(8,128)(2,1)S(1)} collective-permute-done((bf16[2,3,64,512]{3,2,1,0:T(8,128)(2,1)S(1)}, bf16[2,3,64,512]{3,2,1,0:T(8,128)(2,1)S(1)}, u32[]{:S(2)}, u32[]{:S(2)}) %collective-permute-start.1) | collective-permute-done | bytes 393248 | tf_op jit(solution)/shard_map/ppermute | solution.py:522
  33.3 1.6 collective-permute-start.2
  38.4 8.6 %collective-permute-done.3 = bf16[1,64,2560]{2,1,0:T(8,128)(2,1)S(1)} collective-permute-done((bf16[1,64,2560]{2,1,0:T(8,128)(2,1)S(1)}, bf16[1,64,2560]{2,1,0:T(8,128)(2,1)S(1)}, u32[]{:S(2)}, u32[]{:S(2)}) %collective-permute-start.3) | collective-permute-done | bytes 327712 | tf_op jit(solution)/shard_map/ppermute | solution.py:522
  47.1 1.5 collective-permute-start.7
  48.6 1.5 collective-permute-start.5
  54.1 11.6 %collective-permute-done.7 = bf16[2,64,2560]{2,1,0:T(8,128)(2,1)S(1)} collective-permute-done((bf16[2,64,2560]{2,1,0:T(8,128)(2,1)S(1)}, bf16[2,64,2560]{2,1,0:T(8,128)(2,1)S(1)}, u32[]{:S(2)}, u32[]{:S(2)}) %collective-permute-start.7) | collective-permute-done | bytes 655392 | tf_op jit(solution)/shard_map/ppermute | solution.py:522
  65.7 3.5 collective-permute-done.6.rest_3_
  69.1 2.5 collective-permute-start.9
  73.5 4.0 %collective-permute-done.9 = bf16[1,64,2048]{2,1,0:T(8,128)(2,1)S(1)} collective-permute-done((bf16[1,64,2048]{2,1,0:T(8,128)(2,1)S(1)}, bf16[1,64,2048]{2,1,0:T(8,128)(2,1)S(1)}, u32[]{:S(2)}, u32[]{:S(2)}) %collective-permute-start.9) | collective-permute-done | bytes 262176 | tf_op jit(solution)/shard_map/ppermute | solution.py:522
  78.3 13.9 %attend.4 = (bf16[2,4,1024,512]{3,2,1,0:T(8,128)(2,1)}, bf16[2,2048,1024]{2,1,0:T(8,128)(2,1)}, bf16[4,1024,512]{2,1,0:T(8,128)(2,1)}, f32[4,4,4,512]{3,2,1,0:T(4,128)}) custom-call(s32[4]{0:T(128)} %dynamic_slice.7.fill_ref, s32[2,16]{1,0:T(2,128)} %add_select_fusion.slot_ref, bf16[2048,1024]{1,0:T(8,128)(2,1)} %x_ref.9, s32[4,512,1]{2,1,0:T(8,128)} %copy.53.segc_ref, ...), custom_call_target="tpu_custom_call" | custom-call | flops 15000000512 | bytes 10000000 | tf_op jit(solution)/shard_map/attend/pallas_call | solution.py:372
  92.2 3.3 collective-permute-done.8.rest_1_
  95.6 1.9 collective-permute-start.14
  97.7 13.8 %attend.5 = (bf16[2,4,1024,512]{3,2,1,0:T(8,128)(2,1)}, bf16[2,2048,1024]{2,1,0:T(8,128)(2,1)}, bf16[4,1024,512]{2,1,0:T(8,128)(2,1)}, f32[4,4,4,512]{3,2,1,0:T(4,128)}) custom-call(s32[4]{0:T(128)} %dynamic_slice.7.fill_ref, s32[2,16]{1,0:T(2,128)} %add_select_fusion.slot_ref, ...), custom_call_target="tpu_custom_call", output_to_operand_aliasing={{0}: (10, {}), {1}: (11, {}), {2}: (12, {}), {3}: (13, {})} | custom-call | flops 15000000512 | bytes 10000000 | tf_op jit(solution)/shard_map/attend/pallas_call | solution.py:372
  111.6 13.8 %attend.6 = (bf16[2,4,1024,512]{3,2,1,0:T(8,128)(2,1)}, bf16[2,2048,1024]{2,1,0:T(8,128)(2,1)}, bf16[4,1024,512]{2,1,0:T(8,128)(2,1)}, f32[4,4,4,512]{3,2,1,0:T(4,128)}) custom-call(s32[4]{0:T(128)} %dynamic_slice.7.fill_ref, s32[2,16]{1,0:T(2,128)} %add_select_fusion.slot_ref, ...), custom_call_target="tpu_custom_call", output_to_operand_aliasing={{0}: (10, {}), {1}: (11, {}), {2}: (12, {}), {3}: (13, {})} | custom-call | flops 15000000512 | bytes 10000000 | tf_op jit(solution)/shard_map/attend/pallas_call | solution.py:372
  125.5 3.2 collective-permute-done.15.rest_3_
  130.1 13.8 %attend.7 = (bf16[2,4,1024,512]{3,2,1,0:T(8,128)(2,1)}, bf16[2,2048,1024]{2,1,0:T(8,128)(2,1)}, bf16[4,1024,512]{2,1,0:T(8,128)(2,1)}, f32[4,4,4,512]{3,2,1,0:T(4,128)}) custom-call(s32[4]{0:T(128)} %dynamic_slice.7.fill_ref, s32[2,16]{1,0:T(2,128)} %add_select_fusion.slot_ref, ...), custom_call_target="tpu_custom_call", output_to_operand_aliasing={{0}: (10, {}), {1}: (11, {}), {2}: (12, {}), {3}: (13, {})} | custom-call | flops 15000000512 | bytes 10000000 | tf_op jit(solution)/shard_map/attend/pallas_call | solution.py:372
  144.0 2.3 collective-permute-start.22
  147.3 36.0 %feed_front.1 = (f32[2048,1024]{1,0:T(8,128)}, f32[2048,128]{1,0:T(8,128)}, f32[2048,1024]{1,0:T(8,128)}, bf16[2048,2048]{1,0:T(8,128)(2,1)}) custom-call(s32[2,16]{1,0:T(2,128)} %add_select_fusion.slot_ref, bf16[2048,1024]{1,0:T(8,128)(2,1)} %x_ref.9, bf16[4,1024,512]{2,1,0:T(8,128)(2,1)} %get-tuple-element.138.ctx_ref, f32[8,1024]{1,0:T(8,128)} %reshape.143.vec_ref, ...), custom_call_target="tpu_custom_call" | custom-call | flops 24999999488 | bytes 30000000 | tf_op jit(solution)/shard_map/feed_front/pallas_call | solution.py:454
  184.4 1.6 collective-permute-done.24.rest_12_
  186.1 4.5 %collective-permute-done.25.rest_13_ = bf16[4,64,2048]{2,1,0:T(8,128)(2,1)S(1)} collective-permute-done((bf16[4,64,2048]{2,1,0:T(8,128)(2,1)S(1)}, bf16[4,64,2048]{2,1,0:T(8,128)(2,1)S(1)}, u32[]{:S(2)}, u32[]{:S(2)}) %collective-permute-start.25) | collective-permute-done | bytes 1048608 | tf_op jit(solution)/shard_map/ppermute | solution.py:530
  192.5 81.3 %feed_back.1 = (bf16[2048,1024]{1,0:T(8,128)(2,1)}, bf16[4,1024,512]{2,1,0:T(8,128)(2,1)}, f32[4,4,4,512]{3,2,1,0:T(4,128)}, bf16[2048,1024]{1,0:T(8,128)(2,1)}, f32[8,1024]{1,0:T(8,128)}, /*index=5*/f32[8,4096]{1,0:T(8,128)}) custom-call(s32[2,16]{1,0:T(2,128)} %add_select_fusion.slot_ref, f32[2048,1024]{1,0:T(8,128)} %get-tuple-element.151.normal_ref, ...), custom_call_target="tpu_custom_call" | custom-call | flops 74999996416 | bytes 40000000 | tf_op jit(solution)/shard_map/feed_back/pallas_call | solution.py:474
  276.3 66.3 %attend_back.1 = (bf16[2048,1024]{1,0:T(8,128)(2,1)}, f32[8,1024]{1,0:T(8,128)}) custom-call(s32[4]{0:T(128)} %dynamic_slice.7.fill_ref, s32[2,16]{1,0:T(2,128)} %add_select_fusion.slot_ref, bf16[2,4,1024,512]{3,2,1,0:T(8,128)(2,1)} %get-tuple-element.160.qk_ref, bf16[2,2048,1024]{2,1,0:T(8,128)(2,1)} %get-tuple-element.161.kv_ref, ...), custom_call_target="tpu_custom_call" | custom-call | flops 49999998976 | bytes 30000000 | tf_op jit(solution)/shard_map/attend_back/pallas_call | solution.py:409
  346.1 2.3 collective-permute-done.29
  348.5 1.9 collective-permute-start.30
  350.4 1.7 collective-permute-done.30
  352.1 2.8 collective-permute-start.31
  355.0 1.6 collective-permute-done.31
  356.6 3.2 collective-permute-start.32
  359.8 1.6 collective-permute-done.32
  362.0 1.4 reshape.144
  (128 shorter events, 35.3 us)
Async XLA Ops:
  7.2 354.8 %all-gather.3.cloned.1.call-start = ((), (), s32[]{:S(2)}) async-start(), calls=%async_computation | async-start | bytes 1081344 | tf_op jit(solution)/shard_map/all_gather | solution.py:655
  8.6 29.1 %collective-permute-start.4 = (bf16[3072]{0:T(1024)(128)(2,1)S(1)}, bf16[3072]{0:T(1024)(128)(2,1)S(1)}, u32[]{:S(2)}, u32[]{:S(2)}) collective-permute-start(bf16[3072]{0:T(1024)(128)(2,1)S(1)} %constant_dynamic-update-slice_fusion.7), channel_id=1, source_target_pairs={{0,1},{1,0},{2,3},{3,2},{4,5},{5,4},{6,7},{7,6},{8,9},{9,8},{10,11... | collective-permute-start | bytes 18440 | tf_op jit(solution)/shard_map/ppermute | solution.py:530
  9.1 9.3 %collective-permute-start = (bf16[1,3,64,512]{3,2,1,0:T(8,128)(2,1)}, bf16[1,3,64,512]{3,2,1,0:T(8,128)(2,1)S(1)}, u32[]{:S(2)}, u32[]{:S(2)}) collective-permute-start(bf16[1,3,64,512]{3,2,1,0:T(8,128)(2,1)} %bitcast.24), channel_id=1, source_target_pairs={{0,8},{1,17},{2,10},{3,19},{4,12},{5,21},{6,14},{7,23},{8,0},{9,25... | collective-permute-start | bytes 589832 | tf_op jit(solution)/shard_map/ppermute | solution.py:522
  19.3 13.0 %collective-permute-start.1 = (bf16[2,3,64,512]{3,2,1,0:T(8,128)(2,1)S(1)}, bf16[2,3,64,512]{3,2,1,0:T(8,128)(2,1)S(1)}, u32[]{:S(2)}, u32[]{:S(2)}) collective-permute-start(bf16[2,3,64,512]{3,2,1,0:T(8,128)(2,1)S(1)} %pad_maximum_fusion.3), channel_id=1, source_target_pairs={{0,16},{1,9},{2,18},{3,11},{4,20},{5,13},{6,22},{7,15},{8,24},{9,1... | collective-permute-start | bytes 1179656 | tf_op jit(solution)/shard_map/ppermute | solution.py:522
  33.3 13.8 %collective-permute-start.2 = (bf16[4,3,64,512]{3,2,1,0:T(8,128)(2,1)S(1)}, bf16[4,3,64,512]{3,2,1,0:T(8,128)(2,1)}, u32[]{:S(2)}, u32[]{:S(2)}) collective-permute-start(bf16[4,3,64,512]{3,2,1,0:T(8,128)(2,1)S(1)} %pad_maximum_fusion.rest_0_), channel_id=1, source_target_pairs={{0,4},{1,3},{2,6},{3,1},{4,0},{5,7},{6,2},{7,5},{8,12},{9,11},{10,... | collective-permute-start | bytes 2359304 | tf_op jit(solution)/shard_map/ppermute | solution.py:522
  37.4 9.7 %collective-permute-start.3 = (bf16[1,64,2560]{2,1,0:T(8,128)(2,1)S(1)}, bf16[1,64,2560]{2,1,0:T(8,128)(2,1)S(1)}, u32[]{:S(2)}, u32[]{:S(2)}) collective-permute-start(bf16[1,64,2560]{2,1,0:T(8,128)(2,1)S(1)} %maximum_bitcast_fusion), channel_id=1, source_target_pairs={{0,8},{1,17},{2,10},{3,19},{4,12},{5,21},{6,14},{7,23},{8,0},{9,25... | collective-permute-start | bytes 983048 | tf_op jit(solution)/shard_map/ppermute | solution.py:522
  47.1 18.6 %collective-permute-start.7 = (bf16[2,64,2560]{2,1,0:T(8,128)(2,1)S(1)}, bf16[2,64,2560]{2,1,0:T(8,128)(2,1)S(1)}, u32[]{:S(2)}, u32[]{:S(2)}) collective-permute-start(bf16[2,64,2560]{2,1,0:T(8,128)(2,1)S(1)} %pad_maximum_fusion.1), channel_id=1, source_target_pairs={{0,16},{1,9},{2,18},{3,11},{4,20},{5,13},{6,22},{7,15},{8,24},{9,1... | collective-permute-start | bytes 1966088 | tf_op jit(solution)/shard_map/ppermute | solution.py:522
  48.6 17.1 %collective-permute-start.5 = (bf16[4,3,64,512]{3,2,1,0:T(8,128)(2,1)S(1)}, bf16[4,3,64,512]{3,2,1,0:T(8,128)(2,1)}, u32[]{:S(2)}, u32[]{:S(2)}) collective-permute-start(bf16[4,3,64,512]{3,2,1,0:T(8,128)(2,1)S(1)} %pad_maximum_fusion.rest_0_), channel_id=1, source_target_pairs={{0,2},{1,5},{2,0},{3,7},{4,6},{5,1},{6,4},{7,3},{8,10},{9,13},{10,... | collective-permute-start | bytes 2359304 | tf_op jit(solution)/shard_map/ppermute | solution.py:522
  50.1 19.0 %collective-permute-start.6 = (bf16[4,3,64,512]{3,2,1,0:T(8,128)(2,1)}, bf16[4,3,64,512]{3,2,1,0:T(8,128)(2,1)}, u32[]{:S(2)}, u32[]{:S(2)}) collective-permute-start(bf16[4,3,64,512]{3,2,1,0:T(8,128)(2,1)} %collective-permute-done.2.rest_1_), channel_id=1, source_target_pairs={{0,2},{1,5},{2,0},{3,7},{4,6},{5,1},{6,4},{7,3},{8,10},{9,13},{10,... | collective-permute-start | bytes 2359304 | tf_op jit(solution)/shard_map/ppermute | solution.py:522
  69.1 8.4 %collective-permute-start.9 = (bf16[1,64,2048]{2,1,0:T(8,128)(2,1)S(1)}, bf16[1,64,2048]{2,1,0:T(8,128)(2,1)S(1)}, u32[]{:S(2)}, u32[]{:S(2)}) collective-permute-start(bf16[1,64,2048]{2,1,0:T(8,128)(2,1)S(1)} %maximum_bitcast_fusion.1), channel_id=1, source_target_pairs={{0,8},{1,17},{2,10},{3,19},{4,12},{5,21},{6,14},{7,23},{8,0},{9,25... | collective-permute-start | bytes 786440 | tf_op jit(solution)/shard_map/ppermute | solution.py:522
  71.6 20.5 %collective-permute-start.10 = (bf16[4,3,64,512]{3,2,1,0:T(8,128)(2,1)S(1)}, bf16[4,3,64,512]{3,2,1,0:T(8,128)(2,1)S(1)}, u32[]{:S(2)}, u32[]{:S(2)}) collective-permute-start(bf16[4,3,64,512]{3,2,1,0:T(8,128)(2,1)S(1)} %pad_maximum_fusion.rest_0_), channel_id=1, source_target_pairs={{0,1},{1,0},{2,3},{3,2},{4,5},{5,4},{6,7},{7,6},{8,9},{9,8},{10,11... | collective-permute-start | bytes 2359304 | tf_op jit(solution)/shard_map/ppermute | solution.py:530
  71.6 20.5 %collective-permute-start.11 = (bf16[4,3,64,512]{3,2,1,0:T(8,128)(2,1)}, bf16[4,3,64,512]{3,2,1,0:T(8,128)(2,1)}, u32[]{:S(2)}, u32[]{:S(2)}) collective-permute-start(bf16[4,3,64,512]{3,2,1,0:T(8,128)(2,1)} %collective-permute-done.2.rest_1_), channel_id=1, source_target_pairs={{0,1},{1,0},{2,3},{3,2},{4,5},{5,4},{6,7},{7,6},{8,9},{9,8},{10,11... | collective-permute-start | bytes 2359304 | tf_op jit(solution)/shard_map/ppermute | solution.py:530
  72.1 20.0 %collective-permute-start.12 = (bf16[4,3,64,512]{3,2,1,0:T(8,128)(2,1)}, bf16[4,3,64,512]{3,2,1,0:T(8,128)(2,1)}, u32[]{:S(2)}, u32[]{:S(2)}) collective-permute-start(bf16[4,3,64,512]{3,2,1,0:T(8,128)(2,1)} %collective-permute-done.5.rest_2_), channel_id=1, source_target_pairs={{0,1},{1,0},{2,3},{3,2},{4,5},{5,4},{6,7},{7,6},{8,9},{9,8},{10,11... | collective-permute-start | bytes 2359304 | tf_op jit(solution)/shard_map/ppermute | solution.py:530
  72.1 20.1 %collective-permute-start.13 = (bf16[4,3,64,512]{3,2,1,0:T(8,128)(2,1)}, bf16[4,3,64,512]{3,2,1,0:T(8,128)(2,1)}, u32[]{:S(2)}, u32[]{:S(2)}) collective-permute-start(bf16[4,3,64,512]{3,2,1,0:T(8,128)(2,1)} %collective-permute-done.6.rest_3_), channel_id=1, source_target_pairs={{0,1},{1,0},{2,3},{3,2},{4,5},{5,4},{6,7},{7,6},{8,9},{9,8},{10,11... | collective-permute-start | bytes 2359304 | tf_op jit(solution)/shard_map/ppermute | solution.py:530
  77.6 17.9 %collective-permute-start.8 = (bf16[4,64,2560]{2,1,0:T(8,128)(2,1)}, bf16[4,64,2560]{2,1,0:T(8,128)(2,1)}, u32[]{:S(2)}, u32[]{:S(2)}) collective-permute-start(bf16[4,64,2560]{2,1,0:T(8,128)(2,1)} %constant_dynamic-update-slice_fusion.2.rest_0_), channel_id=1, source_target_pairs={{0,4},{1,3},{2,6},{3,1},{4,0},{5,7},{6,2},{7,5},{8,12},{9,11},{10,... | collective-permute-start | bytes 3932168 | tf_op jit(solution)/shard_map/ppermute | solution.py:522
  95.6 29.9 %collective-permute-start.16 = (bf16[2,64,2048]{2,1,0:T(8,128)(2,1)S(1)}, bf16[2,64,2048]{2,1,0:T(8,128)(2,1)S(1)}, u32[]{:S(2)}, u32[]{:S(2)}) collective-permute-start(bf16[2,64,2048]{2,1,0:T(8,128)(2,1)S(1)} %pad_maximum_fusion.2), channel_id=1, source_target_pairs={{0,16},{1,9},{2,18},{3,11},{4,20},{5,13},{6,22},{7,15},{8,24},{9,1... | collective-permute-start | bytes 1572872 | tf_op jit(solution)/shard_map/ppermute | solution.py:522
  95.6 29.8 %collective-permute-start.14 = (bf16[4,64,2560]{2,1,0:T(8,128)(2,1)}, bf16[4,64,2560]{2,1,0:T(8,128)(2,1)}, u32[]{:S(2)}, u32[]{:S(2)}) collective-permute-start(bf16[4,64,2560]{2,1,0:T(8,128)(2,1)} %constant_dynamic-update-slice_fusion.2.rest_0_), channel_id=1, source_target_pairs={{0,2},{1,5},{2,0},{3,7},{4,6},{5,1},{6,4},{7,3},{8,10},{9,13},{10,... | collective-permute-start | bytes 3932168 | tf_op jit(solution)/shard_map/ppermute | solution.py:522
  97.5 31.2 %collective-permute-start.15 = (bf16[4,64,2560]{2,1,0:T(8,128)(2,1)}, bf16[4,64,2560]{2,1,0:T(8,128)(2,1)}, u32[]{:S(2)}, u32[]{:S(2)}) collective-permute-start(bf16[4,64,2560]{2,1,0:T(8,128)(2,1)} %collective-permute-done.8.rest_1_), channel_id=1, source_target_pairs={{0,2},{1,5},{2,0},{3,7},{4,6},{5,1},{6,4},{7,3},{8,10},{9,13},{10,... | collective-permute-start | bytes 3932168 | tf_op jit(solution)/shard_map/ppermute | solution.py:522
  128.7 15.2 %collective-permute-start.17 = (bf16[4,64,2048]{2,1,0:T(8,128)(2,1)S(1)}, bf16[4,64,2048]{2,1,0:T(8,128)(2,1)S(1)}, u32[]{:S(2)}, u32[]{:S(2)}) collective-permute-start(bf16[4,64,2048]{2,1,0:T(8,128)(2,1)S(1)} %constant_dynamic-update-slice_fusion.4.rest_8_), channel_id=1, source_target_pairs={{0,4},{1,3},{2,6},{3,1},{4,0},{5,7},{6,2},{7,5},{8,12},{9,11},{10,... | collective-permute-start | bytes 3145736 | tf_op jit(solution)/shard_map/ppermute | solution.py:522
  129.1 17.2 %collective-permute-start.18 = (bf16[4,64,2560]{2,1,0:T(8,128)(2,1)}, bf16[4,64,2560]{2,1,0:T(8,128)(2,1)S(1)}, u32[]{:S(2)}, u32[]{:S(2)}) collective-permute-start(bf16[4,64,2560]{2,1,0:T(8,128)(2,1)} %constant_dynamic-update-slice_fusion.2.rest_0_), channel_id=1, source_target_pairs={{0,1},{1,0},{2,3},{3,2},{4,5},{5,4},{6,7},{7,6},{8,9},{9,8},{10,11... | collective-permute-start | bytes 3932168 | tf_op jit(solution)/shard_map/ppermute | solution.py:530
  129.1 17.3 %collective-permute-start.19 = (bf16[4,64,2560]{2,1,0:T(8,128)(2,1)}, bf16[4,64,2560]{2,1,0:T(8,128)(2,1)}, u32[]{:S(2)}, u32[]{:S(2)}) collective-permute-start(bf16[4,64,2560]{2,1,0:T(8,128)(2,1)} %collective-permute-done.8.rest_1_), channel_id=1, source_target_pairs={{0,1},{1,0},{2,3},{3,2},{4,5},{5,4},{6,7},{7,6},{8,9},{9,8},{10,11... | collective-permute-start | bytes 3932168 | tf_op jit(solution)/shard_map/ppermute | solution.py:530
  129.6 16.8 %collective-permute-start.20 = (bf16[4,64,2560]{2,1,0:T(8,128)(2,1)}, bf16[4,64,2560]{2,1,0:T(8,128)(2,1)}, u32[]{:S(2)}, u32[]{:S(2)}) collective-permute-start(bf16[4,64,2560]{2,1,0:T(8,128)(2,1)} %collective-permute-done.14.rest_2_), channel_id=1, source_target_pairs={{0,1},{1,0},{2,3},{3,2},{4,5},{5,4},{6,7},{7,6},{8,9},{9,8},{10,11... | collective-permute-start | bytes 3932168 | tf_op jit(solution)/shard_map/ppermute | solution.py:530
  129.6 16.8 %collective-permute-start.21 = (bf16[4,64,2560]{2,1,0:T(8,128)(2,1)}, bf16[4,64,2560]{2,1,0:T(8,128)(2,1)}, u32[]{:S(2)}, u32[]{:S(2)}) collective-permute-start(bf16[4,64,2560]{2,1,0:T(8,128)(2,1)} %collective-permute-done.15.rest_3_), channel_id=1, source_target_pairs={{0,1},{1,0},{2,3},{3,2},{4,5},{5,4},{6,7},{7,6},{8,9},{9,8},{10,11... | collective-permute-start | bytes 3932168 | tf_op jit(solution)/shard_map/ppermute | solution.py:530
  144.0 39.3 %collective-permute-start.22 = (bf16[4,64,2048]{2,1,0:T(8,128)(2,1)S(1)}, bf16[4,64,2048]{2,1,0:T(8,128)(2,1)}, u32[]{:S(2)}, u32[]{:S(2)}) collective-permute-start(bf16[4,64,2048]{2,1,0:T(8,128)(2,1)S(1)} %constant_dynamic-update-slice_fusion.4.rest_8_), channel_id=1, source_target_pairs={{0,2},{1,5},{2,0},{3,7},{4,6},{5,1},{6,4},{7,3},{8,10},{9,13},{10,... | collective-permute-start | bytes 3145736 | tf_op jit(solution)/shard_map/ppermute | solution.py:522
  146.3 37.0 %collective-permute-start.23 = (bf16[4,64,2048]{2,1,0:T(8,128)(2,1)S(1)}, bf16[4,64,2048]{2,1,0:T(8,128)(2,1)}, u32[]{:S(2)}, u32[]{:S(2)}) collective-permute-start(bf16[4,64,2048]{2,1,0:T(8,128)(2,1)S(1)} %collective-permute-done.17.rest_9_), channel_id=1, source_target_pairs={{0,2},{1,5},{2,0},{3,7},{4,6},{5,1},{6,4},{7,3},{8,10},{9,13},{10,... | collective-permute-start | bytes 3145736 | tf_op jit(solution)/shard_map/ppermute | solution.py:522
  183.4 7.1 %collective-permute-start.25 = (bf16[4,64,2048]{2,1,0:T(8,128)(2,1)S(1)}, bf16[4,64,2048]{2,1,0:T(8,128)(2,1)S(1)}, u32[]{:S(2)}, u32[]{:S(2)}) collective-permute-start(bf16[4,64,2048]{2,1,0:T(8,128)(2,1)S(1)} %collective-permute-done.17.rest_9_), channel_id=1, source_target_pairs={{0,1},{1,0},{2,3},{3,2},{4,5},{5,4},{6,7},{7,6},{8,9},{9,8},{10,11... | collective-permute-start | bytes 3145736 | tf_op jit(solution)/shard_map/ppermute | solution.py:530
  183.9 7.6 %collective-permute-start.26 = (bf16[4,64,2048]{2,1,0:T(8,128)(2,1)}, bf16[4,64,2048]{2,1,0:T(8,128)(2,1)S(1)}, u32[]{:S(2)}, u32[]{:S(2)}) collective-permute-start(bf16[4,64,2048]{2,1,0:T(8,128)(2,1)} %collective-permute-done.22.rest_10_), channel_id=1, source_target_pairs={{0,1},{1,0},{2,3},{3,2},{4,5},{5,4},{6,7},{7,6},{8,9},{9,8},{10,11... | collective-permute-start | bytes 3145736 | tf_op jit(solution)/shard_map/ppermute | solution.py:530
  184.0 8.5 %collective-permute-start.27 = (bf16[4,64,2048]{2,1,0:T(8,128)(2,1)}, bf16[4,64,2048]{2,1,0:T(8,128)(2,1)}, u32[]{:S(2)}, u32[]{:S(2)}) collective-permute-start(bf16[4,64,2048]{2,1,0:T(8,128)(2,1)} %collective-permute-done.23.rest_11_), channel_id=1, source_target_pairs={{0,1},{1,0},{2,3},{3,2},{4,5},{5,4},{6,7},{7,6},{8,9},{9,8},{10,11... | collective-permute-start | bytes 3145736 | tf_op jit(solution)/shard_map/ppermute | solution.py:530
  344.8 3.7 collective-permute-start.29
  348.5 3.7 collective-permute-start.30
  352.1 4.5 %collective-permute-start.31 = (f32[2,1024]{1,0:T(2,128)S(1)}, f32[2,1024]{1,0:T(2,128)S(1)}, u32[]{:S(2)}, u32[]{:S(2)}) collective-permute-start(f32[2,1024]{1,0:T(2,128)S(1)} %add.88), channel_id=1, source_target_pairs={{0,8},{2,10},{4,12},{6,14},{8,0},{10,2},{12,4},{14,6},{16,24},{18,... | collective-permute-start | bytes 24584 | tf_op jit(solution)/shard_map/ppermute | solution.py:554
  356.6 4.8 %collective-permute-start.32 = (f32[2,1024]{1,0:T(2,128)S(1)}, f32[2,1024]{1,0:T(2,128)S(1)}, u32[]{:S(2)}, u32[]{:S(2)}) collective-permute-start(f32[2,1024]{1,0:T(2,128)S(1)} %add.89), channel_id=1, source_target_pairs={{0,16},{2,18},{4,20},{6,22},{8,24},{10,26},{12,28},{14,30},{16,0},... | collective-permute-start | bytes 24584 | tf_op jit(solution)/shard_map/ppermute | solution.py:554
  (14 other events, 305.3 us)
Sparse Core Ops, SparseCore 0:
  276.4 55.3 all-gather.2

commit v4 on v3

--- a/solution.py
+++ b/solution.py
@@ -18,7 +18,6 @@
 PAIR = 2 * HEAD_DIM
 GROUPS = HEADS // GROUP
 TILE = 256
-HIDDEN = 1024
 STRIP = 32
 EPSILON = 1e-05
 MASKED = -1e30
@@ -71,17 +70,22 @@
     return jnp.concatenate([rows, zeros] if head % 2 == 0 else [zeros, rows], 0)
 
 
-def fetch(refs, scratch, sem, columns=None, start=True):
+def fetch(refs, scratch, sem, start=True):
     copies = []
-    half = len(refs) // 2
     for i, ref in enumerate(refs):
         size = ref.shape[0]
-        target = scratch.at[i // half, pl.ds(i % half * size, size)]
-        if columns is not None:
-            ref, target = ref.at[:, :, columns], target.at[:, :, columns]
-        copies.append(pltpu.make_async_copy(ref, target, sem.at[i]))
+        copies.append(pltpu.make_async_copy(ref, scratch.at[pl.ds(i * size, size)], sem.at[i]))
         if start:
             copies[-1].start()
+    return copies
+
+
+def fetch_sets(refs, scratch, sem, start=True):
+    sets = scratch.shape[0]
+    size = len(refs) // sets
+    copies = []
+    for i in range(sets):
+        copies += fetch(refs[i * size : (i + 1) * size], scratch.at[i], sem.at[i], start)
     return copies
 
 
@@ -100,9 +104,8 @@
         copy.wait()
 
 
-def set_weight(w_ref, slot_ref, other, part, columns=slice(None)):
-    parts = [w_ref[slot_ref[other, c], part, :, columns] for c in range(w_ref.shape[0])]
-    return jnp.concatenate(parts, 0)
+def set_weight(w_ref, slot_ref, other, part):
+    return jnp.concatenate([w_ref[slot_ref[other, c], part] for c in range(w_ref.shape[0])], 0)
 
 
 def columns_of(w_ref, slot_ref, other, columns):
@@ -111,25 +114,21 @@
 
 
 def attend_kernel(step, count, fill_ref, slot_ref, x_ref, segc_ref, segr_ref, b_ref, *rest):
+    other, half = step % 2, step // 2
     qk_ref, kv_ref, ctx_ref, lse_ref, w_ref, sem = rest[-6:]
 
     @pl.when(pl.program_id(0) == 0)
     def _():
-        copies = []
-        for i, ref in enumerate(rest[:count]):
-            size = ref.shape[0]
-            source = ref.at[:, :, :, pl.ds(step % 2 * WIDE, WIDE)]
-            copies.append(pltpu.make_async_copy(source, w_ref.at[pl.ds(i * size, size)], sem.at[i]))
-            copies[-1].start()
-        for copy in copies:
-            copy.wait()
+        wait_all(fetch(rest[:count], w_ref, sem))
 
     x = x_ref[...]
-    weight = [set_weight(w_ref, slot_ref, step // 2, i) for i in range(3)]
+    weight = [set_weight(w_ref, slot_ref, other, i) for i in range(3)]
+    columns = slice(half * WIDE, (half + 1) * WIDE)
+    b_q, b_v = wide(b_ref[0:1, columns]), wide(b_ref[1:2, columns])
     bias = mask_bias(segc_ref[0], segr_ref[0], fill_ref[pl.program_id(0)])
-    q = low(mul(x, weight[0]) + b_ref[0:1, :])
+    q = low(mul(x, weight[0]) + b_q)
     k = low(mul(x, weight[1]))
-    v = low(mul(x, weight[2]) + b_ref[1:2, :])
+    v = low(mul(x, weight[2]) + b_v)
     q_t = (q * jnp.bfloat16(SCALE)).T
     v_t = v.T
     qk_ref[0, 0] = q_t
@@ -175,7 +174,7 @@
     def body(arriving):
         if arriving:
             qvb_ref[...] = jnp.zeros_like(qvb_ref)
-            fetch(rest[:count], w_ref, sem)
+            fetch_sets(rest[:count], w_ref, sem)
         d_q, d_k, d_v = [], [], []
         for head in range(GROUP):
             own = slice(head * HEAD_DIM, (head + 1) * HEAD_DIM)
@@ -190,14 +189,13 @@
             d_k.append(low(mul(q_t, scores_grad, NT)))
             d_q.append(low(mul(k_t, scores_grad) * SCALE))
         if arriving:
-            wait_all(fetch(rest[:count], w_ref, sem, start=False))
+            wait_all(fetch_sets(rest[:count], w_ref, sem, start=False))
         ones = jnp.ones((16, SLOTS), jnp.bfloat16)
         columns = pl.ds(pl.multiple_of(group * WIDE, WIDE), WIDE)
-        half_set = pl.ds(pl.multiple_of(group % 2 * WIDE, WIDE), WIDE)
         total = acc_ref[...]
         for i, grad in enumerate((d_q, d_k, d_v)):
             grad = jnp.concatenate(grad, 0)
-            weight = set_weight(w_ref.at[group // 2], slot_ref, group // 2, i, half_set)
+            weight = set_weight(w_ref.at[group], slot_ref, group % 2, i)
             total = total + mul(grad, weight, TT)
             if i != 1:
                 qvb_ref[i // 2 : i // 2 + 1, columns] += mul(ones, grad, NT)[0:1]
@@ -216,33 +214,49 @@
     return v * phi, phi + v * bell
 
 
-FLAT = 1024
-PIECES = 2 * FLAT // HIDDEN
+FIRST = 1024
+LATE = FF // 2 - FIRST
+LATE_PIECE = 1024
+PIECES = [(False, other, 0, FIRST) for other in range(2)]
+PIECES += [(True, other, start, LATE_PIECE) for other in range(2) for start in range(0, LATE, LATE_PIECE)]
+
+
+def flat_of(piece):
+    late, other, start, size = piece
+    begin = 2 * FIRST + other * LATE + start if late else other * FIRST
+    return slice(begin, begin + size)
+
+
+def first_columns(first_ref, slot_ref, other, columns):
+    n, _, chunk, _ = first_ref.shape
+    return first_ref[:, slot_ref[2, 0] ^ other, :, columns].reshape(n * chunk, columns.size)
 
 
 def piece_weight(first_ref, late_ref, slot_ref, piece, down):
-    ref, width = (first_ref, FLAT) if piece < PIECES else (late_ref, FF // 2 - FLAT)
-    other, start = divmod(piece % PIECES * HIDDEN, width)
-    return columns_of(ref, slot_ref, other, pl.ds(down * width + start, HIDDEN))
+    late, other, start, size = piece
+    if late:
+        return columns_of(late_ref, slot_ref, other, pl.ds(down * LATE + start, size))
+    return first_columns(first_ref, slot_ref, other, pl.ds(down * FIRST + start, size))
+
+
+def piece_bias(b_refs, piece):
+    late, other, start, size = piece
+    begin = FIRST * late + start
+    return wide(b_refs[other][begin : begin + size]).reshape(1, size)
 
 
 def out_columns(first_ref, slot_ref, group):
-    return columns_of(first_ref, slot_ref, group // 2, pl.ds(2 * FLAT + group % 2 * WIDE, WIDE))
-
-
-def vectors_of(vec_ref):
-    return [vec_ref[i : i + 1, :] for i in range(6)]
-
-
-def front_kernel(count, slot_ref, x_ref, ctx_ref, vec_ref, bi_ref, *rest):
-    normal_ref, inv_ref, branch_ref, slope_ref, low_ref, first_ref, sem = rest[-7:]
-
-
-    @pl.when(pl.program_id(0) == 0)
-    def _():
-        wait_all(fetch(rest[:count], first_ref, sem))
-
-    out_bias, gain_one, bias_one, down_bias, _, _ = vectors_of(vec_ref)
+    return first_columns(first_ref, slot_ref, group % 2, pl.ds(2 * FIRST + group // 2 * WIDE, WIDE))
+
+
+def row_of(ref):
+    return wide(ref[...]).reshape(1, D)
+
+
+def front_kernel(
+    slot_ref, x_ref, ctx_ref, vec_refs, bi_refs, first_ref, normal_ref, inv_ref, branch_ref, slope_ref, low_ref
+):
+    out_bias, gain_one, bias_one, down_bias = [row_of(ref) for ref in vec_refs]
     attention = out_bias
     for group in range(GROUPS):
         part = slice(group * WIDE, (group + 1) * WIDE)
@@ -258,29 +272,27 @@
     normed_low = low_ref[...]
     branch = branch_ref[...]
 
-    for piece in range(PIECES):
-        flat = slice(piece * HIDDEN, (piece + 1) * HIDDEN)
-        inner = mul(normed_low, piece_weight(first_ref, None, slot_ref, piece, 0)) + bi_ref[0:1, flat]
+    for piece in PIECES[:2]:
+        inner = mul(normed_low, piece_weight(first_ref, None, slot_ref, piece, 0)) + piece_bias(bi_refs, piece)
         act, slope = gelu_and_slope(inner)
-        slope_ref[:, flat] = low(slope)
+        slope_ref[:, flat_of(piece)] = low(slope)
         branch = branch + mul(low(act), piece_weight(first_ref, None, slot_ref, piece, 1), NT)
     branch_ref[...] = branch
 
 
 def back_kernel(
-    counts, slot_ref, normal_ref, inv_ref, branch_ref, slope_ref, ct_ref, ctx_ref, vec_ref, bi_ref, *rest
+    count, slot_ref, normal_ref, inv_ref, branch_ref, slope_ref, ct_ref, ctx_ref, vec_refs, bi_refs, first_ref, *rest
 ):
-    out_ref, dctx_ref, delta_ref, sum_ref, vecg_ref, big_ref, keep_ref, acc_ref, low_ref, first_ref, first_sem, late_ref, late_sem = rest[-13:]
+    out_ref, dctx_ref, delta_ref, sum_ref, vecg_ref, big_ref, keep_ref, acc_ref, low_ref, late_ref, late_sem = rest[-11:]
 
 
     @pl.when(pl.program_id(0) == 0)
     def _():
         vecg_ref[...] = jnp.zeros_like(vecg_ref)
         big_ref[...] = jnp.zeros_like(big_ref)
-        late = fetch(rest[counts[0] : sum(counts)], late_ref, late_sem)
-        wait_all(late + fetch(rest[: counts[0]], first_ref, first_sem))
-
-    _, gain_one, bias_one, _, gain_two, bias_two = vectors_of(vec_ref)
+        wait_all(fetch_sets(rest[:count], late_ref, late_sem))
+
+    gain_one, bias_one, gain_two, bias_two = [row_of(ref) for ref in vec_refs]
     weight = partial(piece_weight, first_ref, late_ref, slot_ref)
     strips = [slice(start, start + STRIP) for start in range(0, TILE, STRIP)]
 
@@ -292,11 +304,11 @@
         low_ref[rows] = low(normal_ref[rows] * gain_one + bias_one)
     normed_low = low_ref[...]
     branch = branch_ref[...]
-    for piece in range(PIECES, FF // HIDDEN):
-        flat = slice(piece * HIDDEN, (piece + 1) * HIDDEN)
-        inner = mul(normed_low, weight(piece, 0)) + bi_ref[0:1, flat]
+    for piece in PIECES[2:]:
+        inner = mul(normed_low, weight(piece, 0)) + piece_bias(bi_refs, piece)
         act, slope = gelu_and_slope(inner)
-        keep_ref[:, (piece - PIECES) * HIDDEN : (piece - PIECES + 1) * HIDDEN] = low(slope)
+        flat = flat_of(piece)
+        keep_ref[:, flat.start - 2 * FIRST : flat.stop - 2 * FIRST] = low(slope)
         branch = branch + mul(low(act), weight(piece, 1), NT)
     acc_ref[...] = branch
     sums = [None] * 4
@@ -311,12 +323,9 @@
         sums[3] = add(sums[3], final_grad)
     branch_grad = low_ref[...]
     normed_grad = acc_ref[...]
-    for piece in range(FF // HIDDEN):
-        flat = slice(piece * HIDDEN, (piece + 1) * HIDDEN)
-        if piece < PIECES:
-            slope = slope_ref[:, flat]
-        else:
-            slope = keep_ref[:, (piece - PIECES) * HIDDEN : (piece - PIECES + 1) * HIDDEN]
+    for piece in PIECES:
+        flat = flat_of(piece)
+        slope = keep_ref[:, flat.start - 2 * FIRST : flat.stop - 2 * FIRST] if piece[0] else slope_ref[:, flat]
         inner_grad = low(mul(branch_grad, weight(piece, 1)) * wide(slope))
         big_ref[0:1, flat] += jnp.sum(wide(inner_grad), 0, keepdims=True)
         normed_grad = normed_grad + mul(inner_grad, weight(piece, 0), NT)
@@ -354,16 +363,20 @@
 ANYWHERE = pl.BlockSpec(memory_space=pl.ANY)
 
 
+def wholes(arrays):
+    return tuple(whole(array) for array in arrays)
+
+
 def whole(array):
     return pl.BlockSpec(array.shape, lambda *_: (0,) * array.ndim, pipeline_mode=pl.Buffered(1))
 
 
-def slot_scratch(pieces):
-    half = len(pieces) // 2
-    n = sum(w.shape[0] for w in pieces[:half])
+def slot_scratch(pieces, sets):
+    count = len(pieces) // sets
+    n = sum(w.shape[0] for w in pieces[:count])
     return [
-        pltpu.VMEM((2, n) + pieces[0].shape[1:], pieces[0].dtype),
-        pltpu.SemaphoreType.DMA((len(pieces),)),
+        pltpu.VMEM((sets, n) + pieces[0].shape[1:], pieces[0].dtype),
+        pltpu.SemaphoreType.DMA((sets, count)),
     ]
 
 
@@ -394,7 +407,7 @@
             jax.ShapeDtypeStruct((rows, GROUPS, GROUP, SLOTS), jnp.float32),
         ],
         scratch_shapes=[
-            pltpu.VMEM((sum(w.shape[0] for w in pieces),) + pieces[0].shape[1:3] + (WIDE,), jnp.bfloat16),
+            pltpu.VMEM((sum(w.shape[0] for w in pieces),) + pieces[0].shape[1:], jnp.bfloat16),
             pltpu.SemaphoreType.DMA((len(pieces),)),
         ],
         input_output_aliases={6 + len(pieces) + i: i for i in range(len(earlier))},
@@ -434,7 +447,7 @@
             pltpu.VMEM((SLOTS, SLOTS), jnp.float32),
             pltpu.VMEM((SLOTS, D), jnp.float32),
         ]
-        + slot_scratch(weights),
+        + slot_scratch(weights, GROUPS),
         compiler_params=params(2),
         cost_estimate=cost(50e9, 30e6),
         name="attend_back",
@@ -452,30 +465,30 @@
 def feed_front(slots, tokens, context, first, vectors, in_bias):
     count = tokens.shape[0]
     return pl.pallas_call(
-        partial(front_kernel, len(first)),
+        front_kernel,
         grid=(count // TILE,),
-        in_specs=[SCALARS, tiles(D), ROWS_T, whole(vectors), whole(in_bias)] + [ANYWHERE] * len(first),
-        out_specs=[tiles(D), tiles(128), tiles(D), tiles(2 * FLAT)],
+        in_specs=[SCALARS, tiles(D), ROWS_T, wholes(vectors), wholes(in_bias), whole(first)],
+        out_specs=[tiles(D), tiles(128), tiles(D), tiles(2 * FIRST)],
         out_shape=[
             jax.ShapeDtypeStruct((count, D), jnp.float32),
             jax.ShapeDtypeStruct((count, 128), jnp.float32),
             jax.ShapeDtypeStruct((count, D), jnp.float32),
-            jax.ShapeDtypeStruct((count, 2 * FLAT), jnp.bfloat16),
+            jax.ShapeDtypeStruct((count, 2 * FIRST), jnp.bfloat16),
         ],
-        scratch_shapes=[pltpu.VMEM((TILE, D), jnp.bfloat16)] + slot_scratch(first),
+        scratch_shapes=[pltpu.VMEM((TILE, D), jnp.bfloat16)],
         compiler_params=params(1),
         cost_estimate=cost(25e9, 30e6),
         name="feed_front",
-    )(slots, tokens, context, vectors, in_bias, *first)
+    )(slots, tokens, context, vectors, in_bias, first)
 
 
 def feed_back(slots, front, cotangent, context, first, late, vectors, in_bias):
     count = cotangent.shape[0]
     return pl.pallas_call(
-        partial(back_kernel, (len(first), len(late))),
+        partial(back_kernel, len(late)),
         grid=(count // TILE,),
-        in_specs=[SCALARS, tiles(D), tiles(128), tiles(D), tiles(2 * FLAT), tiles(D), ROWS_T, whole(vectors), whole(in_bias)]
-        + [ANYWHERE] * (len(first) + len(late)),
+        in_specs=[SCALARS, tiles(D), tiles(128), tiles(D), tiles(2 * FIRST), tiles(D), ROWS_T, wholes(vectors), wholes(in_bias), whole(first)]
+        + [ANYWHERE] * len(late),
         out_specs=[
             tiles(D),
             ROWS_T,
@@ -493,16 +506,15 @@
             jax.ShapeDtypeStruct((8, FF), jnp.float32),
         ],
         scratch_shapes=[
-            pltpu.VMEM((TILE, FF - 2 * FLAT), jnp.bfloat16),
+            pltpu.VMEM((TILE, 2 * LATE), jnp.bfloat16),
             pltpu.VMEM((TILE, D), jnp.float32),
             pltpu.VMEM((TILE, D), jnp.bfloat16),
         ]
-        + slot_scratch(first)
-        + slot_scratch(late),
+        + slot_scratch(late, 2),
         compiler_params=params(1),
         cost_estimate=cost(75e9, 40e6),
         name="feed_back",
-    )(slots, *front, cotangent, context, vectors, in_bias, *first, *late)
+    )(slots, *front, cotangent, context, vectors, in_bias, first, *late)
 
 
 def stage_bits(n):
@@ -544,7 +556,8 @@
     for order in stage_bits(n):
         tables.append(sum(((apart >> bit) & 1) << place for place, bit in enumerate(order)))
     core = lax.axis_index("tp")
-    return jnp.where(core == 0, jnp.stack(tables), jnp.stack(tables[::-1]))
+    ordered = jnp.where(core == 0, jnp.stack(tables), jnp.stack(tables[::-1]))
+    return jnp.concatenate([ordered, jnp.full((1, n), core, jnp.int32)], 0)
 
 
 def sum_over_all(values, n):
@@ -578,88 +591,101 @@
     core = lax.axis_index("tp")
     rows_here = tokens.shape[0] // SLOTS
     down_t = down_weight.T
-    width = qv_bias.shape[1]
 
     last = n.bit_length() - 2
 
-    def spread(blocks, stages):
+    def spread(block, stages):
         for stage in stages:
-            blocks = blocks + [partner(block, n, stage) for block in blocks]
-        return blocks
-
-    middle = range(2, last)
-    q = qkv_weight[None]
-    q = joined(q, partner(q, n, 0))
-    q = joined(q, partner(q, n, 1))
-    first = jnp.concatenate([in_weight[:, :FLAT], down_t[:, :FLAT], out_weight.T], 1)[None]
-    q, first = together(q, first)
-    q_own = spread([q], middle)
-    first = joined(first, partner(first, n, 0))
+            block = joined(block, partner(block, n, stage))
+        return block
+
+    a = qkv_weight[None, :, :, :WIDE]
+    a = joined(a, partner(a, n, 0))
+    a, b = together(a, qkv_weight[None, :, :, WIDE:])
+    a_got = partner(a, n, 1)
+    b_got = partner(b, n, 0)
+    first = jnp.concatenate([in_weight[:, :FIRST], down_t[:, :FIRST], out_weight.T], 1)
+
+    a, a_got, b, b_got, first = together(a, a_got, b, b_got, first)
+    first = lax.all_gather(first, ("rows", "tp"), axis=0, tiled=False).reshape((n, 2) + first.shape)
+    a = joined(a, a_got)
+    b = joined(b, b_got)
+    for stage in range(2, last):
+        a_got = partner(a, n, stage)
+        a = a if stage == last - 1 else joined(a, a_got)
+    b_got = partner(b, n, 1)
     segments = lax.dynamic_slice_in_dim(segment_ids, core * rows_here, rows_here, 0)
     fills = lax.dynamic_slice_in_dim(fill_counts, core * rows_here, rows_here, 0)
-    seg_col = segments[:, :, None]
-    seg_row = segments[:, None, :]
     slots = slot_table(n)
-    own = jnp.concatenate([qv_bias.reshape(-1), in_bias])
-    other = swap_cores(own)
-    by_distance = [wide(b) for b in (own, other)]
-    b_qv = [b[: 2 * width].reshape(2, width) for b in by_distance]
-    b_in = [b[2 * width :] for b in by_distance]
-    b_hidden = jnp.concatenate([b_in[0][:FLAT], b_in[1][:FLAT], b_in[0][FLAT:], b_in[1][FLAT:]]).reshape(1, -1)
-    vectors = wide(
-        jnp.concatenate([out_bias, norm1_gain, norm1_bias, down_bias, norm2_gain, norm2_bias, out_bias, out_bias])
-    ).reshape(8, D)
-    small = (seg_col, seg_row, fills, slots, b_qv, b_hidden, vectors)
-    q_own, first, small = together(q_own, first, small)
-    seg_col, seg_row, fills, slots, b_qv, b_hidden, vectors = small
-    q_own = spread(q_own, [last])
-    first_got = partner(first, n, 1)
-
-    def run(step, earlier):
-        bias = b_qv[step // 2][:, step % 2 * WIDE : (step % 2 + 1) * WIDE]
-        pieces = q_others if step >= 2 else q_own
-        return attend(step, earlier, tokens, seg_col, seg_row, fills, slots, pieces, bias)
-
-    late = jnp.concatenate([in_weight[:, FLAT:], down_t[:, FLAT:]], 1)[None]
-    q_own, first_got, late = together(q_own, first_got, late)
-    first = joined(first, first_got)
-    q_others = [swap_cores(w) for w in q_own]
-    first_own = spread([first], middle)
+    small = (segments[:, :, None], segments[:, None, :], fills, slots)
+    b_qv = (qv_bias, swap_cores(qv_bias))
+    b_in = (in_bias, swap_cores(in_bias))
+    late = jnp.concatenate([in_weight[:, FIRST:], down_t[:, FIRST:]], 1)[None]
+
+    a, a_got, b, b_got, late, small, b_qv, b_in = together(a, a_got, b, b_got, late, small, b_qv, b_in)
+    a = joined(a, a_got)
+    a_other = swap_cores(a)
+    a_got = partner(a, n, last)
+    b = joined(b, b_got)
+
+    def run(step, earlier, *pieces):
+        return attend(step, earlier, tokens, *small, pieces, b_qv[step % 2])
+
+    a, a_got, a_other, b, late = together(a, a_got, a_other, b, late)
+    a_other_got = swap_cores(a_got)
+    for stage in range(2, last):
+        b_got = partner(b, n, stage)
+        b = b if stage == last - 1 else joined(b, b_got)
     late_got = partner(late, n, 0)
-    results = run(0, ())
-    results, first_own, late_got, q_others = together(results, first_own, late_got, q_others)
+    results = run(0, (), a, a_got)
+
+    results, a_other_got, b, b_got, late, late_got = together(results, a_other_got, b, b_got, late, late_got)
+    b = joined(b, b_got)
     late = joined(late, late_got)
-    first_own = spread(first_own, [last])
     late_got = partner(late, n, 1)
-    results = run(1, results)
-    results = run(2, results)
-    results, first_own, late_got = together(results, first_own, late_got)
+    b_other = swap_cores(b)
+    b_got = partner(b, n, last)
+    results = run(1, results, a_other, a_other_got)
+
+    results, b_other, b_got, late, late_got = together(results, b_other, b_got, late, late_got)
+    b_other_got = swap_cores(b_got)
     late = joined(late, late_got)
-    first_others = [swap_cores(w) for w in first_own]
-    late_own = spread([late], middle)
-    results = run(3, results)
-    results, late_own = together(results, late_own)
-    late_own = spread(late_own, [last])
+    for stage in range(2, last):
+        late_got = partner(late, n, stage)
+        late = late if stage == last - 1 else joined(late, late_got)
+    results = run(2, results, b, b_got)
+
+    results, b_other_got = together(results, b_other_got)
+    results = run(3, results, b_other, b_other_got)
+
+    results, late, late_got = together(results, late, late_got)
+    late_own = [late, late_got]
+    late_others = [swap_cores(w) for w in late_own]
+    late_far = [partner(w, n, last) for w in late_own]
 
     qk, kv, context, lse = results
-    first = first_own + first_others
-    front = feed_front(slots, tokens, context, first, vectors, b_hidden)
-    front, late_own = together(front, late_own)
-    late = late_own + [swap_cores(w) for w in late_own]
+    front = feed_front(slots, tokens, context, first, (out_bias, norm1_gain, norm1_bias, down_bias), b_in)
+
+    front, late_others, late_far = together(front, late_others, late_far)
+    late_others += [swap_cores(w) for w in late_far]
+    vectors = (norm1_gain, norm1_bias, norm2_gain, norm2_bias)
     layer_out, context_grad, delta, sum_one, vec_grads, in_grads = feed_back(
-        slots, front, cotangent, context, first, late, vectors, b_hidden
+        slots, front, cotangent, context, first, late_own + late_far + late_others, vectors, b_in
     )
-    hidden = in_grads[0].reshape(2, 2, FF // 4)
-    hidden = jnp.where(core == 0, hidden, hidden[:, ::-1]).transpose(1, 0, 2)
+    hidden = [in_grads[0, : 2 * FIRST].reshape(2, FIRST), in_grads[0, 2 * FIRST :].reshape(2, LATE)]
+    hidden = jnp.concatenate(hidden, 1)
+    hidden = jnp.where(core == 0, hidden, hidden[::-1])
     early = jnp.concatenate([vec_grads[:4].reshape(-1), hidden.reshape(-1)])
     early = jnp.sum(lax.all_gather(early, ("rows", "tp"), axis=0), 0)
     vec = early[: 4 * D].reshape(4, D)
 
+    a_set = [a, a_got, a_other, a_other_got]
+    b_set = [b, b_got, b_other, b_other_got]
     tokens_grad, qv_grads = attend_back(
-        qk, kv, context_grad, delta, lse, seg_col, seg_row, fills, slots, q_own + q_others, sum_one
+        qk, kv, context_grad, delta, lse, *small, a_set + b_set, sum_one
     )
-    qv = qv_grads[:2].reshape(2, 2, D // 2)
-    qv = jnp.where(core == 0, qv, qv[:, ::-1]).reshape(2, D)
+    qv = qv_grads[:2].reshape(2, 2, 2, WIDE)
+    qv = jnp.where(core == 0, qv, qv[:, :, ::-1]).transpose(0, 2, 1, 3).reshape(2, D)
     qv = sum_over_all(qv, n)
     return (layer_out, tokens_grad, qv, vec[0], vec[1], early[4 * D :], vec[2], vec[3])
 

time: 373 us -> 342 us (0.917)
  waiting for transfers between devices: 58.2 us -> 39 us
  local copies, waits for them, and re-layouts: 22.6 us -> 12.9 us
    ppermute x15 -> x13, waiting for transfers between devices: 43.7 us -> 19.9 us  [partner(): return lax.ppermute(block, ('rows', 'tp'), pairs)]
    unnamed x40 -> x36, local copies, waits for them, and re-layouts: 10.2 us -> 1.95 us
    ppermute x15 -> x13, starting transfers between devices: 18.8 us -> 24.5 us  [partner(): return lax.ppermute(block, ('rows', 'tp'), pairs)]
    all_gather x0 -> x1, waiting for transfers between devices: none -> 5.33 us  [shards(): lax.all_gather(first, ('rows', 'tp'), axis=0, tiled=False)]
  transfers between devices with their start and end apart: 34 -> 30, of which waited for: 14 -> 13; matrix products, arithmetic and copies ran while one was open for 5% -> 2% of each run, Pallas kernels for 42% -> 46%
where the time goes in v4:
time: 342 us; the launch traced here: 341 us
  Pallas kernels  238 us (70%)
  waiting for transfers between devices  39 us (11%)
  starting transfers between devices  34.5 us (10%)
  between operations  14.5 us (4%)
  local copies, waits for them, and re-layouts  12.9 us (4%)
    pallas_call x1, Pallas kernels, feed_back(): pl.pallas_call(partial(back_kernel, len(late)), grid=(count // TILE,), in...  81.5 us
    pallas_call x1, Pallas kernels, attend_back(): pl.pallas_call(partial(attend_back_kernel, len(weights)), grid=(rows, GRO...  66.1 us
    pallas_call x4, Pallas kernels, attend(): pl.pallas_call(partial(attend_kernel, step, len(pieces)), grid=(rows,), i...  55.5 us
    pallas_call x1, Pallas kernels, feed_front(): pl.pallas_call(front_kernel, grid=(count // TILE,), in_specs=[SCALARS, ti...  34.5 us
    ppermute x13, starting transfers between devices, partner(): return lax.ppermute(block, ('rows', 'tp'), pairs)  24.5 us
    ppermute x13, waiting for transfers between devices, partner(): return lax.ppermute(block, ('rows', 'tp'), pairs)  19.9 us
    ppermute x4, waiting for transfers between devices, sum_over_all(): lax.ppermute(values, 'rows', [(i, i ^ step) for i in range(n)])  8.94 us
  transfers between devices with their start and end apart: 30, of which 13 were waited for; matrix products, arithmetic and copies ran while one was open for 2% of the time, Pallas kernels for 46%

profile of v4, /device:TPU:0, one launch (start us, length us, event | category | flops | bytes accessed | tf_op | source)
XLA Modules:
  0.0 341.5 jit_solution(7489744757199237034)
XLA Ops:
  8.2 3.1 collective-permute-start
  12.4 2.5 collective-permute-done
  15.0 2.0 collective-permute-start.2
  16.9 2.6 collective-permute-start.1
  19.5 1.6 pad_maximum_fusion.1
  21.1 3.4 collective-permute-done.1
  25.2 1.6 collective-permute-start.3
  26.8 2.9 collective-permute-start.4
  32.2 2.0 collective-permute-done.4
  34.4 2.8 collective-permute-start.7
  38.7 8.8 %collective-permute-done.7.rest_1_ = bf16[8,3,64,256]{3,2,1,0:T(8,128)(2,1)S(1)} collective-permute-done((bf16[8,3,64,256]{3,2,1,0:T(8,128)(2,1)S(1)}, bf16[8,3,64,256]{3,2,1,0:T(8,128)(2,1)S(1)}, u32[]{:S(2)}, u32[]{:S(2)}) %collective-permute-start.7) | collective-permute-done | bytes 786464 | tf_op jit(solution)/shard_map/ppermute | solution.py:534
  47.5 1.5 collective-permute-start.11
  50.8 13.9 %attend.4 = (bf16[2,4,1024,512]{3,2,1,0:T(8,128)(2,1)}, bf16[2,2048,1024]{2,1,0:T(8,128)(2,1)}, bf16[4,1024,512]{2,1,0:T(8,128)(2,1)}, f32[4,4,4,512]{3,2,1,0:T(4,128)}) custom-call(s32[4]{0:T(128)} %dynamic_slice.7.fill_ref, s32[3,16]{1,0:T(4,128)} %concatenate.39.slot_ref, bf16[2048,1024]{1,0:T(8,128)(2,1)} %x_ref.9, s32[4,512,1]{2,1,0:T(8,128)} %copy.52.segc_ref, ...), custom_call_target="tpu_custom_call" | custom-call | flops 15000000512 | bytes 10000000 | tf_op jit(solution)/shard_map/attend/pallas_call | solution.py:385
  65.6 2.3 collective-permute-start.14
  67.9 13.9 %attend.5 = (bf16[2,4,1024,512]{3,2,1,0:T(8,128)(2,1)}, bf16[2,2048,1024]{2,1,0:T(8,128)(2,1)}, bf16[4,1024,512]{2,1,0:T(8,128)(2,1)}, f32[4,4,4,512]{3,2,1,0:T(4,128)}) custom-call(s32[4]{0:T(128)} %dynamic_slice.7.fill_ref, s32[3,16]{1,0:T(4,128)} %concatenate.39.slot_ref, ...), custom_call_target="tpu_custom_call", output_to_operand_aliasing={{0}: (8, {}), {1}: (9, {}), {2}: (10, {}), {3}: (11, {})} | custom-call | flops 15000000512 | bytes 10000000 | tf_op jit(solution)/shard_map/attend/pallas_call | solution.py:385
  81.8 3.2 collective-permute-done.14
  85.8 1.5 collective-permute-start.16
  87.3 13.8 %attend.6 = (bf16[2,4,1024,512]{3,2,1,0:T(8,128)(2,1)}, bf16[2,2048,1024]{2,1,0:T(8,128)(2,1)}, bf16[4,1024,512]{2,1,0:T(8,128)(2,1)}, f32[4,4,4,512]{3,2,1,0:T(4,128)}) custom-call(s32[4]{0:T(128)} %dynamic_slice.7.fill_ref, s32[3,16]{1,0:T(4,128)} %concatenate.39.slot_ref, ...), custom_call_target="tpu_custom_call", output_to_operand_aliasing={{0}: (8, {}), {1}: (9, {}), {2}: (10, {}), {3}: (11, {})} | custom-call | flops 15000000512 | bytes 10000000 | tf_op jit(solution)/shard_map/attend/pallas_call | solution.py:385
  101.1 13.8 %attend.7 = (bf16[2,4,1024,512]{3,2,1,0:T(8,128)(2,1)}, bf16[2,2048,1024]{2,1,0:T(8,128)(2,1)}, bf16[4,1024,512]{2,1,0:T(8,128)(2,1)}, f32[4,4,4,512]{3,2,1,0:T(4,128)}) custom-call(s32[4]{0:T(128)} %dynamic_slice.7.fill_ref, s32[3,16]{1,0:T(4,128)} %concatenate.39.slot_ref, ...), custom_call_target="tpu_custom_call", output_to_operand_aliasing={{0}: (8, {}), {1}: (9, {}), {2}: (10, {}), {3}: (11, {})} | custom-call | flops 15000000512 | bytes 10000000 | tf_op jit(solution)/shard_map/attend/pallas_call | solution.py:385
  117.8 5.3 %all-gather.5.cloned.1.call-done = bf16[2048,2560]{1,0:T(8,128)(2,1)} async-done(((bf16[64,2560]{1,0:T(8,128)(2,1)}), bf16[2048,2560]{1,0:T(8,128)(2,1)}) %all-gather.5.cloned.1.call-update) | async-done | bytes 10485776 | tf_op jit(solution)/shard_map/all_gather | solution.py:610
  123.2 34.5 %feed_front.1 = (f32[2048,1024]{1,0:T(8,128)}, f32[2048,128]{1,0:T(8,128)}, f32[2048,1024]{1,0:T(8,128)}, bf16[2048,2048]{1,0:T(8,128)(2,1)}) custom-call(s32[3,16]{1,0:T(4,128)} %concatenate.39.slot_ref, bf16[2048,1024]{1,0:T(8,128)(2,1)} %x_ref.9, bf16[4,1024,512]{2,1,0:T(8,128)(2,1)} %get-tuple-element.157.ctx_ref, bf16[1024]{0:T(1024)(128)(2,1)} %vec_refs_0_.2, ...), custom_call_target="tpu_custom_call" | custom-call | flops 24999999488 | bytes 30000000 | tf_op jit(solution)/shard_map/feed_front/pallas_call | solution.py:467
  158.3 2.4 collective-permute-done.21.rest_6_
  160.6 1.5 collective-permute-done.22.rest_7_
  163.1 81.5 %feed_back.1 = (bf16[2048,1024]{1,0:T(8,128)(2,1)}, bf16[4,1024,512]{2,1,0:T(8,128)(2,1)}, f32[4,4,4,512]{3,2,1,0:T(4,128)}, bf16[2048,1024]{1,0:T(8,128)(2,1)}, f32[8,1024]{1,0:T(8,128)}, /*index=5*/f32[8,4096]{1,0:T(8,128)}) custom-call(s32[3,16]{1,0:T(4,128)} %concatenate.39.slot_ref, f32[2048,1024]{1,0:T(8,128)} %get-tuple-element.167.normal_ref, ...), custom_call_target="tpu_custom_call" | custom-call | flops 74999996416 | bytes 40000000 | tf_op jit(solution)/shard_map/feed_back/pallas_call | solution.py:487
  247.5 66.1 %attend_back.1 = (bf16[2048,1024]{1,0:T(8,128)(2,1)}, f32[8,1024]{1,0:T(8,128)}) custom-call(s32[4]{0:T(128)} %dynamic_slice.7.fill_ref, s32[3,16]{1,0:T(4,128)} %concatenate.39.slot_ref, bf16[2,4,1024,512]{3,2,1,0:T(8,128)(2,1)} %get-tuple-element.176.qk_ref, bf16[2,2048,1024]{2,1,0:T(8,128)(2,1)} %get-tuple-element.177.kv_ref, ...), custom_call_target="tpu_custom_call" | custom-call | flops 49999998976 | bytes 30000000 | tf_op jit(solution)/shard_map/attend_back/pallas_call | solution.py:422
  316.9 2.5 collective-permute-done.24
  319.4 1.8 collective-permute-start.25
  321.2 1.9 collective-permute-done.25
  323.1 1.6 collective-permute-start.26
  324.7 2.0 collective-permute-done.26
  326.8 2.1 collective-permute-start.27
  328.8 2.5 collective-permute-done.27
  (115 shorter events, 24.0 us)
Async XLA Ops:
  7.2 116.0 %all-gather.5.cloned.1.call-start = ((), (), s32[]{:S(2)}) async-start(), calls=%async_computation | async-start | bytes 10813440 | tf_op jit(solution)/shard_map/all_gather | solution.py:610
  8.2 6.7 %collective-permute-start = (bf16[1,3,64,256]{3,2,1,0:T(8,128)(2,1)S(1)}, bf16[1,3,64,256]{3,2,1,0:T(8,128)(2,1)S(1)}, u32[]{:S(2)}, u32[]{:S(2)}) collective-permute-start(bf16[1,3,64,256]{3,2,1,0:T(8,128)(2,1)S(1)} %get-tuple-element.193), channel_id=1, source_target_pairs={{0,8},{1,17},{2,10},{3,19},{4,12},{5,21},{6,14},{7,23},{8,0},{9,25... | collective-permute-start | bytes 294920 | tf_op jit(solution)/shard_map/ppermute | solution.py:534
  15.0 6.1 %collective-permute-start.2 = (bf16[1,3,64,256]{3,2,1,0:T(8,128)(2,1)S(1)}, bf16[1,3,64,256]{3,2,1,0:T(8,128)(2,1)S(1)}, u32[]{:S(2)}, u32[]{:S(2)}) collective-permute-start(bf16[1,3,64,256]{3,2,1,0:T(8,128)(2,1)S(1)} %get-tuple-element.101), channel_id=1, source_target_pairs={{0,8},{1,17},{2,10},{3,19},{4,12},{5,21},{6,14},{7,23},{8,0},{9,25... | collective-permute-start | bytes 294920 | tf_op jit(solution)/shard_map/ppermute | solution.py:534
  16.9 7.5 %collective-permute-start.1 = (bf16[2,3,64,256]{3,2,1,0:T(8,128)(2,1)S(1)}, bf16[2,3,64,256]{3,2,1,0:T(8,128)(2,1)S(1)}, u32[]{:S(2)}, u32[]{:S(2)}) collective-permute-start(bf16[2,3,64,256]{3,2,1,0:T(8,128)(2,1)S(1)} %pad_maximum_fusion.2), channel_id=1, source_target_pairs={{0,16},{1,9},{2,18},{3,11},{4,20},{5,13},{6,22},{7,15},{8,24},{9,1... | collective-permute-start | bytes 589832 | tf_op jit(solution)/shard_map/ppermute | solution.py:534
  24.5 307.4 %all-gather.7.cloned.1.call-start = ((), (), s32[]{:S(2)}) async-start(), calls=%async_computation.1 | async-start | bytes 1081344 | tf_op jit(solution)/shard_map/all_gather | solution.py:679
  24.5 7.7 %collective-permute-start.5 = (bf16[2,512]{1,0:T(2,128)(2,1)}, bf16[2,512]{1,0:T(2,128)(2,1)S(1)}, u32[]{:S(2)}, u32[]{:S(2)}) collective-permute-start(bf16[2,512]{1,0:T(2,128)(2,1)} %b_ref.1), channel_id=1, source_target_pairs={{0,1},{1,0},{2,3},{3,2},{4,5},{5,4},{6,7},{7,6},{8,9},{9,8},{10,11... | collective-permute-start | bytes 6152 | tf_op jit(solution)/shard_map/ppermute | solution.py:542
  24.7 7.5 %collective-permute-start.6 = (bf16[2048]{0:T(1024)(128)(2,1)}, bf16[2048]{0:T(1024)(128)(2,1)S(1)}, u32[]{:S(2)}, u32[]{:S(2)}) collective-permute-start(bf16[2048]{0:T(1024)(128)(2,1)} %bi_refs_0_.1), channel_id=1, source_target_pairs={{0,1},{1,0},{2,3},{3,2},{4,5},{5,4},{6,7},{7,6},{8,9},{9,8},{10,11... | collective-permute-start | bytes 12296 | tf_op jit(solution)/shard_map/ppermute | solution.py:542
  25.2 9.1 %collective-permute-start.3 = (bf16[4,3,64,256]{3,2,1,0:T(8,128)(2,1)S(1)}, bf16[4,3,64,256]{3,2,1,0:T(8,128)(2,1)S(1)}, u32[]{:S(2)}, u32[]{:S(2)}) collective-permute-start(bf16[4,3,64,256]{3,2,1,0:T(8,128)(2,1)S(1)} %constant_dynamic-update-slice_fusion), channel_id=1, source_target_pairs={{0,4},{1,3},{2,6},{3,1},{4,0},{5,7},{6,2},{7,5},{8,12},{9,11},{10,... | collective-permute-start | bytes 1179656 | tf_op jit(solution)/shard_map/ppermute | solution.py:534
  26.8 7.5 %collective-permute-start.4 = (bf16[2,3,64,256]{3,2,1,0:T(8,128)(2,1)S(1)}, bf16[2,3,64,256]{3,2,1,0:T(8,128)(2,1)S(1)}, u32[]{:S(2)}, u32[]{:S(2)}) collective-permute-start(bf16[2,3,64,256]{3,2,1,0:T(8,128)(2,1)S(1)} %constant_dynamic-update-slice_fusion.2), channel_id=1, source_target_pairs={{0,16},{1,9},{2,18},{3,11},{4,20},{5,13},{6,22},{7,15},{8,24},{9,1... | collective-permute-start | bytes 589832 | tf_op jit(solution)/shard_map/ppermute | solution.py:534
  34.3 4.3 %collective-permute-start.8 = (bf16[8,3,64,256]{3,2,1,0:T(8,128)(2,1)S(1)}, bf16[8,3,64,256]{3,2,1,0:T(8,128)(2,1)S(1)}, u32[]{:S(2)}, u32[]{:S(2)}) collective-permute-start(bf16[8,3,64,256]{3,2,1,0:T(8,128)(2,1)S(1)} %constant_dynamic-update-slice_fusion.4.rest_0_), channel_id=1, source_target_pairs={{0,1},{1,0},{2,3},{3,2},{4,5},{5,4},{6,7},{7,6},{8,9},{9,8},{10,11... | collective-permute-start | bytes 2359304 | tf_op jit(solution)/shard_map/ppermute | solution.py:542
  34.4 13.1 %collective-permute-start.7 = (bf16[8,3,64,256]{3,2,1,0:T(8,128)(2,1)S(1)}, bf16[8,3,64,256]{3,2,1,0:T(8,128)(2,1)S(1)}, u32[]{:S(2)}, u32[]{:S(2)}) collective-permute-start(bf16[8,3,64,256]{3,2,1,0:T(8,128)(2,1)S(1)} %constant_dynamic-update-slice_fusion.4.rest_0_), channel_id=1, source_target_pairs={{0,2},{1,5},{2,0},{3,7},{4,6},{5,1},{6,4},{7,3},{8,10},{9,13},{10,... | collective-permute-start | bytes 2359304 | tf_op jit(solution)/shard_map/ppermute | solution.py:534
  47.5 17.3 %collective-permute-start.11 = (bf16[1,64,2048]{2,1,0:T(8,128)(2,1)S(1)}, bf16[1,64,2048]{2,1,0:T(8,128)(2,1)S(1)}, u32[]{:S(2)}, u32[]{:S(2)}) collective-permute-start(bf16[1,64,2048]{2,1,0:T(8,128)(2,1)S(1)} %maximum_bitcast_fusion), channel_id=1, source_target_pairs={{0,8},{1,17},{2,10},{3,19},{4,12},{5,21},{6,14},{7,23},{8,0},{9,25... | collective-permute-start | bytes 786440 | tf_op jit(solution)/shard_map/ppermute | solution.py:534
  49.0 15.8 %collective-permute-start.10 = (bf16[4,3,64,256]{3,2,1,0:T(8,128)(2,1)S(1)}, bf16[4,3,64,256]{3,2,1,0:T(8,128)(2,1)S(1)}, u32[]{:S(2)}, u32[]{:S(2)}) collective-permute-start(bf16[4,3,64,256]{3,2,1,0:T(8,128)(2,1)S(1)} %pad_maximum_fusion), channel_id=1, source_target_pairs={{0,4},{1,3},{2,6},{3,1},{4,0},{5,7},{6,2},{7,5},{8,12},{9,11},{10,... | collective-permute-start | bytes 1179656 | tf_op jit(solution)/shard_map/ppermute | solution.py:534
  50.5 14.3 %collective-permute-start.9 = (bf16[8,3,64,256]{3,2,1,0:T(8,128)(2,1)S(1)}, bf16[8,3,64,256]{3,2,1,0:T(8,128)(2,1)}, u32[]{:S(2)}, u32[]{:S(2)}) collective-permute-start(bf16[8,3,64,256]{3,2,1,0:T(8,128)(2,1)S(1)} %collective-permute-done.7.rest_1_), channel_id=1, source_target_pairs={{0,1},{1,0},{2,3},{3,2},{4,5},{5,4},{6,7},{7,6},{8,9},{9,8},{10,11... | collective-permute-start | bytes 2359304 | tf_op jit(solution)/shard_map/ppermute | solution.py:542
  64.9 20.1 %collective-permute-start.13 = (bf16[8,3,64,256]{3,2,1,0:T(8,128)(2,1)S(1)}, bf16[8,3,64,256]{3,2,1,0:T(8,128)(2,1)S(1)}, u32[]{:S(2)}, u32[]{:S(2)}) collective-permute-start(bf16[8,3,64,256]{3,2,1,0:T(8,128)(2,1)S(1)} %constant_dynamic-update-slice_fusion.6.rest_0_.rest_4_), channel_id=1, source_target_pairs={{0,2},{1,5},{2,0},{3,7},{4,6},{5,1},{6,4},{7,3},{8,10},{9,13},{10,... | collective-permute-start | bytes 2359304 | tf_op jit(solution)/shard_map/ppermute | solution.py:534
  65.5 19.5 %collective-permute-start.12 = (bf16[8,3,64,256]{3,2,1,0:T(8,128)(2,1)S(1)}, bf16[8,3,64,256]{3,2,1,0:T(8,128)(2,1)}, u32[]{:S(2)}, u32[]{:S(2)}) collective-permute-start(bf16[8,3,64,256]{3,2,1,0:T(8,128)(2,1)S(1)} %constant_dynamic-update-slice_fusion.6.rest_0_.rest_4_), channel_id=1, source_target_pairs={{0,1},{1,0},{2,3},{3,2},{4,5},{5,4},{6,7},{7,6},{8,9},{9,8},{10,11... | collective-permute-start | bytes 2359304 | tf_op jit(solution)/shard_map/ppermute | solution.py:542
  65.6 19.4 %collective-permute-start.14 = (bf16[2,64,2048]{2,1,0:T(8,128)(2,1)S(1)}, bf16[2,64,2048]{2,1,0:T(8,128)(2,1)S(1)}, u32[]{:S(2)}, u32[]{:S(2)}) collective-permute-start(bf16[2,64,2048]{2,1,0:T(8,128)(2,1)S(1)} %constant_dynamic-update-slice_fusion.8), channel_id=1, source_target_pairs={{0,16},{1,9},{2,18},{3,11},{4,20},{5,13},{6,22},{7,15},{8,24},{9,1... | collective-permute-start | bytes 1572872 | tf_op jit(solution)/shard_map/ppermute | solution.py:534
  85.0 16.1 %collective-permute-start.15 = (bf16[8,3,64,256]{3,2,1,0:T(8,128)(2,1)S(1)}, bf16[8,3,64,256]{3,2,1,0:T(8,128)(2,1)}, u32[]{:S(2)}, u32[]{:S(2)}) collective-permute-start(bf16[8,3,64,256]{3,2,1,0:T(8,128)(2,1)S(1)} %collective-permute-done.13.rest_1_.rest_5_), channel_id=1, source_target_pairs={{0,1},{1,0},{2,3},{3,2},{4,5},{5,4},{6,7},{7,6},{8,9},{9,8},{10,11... | collective-permute-start | bytes 2359304 | tf_op jit(solution)/shard_map/ppermute | solution.py:542
  85.8 29.2 %collective-permute-start.16 = (bf16[4,64,2048]{2,1,0:T(8,128)(2,1)S(1)}, bf16[4,64,2048]{2,1,0:T(8,128)(2,1)S(1)}, u32[]{:S(2)}, u32[]{:S(2)}) collective-permute-start(bf16[4,64,2048]{2,1,0:T(8,128)(2,1)S(1)} %constant_dynamic-update-slice_fusion.10.rest_0_), channel_id=1, source_target_pairs={{0,4},{1,3},{2,6},{3,1},{4,0},{5,7},{6,2},{7,5},{8,12},{9,11},{10,... | collective-permute-start | bytes 3145736 | tf_op jit(solution)/shard_map/ppermute | solution.py:534
  115.0 42.6 %copy-start.5 = (bf16[4,64,2048]{2,1,0:T(8,128)(2,1)}, bf16[4,64,2048]{2,1,0:T(8,128)(2,1)S(1)}, u32[]{:S(2)}) copy-start(bf16[4,64,2048]{2,1,0:T(8,128)(2,1)S(1)} %collective-permute-done.16.rest_1_) | copy-start | bytes 3145732
  115.0 42.6 %collective-permute-start.19 = (bf16[4,64,2048]{2,1,0:T(8,128)(2,1)S(1)}, bf16[4,64,2048]{2,1,0:T(8,128)(2,1)}, u32[]{:S(2)}, u32[]{:S(2)}) collective-permute-start(bf16[4,64,2048]{2,1,0:T(8,128)(2,1)S(1)} %constant_dynamic-update-slice_fusion.10.rest_0_), channel_id=1, source_target_pairs={{0,2},{1,5},{2,0},{3,7},{4,6},{5,1},{6,4},{7,3},{8,10},{9,13},{10,... | collective-permute-start | bytes 3145736 | tf_op jit(solution)/shard_map/ppermute | solution.py:534
  115.9 41.8 %collective-permute-start.17 = (bf16[4,64,2048]{2,1,0:T(8,128)(2,1)S(1)}, bf16[4,64,2048]{2,1,0:T(8,128)(2,1)}, u32[]{:S(2)}, u32[]{:S(2)}) collective-permute-start(bf16[4,64,2048]{2,1,0:T(8,128)(2,1)S(1)} %constant_dynamic-update-slice_fusion.10.rest_0_), channel_id=1, source_target_pairs={{0,1},{1,0},{2,3},{3,2},{4,5},{5,4},{6,7},{7,6},{8,9},{9,8},{10,11... | collective-permute-start | bytes 3145736 | tf_op jit(solution)/shard_map/ppermute | solution.py:542
  115.9 41.8 %collective-permute-start.20 = (bf16[4,64,2048]{2,1,0:T(8,128)(2,1)S(1)}, bf16[4,64,2048]{2,1,0:T(8,128)(2,1)}, u32[]{:S(2)}, u32[]{:S(2)}) collective-permute-start(bf16[4,64,2048]{2,1,0:T(8,128)(2,1)S(1)} %collective-permute-done.16.rest_1_), channel_id=1, source_target_pairs={{0,2},{1,5},{2,0},{3,7},{4,6},{5,1},{6,4},{7,3},{8,10},{9,13},{10,... | collective-permute-start | bytes 3145736 | tf_op jit(solution)/shard_map/ppermute | solution.py:534
  117.1 40.6 %collective-permute-start.18 = (bf16[4,64,2048]{2,1,0:T(8,128)(2,1)S(1)}, bf16[4,64,2048]{2,1,0:T(8,128)(2,1)}, u32[]{:S(2)}, u32[]{:S(2)}) collective-permute-start(bf16[4,64,2048]{2,1,0:T(8,128)(2,1)S(1)} %collective-permute-done.16.rest_1_), channel_id=1, source_target_pairs={{0,1},{1,0},{2,3},{3,2},{4,5},{5,4},{6,7},{7,6},{8,9},{9,8},{10,11... | collective-permute-start | bytes 3145736 | tf_op jit(solution)/shard_map/ppermute | solution.py:542
  157.7 2.9 collective-permute-start.21
  158.0 4.1 %collective-permute-start.22 = (bf16[4,64,2048]{2,1,0:T(8,128)(2,1)}, bf16[4,64,2048]{2,1,0:T(8,128)(2,1)S(1)}, u32[]{:S(2)}, u32[]{:S(2)}) collective-permute-start(bf16[4,64,2048]{2,1,0:T(8,128)(2,1)} %collective-permute-done.20.rest_3_), channel_id=1, source_target_pairs={{0,1},{1,0},{2,3},{3,2},{4,5},{5,4},{6,7},{7,6},{8,9},{9,8},{10,11... | collective-permute-start | bytes 3145736 | tf_op jit(solution)/shard_map/ppermute | solution.py:542
  247.5 87.2 %copy-start.1 = (s32[8,512]{1,0:T(8,128)S(1)}, s32[8,512]{1,0:T(8,128)}, u32[]{:S(2)}) copy-start(s32[8,512]{1,0:T(8,128)} %param.17) | copy-start | bytes 49156
  314.5 1.2 collective-permute-start.23
  315.8 3.7 %collective-permute-start.24 = (f32[2,1024]{1,0:T(2,128)S(1)}, f32[2,1024]{1,0:T(2,128)S(1)}, u32[]{:S(2)}, u32[]{:S(2)}) collective-permute-start(f32[2,1024]{1,0:T(2,128)S(1)} %add.88), channel_id=1, source_target_pairs={{0,2},{2,0},{4,6},{6,4},{8,10},{10,8},{12,14},{14,12},{16,18},{18,... | collective-permute-start | bytes 24584 | tf_op jit(solution)/shard_map/ppermute | solution.py:567
  319.4 3.7 %collective-permute-start.25 = (f32[2,1024]{1,0:T(2,128)S(1)}, f32[2,1024]{1,0:T(2,128)S(1)}, u32[]{:S(2)}, u32[]{:S(2)}) collective-permute-start(f32[2,1024]{1,0:T(2,128)S(1)} %add.89), channel_id=1, source_target_pairs={{0,4},{2,6},{4,0},{6,2},{8,12},{10,14},{12,8},{14,10},{16,20},{18,... | collective-permute-start | bytes 24584 | tf_op jit(solution)/shard_map/ppermute | solution.py:567
  323.1 3.7 %collective-permute-start.26 = (f32[2,1024]{1,0:T(2,128)S(1)}, f32[2,1024]{1,0:T(2,128)S(1)}, u32[]{:S(2)}, u32[]{:S(2)}) collective-permute-start(f32[2,1024]{1,0:T(2,128)S(1)} %add.90), channel_id=1, source_target_pairs={{0,8},{2,10},{4,12},{6,14},{8,0},{10,2},{12,4},{14,6},{16,24},{18,... | collective-permute-start | bytes 24584 | tf_op jit(solution)/shard_map/ppermute | solution.py:567
  326.8 4.5 %collective-permute-start.27 = (f32[2,1024]{1,0:T(2,128)S(1)}, f32[2,1024]{1,0:T(2,128)S(1)}, u32[]{:S(2)}, u32[]{:S(2)}) collective-permute-start(f32[2,1024]{1,0:T(2,128)S(1)} %add.91), channel_id=1, source_target_pairs={{0,16},{2,18},{4,20},{6,22},{8,24},{10,26},{12,28},{14,30},{16,0},... | collective-permute-start | bytes 24584 | tf_op jit(solution)/shard_map/ppermute | solution.py:567
  (11 other events, 180.7 us)
Sparse Core Ops, SparseCore 0:
  24.6 98.5 all-gather.4
  247.6 52.9 all-gather.6

commit v5 on v4

--- a/solution.py
+++ b/solution.py
@@ -191,7 +191,8 @@
         if arriving:
             wait_all(fetch_sets(rest[:count], w_ref, sem, start=False))
         ones = jnp.ones((16, SLOTS), jnp.bfloat16)
-        columns = pl.ds(pl.multiple_of(group * WIDE, WIDE), WIDE)
+        place = (slot_ref[2, 0] ^ (group % 2)) * 2 + group // 2
+        columns = pl.ds(pl.multiple_of(place * WIDE, WIDE), WIDE)
         total = acc_ref[...]
         for i, grad in enumerate((d_q, d_k, d_v)):
             grad = jnp.concatenate(grad, 0)
@@ -237,6 +238,9 @@
     if late:
         return columns_of(late_ref, slot_ref, other, pl.ds(down * LATE + start, size))
     return first_columns(first_ref, slot_ref, other, pl.ds(down * FIRST + start, size))
+
+
+assert FIRST == LATE == LATE_PIECE == D
 
 
 def piece_bias(b_refs, piece):
@@ -283,13 +287,12 @@
 def back_kernel(
     count, slot_ref, normal_ref, inv_ref, branch_ref, slope_ref, ct_ref, ctx_ref, vec_refs, bi_refs, first_ref, *rest
 ):
-    out_ref, dctx_ref, delta_ref, sum_ref, vecg_ref, big_ref, keep_ref, acc_ref, low_ref, late_ref, late_sem = rest[-11:]
+    out_ref, dctx_ref, delta_ref, sum_ref, sums_ref, keep_ref, acc_ref, low_ref, late_ref, late_sem = rest[-10:]
 
 
     @pl.when(pl.program_id(0) == 0)
     def _():
-        vecg_ref[...] = jnp.zeros_like(vecg_ref)
-        big_ref[...] = jnp.zeros_like(big_ref)
+        sums_ref[...] = jnp.zeros_like(sums_ref)
         wait_all(fetch_sets(rest[:count], late_ref, late_sem))
 
     gain_one, bias_one, gain_two, bias_two = [row_of(ref) for ref in vec_refs]
@@ -327,7 +330,9 @@
         flat = flat_of(piece)
         slope = keep_ref[:, flat.start - 2 * FIRST : flat.stop - 2 * FIRST] if piece[0] else slope_ref[:, flat]
         inner_grad = low(mul(branch_grad, weight(piece, 1)) * wide(slope))
-        big_ref[0:1, flat] += jnp.sum(wide(inner_grad), 0, keepdims=True)
+        late, other = piece[:2]
+        place = pl.ds(4 + 2 * (slot_ref[2, 0] ^ other) + int(late), 1)
+        sums_ref[place, :] += jnp.sum(wide(inner_grad), 0, keepdims=True)
         normed_grad = normed_grad + mul(inner_grad, weight(piece, 0), NT)
     acc_ref[...] = normed_grad
     for rows in strips:
@@ -346,7 +351,7 @@
             own = slice(head * HEAD_DIM, (head + 1) * HEAD_DIM)
             delta_ref[0, group, head : head + 1, :] = jnp.sum(product[own], 0, keepdims=True)
     for i, term in enumerate(sums):
-        vecg_ref[i : i + 1, :] += jnp.sum(term, 0, keepdims=True)
+        sums_ref[i : i + 1, :] += jnp.sum(term, 0, keepdims=True)
 
 
 def params(grid_rank):
@@ -437,11 +442,11 @@
         + [pl.BlockSpec((SLOTS, D), lambda r, g: (r, 0))],
         out_specs=[
             pl.BlockSpec((SLOTS, D), lambda r, g: (r, 0)),
-            pl.BlockSpec((8, D), lambda r, g: (0, 0)),
+            pl.BlockSpec((2, D), lambda r, g: (0, 0)),
         ],
         out_shape=[
             jax.ShapeDtypeStruct((rows * SLOTS, D), jnp.bfloat16),
-            jax.ShapeDtypeStruct((8, D), jnp.float32),
+            jax.ShapeDtypeStruct((2, D), jnp.float32),
         ],
         scratch_shapes=[
             pltpu.VMEM((SLOTS, SLOTS), jnp.float32),
@@ -495,7 +500,6 @@
             pl.BlockSpec((1, GROUPS, GROUP, TILE), lambda i: (i // PER_ROW, 0, 0, i % PER_ROW)),
             tiles(D),
             pl.BlockSpec((8, D), lambda i: (0, 0)),
-            pl.BlockSpec((8, FF), lambda i: (0, 0)),
         ],
         out_shape=[
             jax.ShapeDtypeStruct((count, D), jnp.bfloat16),
@@ -503,7 +507,6 @@
             jax.ShapeDtypeStruct((count // SLOTS, GROUPS, GROUP, SLOTS), jnp.float32),
             jax.ShapeDtypeStruct((count, D), jnp.bfloat16),
             jax.ShapeDtypeStruct((8, D), jnp.float32),
-            jax.ShapeDtypeStruct((8, FF), jnp.float32),
         ],
         scratch_shapes=[
             pltpu.VMEM((TILE, 2 * LATE), jnp.bfloat16),
@@ -560,13 +563,17 @@
     return jnp.concatenate([ordered, jnp.full((1, n), core, jnp.int32)], 0)
 
 
-def sum_over_all(values, n):
-    values = values + swap_cores(values)
-    step = 1
-    while step < n:
-        values = values + lax.ppermute(values, "rows", [(i, i ^ step) for i in range(n)])
-        step *= 2
-    return values
+def sum_over_rows(values, n, beside):
+    bits = n.bit_length() - 1
+
+    def got(distance):
+        return lax.ppermute(values, "rows", [(i, i ^ distance) for i in range(n)])
+
+    for bit in range(0, bits - 1, 2):
+        near, far, both = [got(j << bit) for j in (1, 2, 3)]
+        near, far, both, beside = together(near, far, both, beside)
+        values = (values + near) + (far + both)
+    return values + got(1 << (bits - 1)) if bits % 2 else values, beside
 
 
 def shards(
@@ -647,15 +654,15 @@
     b_got = partner(b, n, last)
     results = run(1, results, a_other, a_other_got)
 
-    results, b_other, b_got, late, late_got = together(results, b_other, b_got, late, late_got)
+    results, b_other, b_got = together(results, b_other, b_got)
     b_other_got = swap_cores(b_got)
+    results = run(2, results, b, b_got)
+
+    results, b_other_got, late, late_got = together(results, b_other_got, late, late_got)
     late = joined(late, late_got)
     for stage in range(2, last):
         late_got = partner(late, n, stage)
         late = late if stage == last - 1 else joined(late, late_got)
-    results = run(2, results, b, b_got)
-
-    results, b_other_got = together(results, b_other_got)
     results = run(3, results, b_other, b_other_got)
 
     results, late, late_got = together(results, late, late_got)
@@ -669,25 +676,18 @@
     front, late_others, late_far = together(front, late_others, late_far)
     late_others += [swap_cores(w) for w in late_far]
     vectors = (norm1_gain, norm1_bias, norm2_gain, norm2_bias)
-    layer_out, context_grad, delta, sum_one, vec_grads, in_grads = feed_back(
+    layer_out, context_grad, delta, sum_one, grads = feed_back(
         slots, front, cotangent, context, first, late_own + late_far + late_others, vectors, b_in
     )
-    hidden = [in_grads[0, : 2 * FIRST].reshape(2, FIRST), in_grads[0, 2 * FIRST :].reshape(2, LATE)]
-    hidden = jnp.concatenate(hidden, 1)
-    hidden = jnp.where(core == 0, hidden, hidden[::-1])
-    early = jnp.concatenate([vec_grads[:4].reshape(-1), hidden.reshape(-1)])
-    early = jnp.sum(lax.all_gather(early, ("rows", "tp"), axis=0), 0)
-    vec = early[: 4 * D].reshape(4, D)
-
+    sums = jnp.sum(lax.all_gather(grads, ("rows", "tp"), axis=0), 0)
+    sums = [sums[0], sums[1], sums[4:].reshape(-1), sums[2], sums[3]]
     a_set = [a, a_got, a_other, a_other_got]
     b_set = [b, b_got, b_other, b_other_got]
     tokens_grad, qv_grads = attend_back(
         qk, kv, context_grad, delta, lse, *small, a_set + b_set, sum_one
     )
-    qv = qv_grads[:2].reshape(2, 2, 2, WIDE)
-    qv = jnp.where(core == 0, qv, qv[:, :, ::-1]).transpose(0, 2, 1, 3).reshape(2, D)
-    qv = sum_over_all(qv, n)
-    return (layer_out, tokens_grad, qv, vec[0], vec[1], early[4 * D :], vec[2], vec[3])
+    qv, sums = sum_over_rows(qv_grads + swap_cores(qv_grads), n, sums)
+    return (layer_out, tokens_grad, qv, *sums)
 
 
 def solution(mesh):

time: 342 us -> 332 us (0.971)
  waiting for transfers between devices: 39 us -> 28.7 us
    ppermute x4 -> x6, waiting for transfers between devices: 8.94 us -> 2.09 us  [got(): return lax.ppermute(values, 'rows', [(i, i ^ distance) for i in range(n)])]
    ppermute x4 -> x6, starting transfers between devices: 6.56 us -> 7.94 us  [got(): return lax.ppermute(values, 'rows', [(i, i ^ distance) for i in range(n)])]
  transfers between devices with their start and end apart: 30 -> 32, of which waited for: 13 -> 10; matrix products, arithmetic and copies ran while one was open for 2% -> 3% of each run, Pallas kernels for 46% -> 47%
where the time goes in v5:
time: 332 us; the launch traced here: 331 us
  Pallas kernels  239 us (72%)
  starting transfers between devices  34.8 us (10%)
  waiting for transfers between devices  28.7 us (9%)
  between operations  14.5 us (4%)
  local copies, waits for them, and re-layouts  10.1 us (3%)
  other arithmetic  4.3 us (1%)
    pallas_call x1, Pallas kernels, feed_back(): pl.pallas_call(partial(back_kernel, len(late)), grid=(count // TILE,), in...  82.5 us
    pallas_call x1, Pallas kernels, attend_back(): pl.pallas_call(partial(attend_back_kernel, len(weights)), grid=(rows, GRO...  66.4 us
    pallas_call x4, Pallas kernels, attend(): pl.pallas_call(partial(attend_kernel, step, len(pieces)), grid=(rows,), i...  55.3 us
    pallas_call x1, Pallas kernels, feed_front(): pl.pallas_call(front_kernel, grid=(count // TILE,), in_specs=[SCALARS, ti...  34.5 us
    ppermute x13, starting transfers between devices, partner(): return lax.ppermute(block, ('rows', 'tp'), pairs)  24.7 us
    ppermute x13, waiting for transfers between devices, partner(): return lax.ppermute(block, ('rows', 'tp'), pairs)  16.8 us
    ppermute x6, starting transfers between devices, got(): return lax.ppermute(values, 'rows', [(i, i ^ distance) for i in range(n)])  7.94 us
  transfers between devices with their start and end apart: 32, of which 10 were waited for; matrix products, arithmetic and copies ran while one was open for 3% of the time, Pallas kernels for 47%

profile of v5, /device:TPU:0, one launch (start us, length us, event | category | flops | bytes accessed | tf_op | source)
XLA Modules:
  0.0 331.1 jit_solution(17703548106522045228)
XLA Ops:
  8.2 3.1 collective-permute-start
  12.4 2.5 collective-permute-done
  15.0 2.0 collective-permute-start.2
  16.9 2.6 collective-permute-start.1
  19.5 1.6 pad_maximum_fusion.1
  21.1 3.4 %collective-permute-done.1 = bf16[2,3,64,256]{3,2,1,0:T(8,128)(2,1)S(1)} collective-permute-done((bf16[2,3,64,256]{3,2,1,0:T(8,128)(2,1)S(1)}, bf16[2,3,64,256]{3,2,1,0:T(8,128)(2,1)S(1)}, u32[]{:S(2)}, u32[]{:S(2)}) %collective-permute-start.1) | collective-permute-done | bytes 196640 | tf_op jit(solution)/shard_map/ppermute | solution.py:537
  25.2 1.6 collective-permute-start.3
  26.8 2.9 collective-permute-start.4
  29.8 1.2 dynamic_slice.7.fill_ref
  32.2 2.0 collective-permute-done.4
  34.4 2.8 collective-permute-start.7
  37.3 1.4 copy.39.segc_ref
  38.7 8.8 %collective-permute-done.7.rest_1_ = bf16[8,3,64,256]{3,2,1,0:T(8,128)(2,1)S(1)} collective-permute-done((bf16[8,3,64,256]{3,2,1,0:T(8,128)(2,1)S(1)}, bf16[8,3,64,256]{3,2,1,0:T(8,128)(2,1)S(1)}, u32[]{:S(2)}, u32[]{:S(2)}) %collective-permute-start.7) | collective-permute-done | bytes 786464 | tf_op jit(solution)/shard_map/ppermute | solution.py:537
  47.5 1.5 collective-permute-start.11
  49.0 1.5 collective-permute-start.10
  50.8 13.9 %attend.4 = (bf16[2,4,1024,512]{3,2,1,0:T(8,128)(2,1)}, bf16[2,2048,1024]{2,1,0:T(8,128)(2,1)}, bf16[4,1024,512]{2,1,0:T(8,128)(2,1)}, f32[4,4,4,512]{3,2,1,0:T(4,128)}) custom-call(s32[4]{0:T(128)} %dynamic_slice.7.fill_ref, s32[3,16]{1,0:T(4,128)} %concatenate.33.slot_ref, bf16[2048,1024]{1,0:T(8,128)(2,1)} %x_ref.9, s32[4,512,1]{2,1,0:T(8,128)} %copy.39.segc_ref, ...), custom_call_target="tpu_custom_call" | custom-call | flops 15000000512 | bytes 10000000 | tf_op jit(solution)/shard_map/attend/pallas_call | solution.py:390
  65.6 2.3 collective-permute-start.15
  67.9 13.8 %attend.5 = (bf16[2,4,1024,512]{3,2,1,0:T(8,128)(2,1)}, bf16[2,2048,1024]{2,1,0:T(8,128)(2,1)}, bf16[4,1024,512]{2,1,0:T(8,128)(2,1)}, f32[4,4,4,512]{3,2,1,0:T(4,128)}) custom-call(s32[4]{0:T(128)} %dynamic_slice.7.fill_ref, s32[3,16]{1,0:T(4,128)} %concatenate.33.slot_ref, ...), custom_call_target="tpu_custom_call", output_to_operand_aliasing={{0}: (8, {}), {1}: (9, {}), {2}: (10, {}), {3}: (11, {})} | custom-call | flops 15000000512 | bytes 10000000 | tf_op jit(solution)/shard_map/attend/pallas_call | solution.py:390
  82.7 13.8 %attend.6 = (bf16[2,4,1024,512]{3,2,1,0:T(8,128)(2,1)}, bf16[2,2048,1024]{2,1,0:T(8,128)(2,1)}, bf16[4,1024,512]{2,1,0:T(8,128)(2,1)}, f32[4,4,4,512]{3,2,1,0:T(4,128)}) custom-call(s32[4]{0:T(128)} %dynamic_slice.7.fill_ref, s32[3,16]{1,0:T(4,128)} %concatenate.33.slot_ref, ...), custom_call_target="tpu_custom_call", output_to_operand_aliasing={{0}: (8, {}), {1}: (9, {}), {2}: (10, {}), {3}: (11, {})} | custom-call | flops 15000000512 | bytes 10000000 | tf_op jit(solution)/shard_map/attend/pallas_call | solution.py:390
  97.5 1.7 collective-permute-start.16
  99.2 13.8 %attend.7 = (bf16[2,4,1024,512]{3,2,1,0:T(8,128)(2,1)}, bf16[2,2048,1024]{2,1,0:T(8,128)(2,1)}, bf16[4,1024,512]{2,1,0:T(8,128)(2,1)}, f32[4,4,4,512]{3,2,1,0:T(4,128)}) custom-call(s32[4]{0:T(128)} %dynamic_slice.7.fill_ref, s32[3,16]{1,0:T(4,128)} %concatenate.33.slot_ref, ...), custom_call_target="tpu_custom_call", output_to_operand_aliasing={{0}: (8, {}), {1}: (9, {}), {2}: (10, {}), {3}: (11, {})} | custom-call | flops 15000000512 | bytes 10000000 | tf_op jit(solution)/shard_map/attend/pallas_call | solution.py:390
  113.0 1.3 collective-permute-start.19
  115.2 4.7 %all-gather.5.cloned.1.call-done = bf16[2048,2560]{1,0:T(8,128)(2,1)} async-done(((bf16[64,2560]{1,0:T(8,128)(2,1)}), bf16[2048,2560]{1,0:T(8,128)(2,1)}) %all-gather.5.cloned.1.call-update) | async-done | bytes 10485776 | tf_op jit(solution)/shard_map/all_gather | solution.py:617
  120.0 34.5 %feed_front.1 = (f32[2048,1024]{1,0:T(8,128)}, f32[2048,128]{1,0:T(8,128)}, f32[2048,1024]{1,0:T(8,128)}, bf16[2048,2048]{1,0:T(8,128)(2,1)}) custom-call(s32[3,16]{1,0:T(4,128)} %concatenate.33.slot_ref, bf16[2048,1024]{1,0:T(8,128)(2,1)} %x_ref.9, bf16[4,1024,512]{2,1,0:T(8,128)(2,1)} %get-tuple-element.172.ctx_ref, bf16[1024]{0:T(1024)(128)(2,1)} %vec_refs_0_.2, ...), custom_call_target="tpu_custom_call" | custom-call | flops 24999999488 | bytes 30000000 | tf_op jit(solution)/shard_map/feed_front/pallas_call | solution.py:472
  155.1 2.4 collective-permute-done.21.rest_6_
  157.4 1.5 collective-permute-done.22.rest_7_
  159.9 82.5 %feed_back.1 = (bf16[2048,1024]{1,0:T(8,128)(2,1)}, bf16[4,1024,512]{2,1,0:T(8,128)(2,1)}, f32[4,4,4,512]{3,2,1,0:T(4,128)}, bf16[2048,1024]{1,0:T(8,128)(2,1)}, f32[8,1024]{1,0:T(8,128)}) custom-call(s32[3,16]{1,0:T(4,128)} %concatenate.33.slot_ref, f32[2048,1024]{1,0:T(8,128)} %get-tuple-element.182.normal_ref, f32[2048,128]{1,0:T(8,128)} %get-tuple-element.183.inv_ref, ...), custom_call_target="tpu_custom_call" | custom-call | flops 74999996416 | bytes 40000000 | tf_op jit(solution)/shard_map/feed_back/pallas_call | solution.py:492
  242.5 66.4 %attend_back.1 = (bf16[2048,1024]{1,0:T(8,128)(2,1)}, f32[2,1024]{1,0:T(2,128)}) custom-call(s32[4]{0:T(128)} %dynamic_slice.7.fill_ref, s32[3,16]{1,0:T(4,128)} %concatenate.33.slot_ref, bf16[2,4,1024,512]{3,2,1,0:T(8,128)(2,1)} %get-tuple-element.191.qk_ref, bf16[2,2048,1024]{2,1,0:T(8,128)(2,1)} %get-tuple-element.192.kv_ref, ...), custom_call_target="tpu_custom_call" | custom-call | flops 49999998976 | bytes 30000000 | tf_op jit(solution)/shard_map/attend_back/pallas_call | solution.py:427
  313.1 1.4 collective-permute-start.24
  314.5 1.3 bitcast_reduce_fusion
  317.1 2.0 collective-permute-start.29
  319.1 2.5 collective-permute-start.27
  (102 shorter events, 17.9 us)
Async XLA Ops:
  7.2 112.8 %all-gather.5.cloned.1.call-start = ((), (), s32[]{:S(2)}) async-start(), calls=%async_computation | async-start | bytes 10813440 | tf_op jit(solution)/shard_map/all_gather | solution.py:617
  8.2 6.7 %collective-permute-start = (bf16[1,3,64,256]{3,2,1,0:T(8,128)(2,1)S(1)}, bf16[1,3,64,256]{3,2,1,0:T(8,128)(2,1)S(1)}, u32[]{:S(2)}, u32[]{:S(2)}) collective-permute-start(bf16[1,3,64,256]{3,2,1,0:T(8,128)(2,1)S(1)} %get-tuple-element.221), channel_id=1, source_target_pairs={{0,8},{1,17},{2,10},{3,19},{4,12},{5,21},{6,14},{7,23},{8,0},{9,25... | collective-permute-start | bytes 294920 | tf_op jit(solution)/shard_map/ppermute | solution.py:537
  15.0 6.1 %collective-permute-start.2 = (bf16[1,3,64,256]{3,2,1,0:T(8,128)(2,1)S(1)}, bf16[1,3,64,256]{3,2,1,0:T(8,128)(2,1)S(1)}, u32[]{:S(2)}, u32[]{:S(2)}) collective-permute-start(bf16[1,3,64,256]{3,2,1,0:T(8,128)(2,1)S(1)} %get-tuple-element.116), channel_id=1, source_target_pairs={{0,8},{1,17},{2,10},{3,19},{4,12},{5,21},{6,14},{7,23},{8,0},{9,25... | collective-permute-start | bytes 294920 | tf_op jit(solution)/shard_map/ppermute | solution.py:537
  16.9 7.5 %collective-permute-start.1 = (bf16[2,3,64,256]{3,2,1,0:T(8,128)(2,1)S(1)}, bf16[2,3,64,256]{3,2,1,0:T(8,128)(2,1)S(1)}, u32[]{:S(2)}, u32[]{:S(2)}) collective-permute-start(bf16[2,3,64,256]{3,2,1,0:T(8,128)(2,1)S(1)} %pad_maximum_fusion.2), channel_id=1, source_target_pairs={{0,16},{1,9},{2,18},{3,11},{4,20},{5,13},{6,22},{7,15},{8,24},{9,1... | collective-permute-start | bytes 589832 | tf_op jit(solution)/shard_map/ppermute | solution.py:537
  24.5 290.0 %all-gather.7.cloned.1.call-start = ((), (), s32[]{:S(2)}) async-start(), calls=%async_computation.1 | async-start | bytes 1081344 | tf_op jit(solution)/shard_map/all_gather | solution.py:682
  24.5 7.7 %collective-permute-start.5 = (bf16[2,512]{1,0:T(2,128)(2,1)}, bf16[2,512]{1,0:T(2,128)(2,1)S(1)}, u32[]{:S(2)}, u32[]{:S(2)}) collective-permute-start(bf16[2,512]{1,0:T(2,128)(2,1)} %b_ref.1), channel_id=1, source_target_pairs={{0,1},{1,0},{2,3},{3,2},{4,5},{5,4},{6,7},{7,6},{8,9},{9,8},{10,11... | collective-permute-start | bytes 6152 | tf_op jit(solution)/shard_map/ppermute | solution.py:545
  24.7 7.5 %collective-permute-start.6 = (bf16[2048]{0:T(1024)(128)(2,1)}, bf16[2048]{0:T(1024)(128)(2,1)S(1)}, u32[]{:S(2)}, u32[]{:S(2)}) collective-permute-start(bf16[2048]{0:T(1024)(128)(2,1)} %bi_refs_0_.1), channel_id=1, source_target_pairs={{0,1},{1,0},{2,3},{3,2},{4,5},{5,4},{6,7},{7,6},{8,9},{9,8},{10,11... | collective-permute-start | bytes 12296 | tf_op jit(solution)/shard_map/ppermute | solution.py:545
  25.2 9.1 %collective-permute-start.3 = (bf16[4,3,64,256]{3,2,1,0:T(8,128)(2,1)S(1)}, bf16[4,3,64,256]{3,2,1,0:T(8,128)(2,1)S(1)}, u32[]{:S(2)}, u32[]{:S(2)}) collective-permute-start(bf16[4,3,64,256]{3,2,1,0:T(8,128)(2,1)S(1)} %constant_dynamic-update-slice_fusion), channel_id=1, source_target_pairs={{0,4},{1,3},{2,6},{3,1},{4,0},{5,7},{6,2},{7,5},{8,12},{9,11},{10,... | collective-permute-start | bytes 1179656 | tf_op jit(solution)/shard_map/ppermute | solution.py:537
  26.8 7.5 %collective-permute-start.4 = (bf16[2,3,64,256]{3,2,1,0:T(8,128)(2,1)S(1)}, bf16[2,3,64,256]{3,2,1,0:T(8,128)(2,1)S(1)}, u32[]{:S(2)}, u32[]{:S(2)}) collective-permute-start(bf16[2,3,64,256]{3,2,1,0:T(8,128)(2,1)S(1)} %constant_dynamic-update-slice_fusion.2), channel_id=1, source_target_pairs={{0,16},{1,9},{2,18},{3,11},{4,20},{5,13},{6,22},{7,15},{8,24},{9,1... | collective-permute-start | bytes 589832 | tf_op jit(solution)/shard_map/ppermute | solution.py:537
  34.3 4.3 %collective-permute-start.8 = (bf16[8,3,64,256]{3,2,1,0:T(8,128)(2,1)S(1)}, bf16[8,3,64,256]{3,2,1,0:T(8,128)(2,1)S(1)}, u32[]{:S(2)}, u32[]{:S(2)}) collective-permute-start(bf16[8,3,64,256]{3,2,1,0:T(8,128)(2,1)S(1)} %constant_dynamic-update-slice_fusion.4.rest_0_), channel_id=1, source_target_pairs={{0,1},{1,0},{2,3},{3,2},{4,5},{5,4},{6,7},{7,6},{8,9},{9,8},{10,11... | collective-permute-start | bytes 2359304 | tf_op jit(solution)/shard_map/ppermute | solution.py:545
  34.4 13.1 %collective-permute-start.7 = (bf16[8,3,64,256]{3,2,1,0:T(8,128)(2,1)S(1)}, bf16[8,3,64,256]{3,2,1,0:T(8,128)(2,1)S(1)}, u32[]{:S(2)}, u32[]{:S(2)}) collective-permute-start(bf16[8,3,64,256]{3,2,1,0:T(8,128)(2,1)S(1)} %constant_dynamic-update-slice_fusion.4.rest_0_), channel_id=1, source_target_pairs={{0,2},{1,5},{2,0},{3,7},{4,6},{5,1},{6,4},{7,3},{8,10},{9,13},{10,... | collective-permute-start | bytes 2359304 | tf_op jit(solution)/shard_map/ppermute | solution.py:537
  47.5 17.3 %collective-permute-start.11 = (bf16[1,64,2048]{2,1,0:T(8,128)(2,1)S(1)}, bf16[1,64,2048]{2,1,0:T(8,128)(2,1)S(1)}, u32[]{:S(2)}, u32[]{:S(2)}) collective-permute-start(bf16[1,64,2048]{2,1,0:T(8,128)(2,1)S(1)} %maximum_bitcast_fusion), channel_id=1, source_target_pairs={{0,8},{1,17},{2,10},{3,19},{4,12},{5,21},{6,14},{7,23},{8,0},{9,25... | collective-permute-start | bytes 786440 | tf_op jit(solution)/shard_map/ppermute | solution.py:537
  49.0 15.8 %collective-permute-start.10 = (bf16[4,3,64,256]{3,2,1,0:T(8,128)(2,1)S(1)}, bf16[4,3,64,256]{3,2,1,0:T(8,128)(2,1)S(1)}, u32[]{:S(2)}, u32[]{:S(2)}) collective-permute-start(bf16[4,3,64,256]{3,2,1,0:T(8,128)(2,1)S(1)} %pad_maximum_fusion), channel_id=1, source_target_pairs={{0,4},{1,3},{2,6},{3,1},{4,0},{5,7},{6,2},{7,5},{8,12},{9,11},{10,... | collective-permute-start | bytes 1179656 | tf_op jit(solution)/shard_map/ppermute | solution.py:537
  50.5 14.3 %collective-permute-start.9 = (bf16[8,3,64,256]{3,2,1,0:T(8,128)(2,1)S(1)}, bf16[8,3,64,256]{3,2,1,0:T(8,128)(2,1)}, u32[]{:S(2)}, u32[]{:S(2)}) collective-permute-start(bf16[8,3,64,256]{3,2,1,0:T(8,128)(2,1)S(1)} %collective-permute-done.7.rest_1_), channel_id=1, source_target_pairs={{0,1},{1,0},{2,3},{3,2},{4,5},{5,4},{6,7},{7,6},{8,9},{9,8},{10,11... | collective-permute-start | bytes 2359304 | tf_op jit(solution)/shard_map/ppermute | solution.py:545
  64.9 16.9 %collective-permute-start.13 = (bf16[8,3,64,256]{3,2,1,0:T(8,128)(2,1)S(1)}, bf16[8,3,64,256]{3,2,1,0:T(8,128)(2,1)S(1)}, u32[]{:S(2)}, u32[]{:S(2)}) collective-permute-start(bf16[8,3,64,256]{3,2,1,0:T(8,128)(2,1)S(1)} %constant_dynamic-update-slice_fusion.6.rest_0_.rest_4_), channel_id=1, source_target_pairs={{0,2},{1,5},{2,0},{3,7},{4,6},{5,1},{6,4},{7,3},{8,10},{9,13},{10,... | collective-permute-start | bytes 2359304 | tf_op jit(solution)/shard_map/ppermute | solution.py:537
  65.6 16.2 %collective-permute-start.12 = (bf16[8,3,64,256]{3,2,1,0:T(8,128)(2,1)S(1)}, bf16[8,3,64,256]{3,2,1,0:T(8,128)(2,1)}, u32[]{:S(2)}, u32[]{:S(2)}) collective-permute-start(bf16[8,3,64,256]{3,2,1,0:T(8,128)(2,1)S(1)} %constant_dynamic-update-slice_fusion.6.rest_0_.rest_4_), channel_id=1, source_target_pairs={{0,1},{1,0},{2,3},{3,2},{4,5},{5,4},{6,7},{7,6},{8,9},{9,8},{10,11... | collective-permute-start | bytes 2359304 | tf_op jit(solution)/shard_map/ppermute | solution.py:545
  65.6 30.9 %collective-permute-start.15 = (bf16[2,64,2048]{2,1,0:T(8,128)(2,1)S(1)}, bf16[2,64,2048]{2,1,0:T(8,128)(2,1)S(1)}, u32[]{:S(2)}, u32[]{:S(2)}) collective-permute-start(bf16[2,64,2048]{2,1,0:T(8,128)(2,1)S(1)} %constant_dynamic-update-slice_fusion.8), channel_id=1, source_target_pairs={{0,16},{1,9},{2,18},{3,11},{4,20},{5,13},{6,22},{7,15},{8,24},{9,1... | collective-permute-start | bytes 1572872 | tf_op jit(solution)/shard_map/ppermute | solution.py:537
  81.8 14.7 %collective-permute-start.14 = (bf16[8,3,64,256]{3,2,1,0:T(8,128)(2,1)S(1)}, bf16[8,3,64,256]{3,2,1,0:T(8,128)(2,1)S(1)}, u32[]{:S(2)}, u32[]{:S(2)}) collective-permute-start(bf16[8,3,64,256]{3,2,1,0:T(8,128)(2,1)S(1)} %collective-permute-done.13.rest_1_.rest_5_), channel_id=1, source_target_pairs={{0,1},{1,0},{2,3},{3,2},{4,5},{5,4},{6,7},{7,6},{8,9},{9,8},{10,11... | collective-permute-start | bytes 2359304 | tf_op jit(solution)/shard_map/ppermute | solution.py:545
  97.5 15.5 %collective-permute-start.16 = (bf16[4,64,2048]{2,1,0:T(8,128)(2,1)S(1)}, bf16[4,64,2048]{2,1,0:T(8,128)(2,1)S(1)}, u32[]{:S(2)}, u32[]{:S(2)}) collective-permute-start(bf16[4,64,2048]{2,1,0:T(8,128)(2,1)S(1)} %constant_dynamic-update-slice_fusion.10.rest_0_), channel_id=1, source_target_pairs={{0,4},{1,3},{2,6},{3,1},{4,0},{5,7},{6,2},{7,5},{8,12},{9,11},{10,... | collective-permute-start | bytes 3145736 | tf_op jit(solution)/shard_map/ppermute | solution.py:537
  113.0 41.4 %collective-permute-start.19 = (bf16[4,64,2048]{2,1,0:T(8,128)(2,1)S(1)}, bf16[4,64,2048]{2,1,0:T(8,128)(2,1)}, u32[]{:S(2)}, u32[]{:S(2)}) collective-permute-start(bf16[4,64,2048]{2,1,0:T(8,128)(2,1)S(1)} %constant_dynamic-update-slice_fusion.10.rest_0_), channel_id=1, source_target_pairs={{0,2},{1,5},{2,0},{3,7},{4,6},{5,1},{6,4},{7,3},{8,10},{9,13},{10,... | collective-permute-start | bytes 3145736 | tf_op jit(solution)/shard_map/ppermute | solution.py:537
  114.4 40.1 %collective-permute-start.17 = (bf16[4,64,2048]{2,1,0:T(8,128)(2,1)S(1)}, bf16[4,64,2048]{2,1,0:T(8,128)(2,1)}, u32[]{:S(2)}, u32[]{:S(2)}) collective-permute-start(bf16[4,64,2048]{2,1,0:T(8,128)(2,1)S(1)} %constant_dynamic-update-slice_fusion.10.rest_0_), channel_id=1, source_target_pairs={{0,1},{1,0},{2,3},{3,2},{4,5},{5,4},{6,7},{7,6},{8,9},{9,8},{10,11... | collective-permute-start | bytes 3145736 | tf_op jit(solution)/shard_map/ppermute | solution.py:545
  114.4 40.0 %collective-permute-start.20 = (bf16[4,64,2048]{2,1,0:T(8,128)(2,1)S(1)}, bf16[4,64,2048]{2,1,0:T(8,128)(2,1)}, u32[]{:S(2)}, u32[]{:S(2)}) collective-permute-start(bf16[4,64,2048]{2,1,0:T(8,128)(2,1)S(1)} %collective-permute-done.16.rest_1_), channel_id=1, source_target_pairs={{0,2},{1,5},{2,0},{3,7},{4,6},{5,1},{6,4},{7,3},{8,10},{9,13},{10,... | collective-permute-start | bytes 3145736 | tf_op jit(solution)/shard_map/ppermute | solution.py:537
  115.1 39.4 %collective-permute-start.18 = (bf16[4,64,2048]{2,1,0:T(8,128)(2,1)S(1)}, bf16[4,64,2048]{2,1,0:T(8,128)(2,1)}, u32[]{:S(2)}, u32[]{:S(2)}) collective-permute-start(bf16[4,64,2048]{2,1,0:T(8,128)(2,1)S(1)} %collective-permute-done.16.rest_1_), channel_id=1, source_target_pairs={{0,1},{1,0},{2,3},{3,2},{4,5},{5,4},{6,7},{7,6},{8,9},{9,8},{10,11... | collective-permute-start | bytes 3145736 | tf_op jit(solution)/shard_map/ppermute | solution.py:545
  154.5 2.9 collective-permute-start.21
  154.8 4.1 %collective-permute-start.22 = (bf16[4,64,2048]{2,1,0:T(8,128)(2,1)}, bf16[4,64,2048]{2,1,0:T(8,128)(2,1)S(1)}, u32[]{:S(2)}, u32[]{:S(2)}) collective-permute-start(bf16[4,64,2048]{2,1,0:T(8,128)(2,1)} %collective-permute-done.20.rest_3_), channel_id=1, source_target_pairs={{0,1},{1,0},{2,3},{3,2},{4,5},{5,4},{6,7},{7,6},{8,9},{9,8},{10,11... | collective-permute-start | bytes 3145736 | tf_op jit(solution)/shard_map/ppermute | solution.py:545
  308.9 1.4 collective-permute-start.23
  311.0 6.0 %collective-permute-start.26 = (f32[2,1024]{1,0:T(2,128)S(1)}, f32[2,1024]{1,0:T(2,128)S(1)}, u32[]{:S(2)}, u32[]{:S(2)}) collective-permute-start(f32[2,1024]{1,0:T(2,128)S(1)} %add.94), channel_id=1, source_target_pairs={{0,6},{2,4},{4,2},{6,0},{8,14},{10,12},{12,10},{14,8},{16,22},{18,... | collective-permute-start | bytes 24584 | tf_op jit(solution)/shard_map/ppermute | solution.py:570
  312.2 4.8 %collective-permute-start.25 = (f32[2,1024]{1,0:T(2,128)S(1)}, f32[2,1024]{1,0:T(2,128)S(1)}, u32[]{:S(2)}, u32[]{:S(2)}) collective-permute-start(f32[2,1024]{1,0:T(2,128)S(1)} %add.94), channel_id=1, source_target_pairs={{0,4},{2,6},{4,0},{6,2},{8,12},{10,14},{12,8},{14,10},{16,20},{18,... | collective-permute-start | bytes 24584 | tf_op jit(solution)/shard_map/ppermute | solution.py:570
  313.1 4.0 %collective-permute-start.24 = (f32[2,1024]{1,0:T(2,128)S(1)}, f32[2,1024]{1,0:T(2,128)S(1)}, u32[]{:S(2)}, u32[]{:S(2)}) collective-permute-start(f32[2,1024]{1,0:T(2,128)S(1)} %add.94), channel_id=1, source_target_pairs={{0,2},{2,0},{4,6},{6,4},{8,10},{10,8},{12,14},{14,12},{16,18},{18,... | collective-permute-start | bytes 24584 | tf_op jit(solution)/shard_map/ppermute | solution.py:570
  317.1 5.5 %collective-permute-start.29 = (f32[2,1024]{1,0:T(2,128)S(1)}, f32[2,1024]{1,0:T(2,128)S(1)}, u32[]{:S(2)}, u32[]{:S(2)}) collective-permute-start(f32[2,1024]{1,0:T(2,128)S(1)} %add_add_fusion.1), channel_id=1, source_target_pairs={{0,24},{2,26},{4,28},{6,30},{8,16},{10,18},{12,20},{14,22},{16,8},... | collective-permute-start | bytes 24584 | tf_op jit(solution)/shard_map/ppermute | solution.py:570
  319.1 4.5 %collective-permute-start.28 = (f32[2,1024]{1,0:T(2,128)S(1)}, f32[2,1024]{1,0:T(2,128)S(1)}, u32[]{:S(2)}, u32[]{:S(2)}) collective-permute-start(f32[2,1024]{1,0:T(2,128)S(1)} %add_add_fusion.1), channel_id=1, source_target_pairs={{0,16},{2,18},{4,20},{6,22},{8,24},{10,26},{12,28},{14,30},{16,0},... | collective-permute-start | bytes 24584 | tf_op jit(solution)/shard_map/ppermute | solution.py:570
  319.1 4.5 %collective-permute-start.27 = (f32[2,1024]{1,0:T(2,128)S(1)}, f32[2,1024]{1,0:T(2,128)S(1)}, u32[]{:S(2)}, u32[]{:S(2)}) collective-permute-start(f32[2,1024]{1,0:T(2,128)S(1)} %add_add_fusion.1), channel_id=1, source_target_pairs={{0,8},{2,10},{4,12},{6,14},{8,0},{10,2},{12,4},{14,6},{16,24},{18,... | collective-permute-start | bytes 24584 | tf_op jit(solution)/shard_map/ppermute | solution.py:570
  (14 other events, 290.1 us)
Sparse Core Ops, SparseCore 0:
  24.6 95.3 all-gather.4
  242.6 51.6 all-gather.6

commit v6 on v5

--- a/solution.py
+++ b/solution.py
@@ -17,6 +17,7 @@
 WIDE = GROUP * HEAD_DIM
 PAIR = 2 * HEAD_DIM
 GROUPS = HEADS // GROUP
+FRONT_TILE = SLOTS
 TILE = 256
 STRIP = 32
 EPSILON = 1e-05
@@ -182,12 +183,12 @@
             q_t, k_t, d_out_t = qk_ref[0, 0, own], qk_ref[1, 0, own], dctx_ref[0, own]
             scores = mul(kv_ref[0, :, pair], half_rows(q_t, head)) + bias_ref[...]
             probs = jnp.exp(scores - lse_ref[0, 0, head : head + 1, :])
+            probs_low = low(probs)
             probs_grad = mul(kv_ref[1, :, pair], half_rows(d_out_t, head))
             scores_grad = low(probs * (probs_grad - delta_ref[0, 0, head : head + 1, :]))
-            probs_low = low(probs)
             d_v.append(low(mul(d_out_t, probs_low, NT)))
+            d_q.append(low(mul(k_t, scores_grad) * SCALE))
             d_k.append(low(mul(q_t, scores_grad, NT)))
-            d_q.append(low(mul(k_t, scores_grad) * SCALE))
         if arriving:
             wait_all(fetch_sets(rest[:count], w_ref, sem, start=False))
         ones = jnp.ones((16, SLOTS), jnp.bfloat16)
@@ -261,12 +262,10 @@
     slot_ref, x_ref, ctx_ref, vec_refs, bi_refs, first_ref, normal_ref, inv_ref, branch_ref, slope_ref, low_ref
 ):
     out_bias, gain_one, bias_one, down_bias = [row_of(ref) for ref in vec_refs]
-    attention = out_bias
-    for group in range(GROUPS):
-        part = slice(group * WIDE, (group + 1) * WIDE)
-        attention = attention + mul(ctx_ref[0, part], out_columns(first_ref, slot_ref, group), TT)
+    out_weight = jnp.concatenate([out_columns(first_ref, slot_ref, group) for group in range(GROUPS)], 1)
+    attention = mul(ctx_ref[0], out_weight, TT) + out_bias
     branch_ref[...] = attention
-    for start in range(0, TILE, STRIP):
+    for start in range(0, FRONT_TILE, STRIP):
         rows = slice(start, start + STRIP)
         normed, normal_one, inverse_one = norm_forward(wide(x_ref[rows]) + branch_ref[rows], gain_one, bias_one)
         normal_ref[rows] = normal_one
@@ -276,11 +275,16 @@
     normed_low = low_ref[...]
     branch = branch_ref[...]
 
+    def inner_of(piece):
+        return mul(normed_low, piece_weight(first_ref, None, slot_ref, piece, 0)) + piece_bias(bi_refs, piece)
+
+    inner = inner_of(PIECES[0])
     for piece in PIECES[:2]:
-        inner = mul(normed_low, piece_weight(first_ref, None, slot_ref, piece, 0)) + piece_bias(bi_refs, piece)
+        following = inner_of(PIECES[1]) if piece is PIECES[0] else None
         act, slope = gelu_and_slope(inner)
         slope_ref[:, flat_of(piece)] = low(slope)
         branch = branch + mul(low(act), piece_weight(first_ref, None, slot_ref, piece, 1), NT)
+        inner = following
     branch_ref[...] = branch
 
 
@@ -307,12 +311,18 @@
         low_ref[rows] = low(normal_ref[rows] * gain_one + bias_one)
     normed_low = low_ref[...]
     branch = branch_ref[...]
-    for piece in PIECES[2:]:
-        inner = mul(normed_low, weight(piece, 0)) + piece_bias(bi_refs, piece)
+    def inner_of(piece):
+        return mul(normed_low, weight(piece, 0)) + piece_bias(bi_refs, piece)
+
+    late_pieces = PIECES[2:]
+    inner = inner_of(late_pieces[0])
+    for i, piece in enumerate(late_pieces):
+        following = inner_of(late_pieces[i + 1]) if i + 1 < len(late_pieces) else None
         act, slope = gelu_and_slope(inner)
         flat = flat_of(piece)
         keep_ref[:, flat.start - 2 * FIRST : flat.stop - 2 * FIRST] = low(slope)
         branch = branch + mul(low(act), weight(piece, 1), NT)
+        inner = following
     acc_ref[...] = branch
     sums = [None] * 4
     for rows in strips:
@@ -342,9 +352,11 @@
         sums[0] = add(sums[0], wide(sum_one))
         sums[1] = add(sums[1], normed_grad)
     sum_one = sum_ref[...]
+    out_weight = jnp.concatenate([out_columns(first_ref, slot_ref, group) for group in range(GROUPS)], 1)
+    all_grads = low(mul(sum_one, out_weight))
     for group in range(GROUPS):
         part = slice(group * WIDE, (group + 1) * WIDE)
-        context_grad = low(mul(sum_one, out_columns(first_ref, slot_ref, group))).T
+        context_grad = all_grads[:, part].T
         dctx_ref[0, part] = context_grad
         product = wide(context_grad) * wide(ctx_ref[0, part])
         for head in range(GROUP):
@@ -459,8 +471,8 @@
     )(fills, slots, qk, kv, context_grad, delta, lse, seg_col, seg_row, *weights, sum_one)
 
 
-def tiles(width):
-    return pl.BlockSpec((TILE, width), lambda i: (i, 0))
+def tiles(width, tile=TILE):
+    return pl.BlockSpec((tile, width), lambda i: (i, 0))
 
 
 PER_ROW = SLOTS // TILE
@@ -471,16 +483,16 @@
     count = tokens.shape[0]
     return pl.pallas_call(
         front_kernel,
-        grid=(count // TILE,),
-        in_specs=[SCALARS, tiles(D), ROWS_T, wholes(vectors), wholes(in_bias), whole(first)],
-        out_specs=[tiles(D), tiles(128), tiles(D), tiles(2 * FIRST)],
+        grid=(count // FRONT_TILE,),
+        in_specs=[SCALARS, tiles(D, FRONT_TILE), pl.BlockSpec((1, D, SLOTS), lambda i: (i, 0, 0)), wholes(vectors), wholes(in_bias), whole(first)],
+        out_specs=[tiles(D, FRONT_TILE), tiles(128, FRONT_TILE), tiles(D, FRONT_TILE), tiles(2 * FIRST, FRONT_TILE)],
         out_shape=[
             jax.ShapeDtypeStruct((count, D), jnp.float32),
             jax.ShapeDtypeStruct((count, 128), jnp.float32),
             jax.ShapeDtypeStruct((count, D), jnp.float32),
             jax.ShapeDtypeStruct((count, 2 * FIRST), jnp.bfloat16),
         ],
-        scratch_shapes=[pltpu.VMEM((TILE, D), jnp.bfloat16)],
+        scratch_shapes=[pltpu.VMEM((FRONT_TILE, D), jnp.bfloat16)],
         compiler_params=params(1),
         cost_estimate=cost(25e9, 30e6),
         name="feed_front",

time: 332 us -> 325 us (0.979)
  Pallas kernels: 239 us -> 232 us
where the time goes in v6:
time: 325 us; the launch traced here: 324 us
  Pallas kernels  232 us (71%)
  starting transfers between devices  34.9 us (11%)
  waiting for transfers between devices  28.6 us (9%)
  between operations  14.5 us (4%)
  local copies, waits for them, and re-layouts  10.1 us (3%)
  other arithmetic  4.3 us (1%)
    pallas_call x1, Pallas kernels, feed_back(): pl.pallas_call(partial(back_kernel, len(late)), grid=(count // TILE,), in...  80.4 us
    pallas_call x1, Pallas kernels, attend_back(): pl.pallas_call(partial(attend_back_kernel, len(weights)), grid=(rows, GRO...  63.9 us
    pallas_call x4, Pallas kernels, attend(): pl.pallas_call(partial(attend_kernel, step, len(pieces)), grid=(rows,), i...  55.3 us
    pallas_call x1, Pallas kernels, feed_front(): pl.pallas_call(front_kernel, grid=(count // FRONT_TILE,), in_specs=[SCALA...  32 us
    ppermute x13, starting transfers between devices, partner(): return lax.ppermute(block, ('rows', 'tp'), pairs)  24.7 us
    ppermute x13, waiting for transfers between devices, partner(): return lax.ppermute(block, ('rows', 'tp'), pairs)  16.8 us
    ppermute x6, starting transfers between devices, got(): return lax.ppermute(values, 'rows', [(i, i ^ distance) for i in range(n)])  7.94 us
  transfers between devices with their start and end apart: 32, of which 10 were waited for; matrix products, arithmetic and copies ran while one was open for 3% of the time, Pallas kernels for 47%

profile of v6, /device:TPU:0, one launch (start us, length us, event | category | flops | bytes accessed | tf_op | source)
XLA Modules:
  0.0 324.0 jit_solution(17767371011987014886)
XLA Ops:
  8.2 3.1 collective-permute-start
  12.4 2.5 collective-permute-done
  15.0 2.0 collective-permute-start.2
  16.9 2.6 collective-permute-start.1
  19.5 1.6 pad_maximum_fusion.1
  21.1 3.4 %collective-permute-done.1 = bf16[2,3,64,256]{3,2,1,0:T(8,128)(2,1)S(1)} collective-permute-done((bf16[2,3,64,256]{3,2,1,0:T(8,128)(2,1)S(1)}, bf16[2,3,64,256]{3,2,1,0:T(8,128)(2,1)S(1)}, u32[]{:S(2)}, u32[]{:S(2)}) %collective-permute-start.1) | collective-permute-done | bytes 196640 | tf_op jit(solution)/shard_map/ppermute | solution.py:549
  25.2 1.6 collective-permute-start.3
  26.8 2.9 collective-permute-start.4
  32.2 2.0 collective-permute-done.4
  34.4 2.8 collective-permute-start.7
  37.3 1.4 copy.39.segc_ref
  38.7 8.8 %collective-permute-done.7.rest_1_ = bf16[8,3,64,256]{3,2,1,0:T(8,128)(2,1)S(1)} collective-permute-done((bf16[8,3,64,256]{3,2,1,0:T(8,128)(2,1)S(1)}, bf16[8,3,64,256]{3,2,1,0:T(8,128)(2,1)S(1)}, u32[]{:S(2)}, u32[]{:S(2)}) %collective-permute-start.7) | collective-permute-done | bytes 786464 | tf_op jit(solution)/shard_map/ppermute | solution.py:549
  47.5 1.5 collective-permute-start.11
  49.0 1.5 collective-permute-start.10
  50.8 13.9 %attend.4 = (bf16[2,4,1024,512]{3,2,1,0:T(8,128)(2,1)}, bf16[2,2048,1024]{2,1,0:T(8,128)(2,1)}, bf16[4,1024,512]{2,1,0:T(8,128)(2,1)}, f32[4,4,4,512]{3,2,1,0:T(4,128)}) custom-call(s32[4]{0:T(128)} %dynamic_slice.7.fill_ref, s32[3,16]{1,0:T(4,128)} %concatenate.33.slot_ref, bf16[2048,1024]{1,0:T(8,128)(2,1)} %x_ref.9, s32[4,512,1]{2,1,0:T(8,128)} %copy.39.segc_ref, ...), custom_call_target="tpu_custom_call" | custom-call | flops 15000000512 | bytes 10000000 | tf_op jit(solution)/shard_map/attend/pallas_call | solution.py:402
  65.6 2.3 collective-permute-start.15
  67.9 13.8 %attend.5 = (bf16[2,4,1024,512]{3,2,1,0:T(8,128)(2,1)}, bf16[2,2048,1024]{2,1,0:T(8,128)(2,1)}, bf16[4,1024,512]{2,1,0:T(8,128)(2,1)}, f32[4,4,4,512]{3,2,1,0:T(4,128)}) custom-call(s32[4]{0:T(128)} %dynamic_slice.7.fill_ref, s32[3,16]{1,0:T(4,128)} %concatenate.33.slot_ref, ...), custom_call_target="tpu_custom_call", output_to_operand_aliasing={{0}: (8, {}), {1}: (9, {}), {2}: (10, {}), {3}: (11, {})} | custom-call | flops 15000000512 | bytes 10000000 | tf_op jit(solution)/shard_map/attend/pallas_call | solution.py:402
  82.7 13.8 %attend.6 = (bf16[2,4,1024,512]{3,2,1,0:T(8,128)(2,1)}, bf16[2,2048,1024]{2,1,0:T(8,128)(2,1)}, bf16[4,1024,512]{2,1,0:T(8,128)(2,1)}, f32[4,4,4,512]{3,2,1,0:T(4,128)}) custom-call(s32[4]{0:T(128)} %dynamic_slice.7.fill_ref, s32[3,16]{1,0:T(4,128)} %concatenate.33.slot_ref, ...), custom_call_target="tpu_custom_call", output_to_operand_aliasing={{0}: (8, {}), {1}: (9, {}), {2}: (10, {}), {3}: (11, {})} | custom-call | flops 15000000512 | bytes 10000000 | tf_op jit(solution)/shard_map/attend/pallas_call | solution.py:402
  97.5 1.7 collective-permute-start.16
  99.2 13.8 %attend.7 = (bf16[2,4,1024,512]{3,2,1,0:T(8,128)(2,1)}, bf16[2,2048,1024]{2,1,0:T(8,128)(2,1)}, bf16[4,1024,512]{2,1,0:T(8,128)(2,1)}, f32[4,4,4,512]{3,2,1,0:T(4,128)}) custom-call(s32[4]{0:T(128)} %dynamic_slice.7.fill_ref, s32[3,16]{1,0:T(4,128)} %concatenate.33.slot_ref, ...), custom_call_target="tpu_custom_call", output_to_operand_aliasing={{0}: (8, {}), {1}: (9, {}), {2}: (10, {}), {3}: (11, {})} | custom-call | flops 15000000512 | bytes 10000000 | tf_op jit(solution)/shard_map/attend/pallas_call | solution.py:402
  113.0 1.3 collective-permute-start.19
  115.2 4.7 %all-gather.5.cloned.1.call-done = bf16[2048,2560]{1,0:T(8,128)(2,1)} async-done(((bf16[64,2560]{1,0:T(8,128)(2,1)}), bf16[2048,2560]{1,0:T(8,128)(2,1)}) %all-gather.5.cloned.1.call-update) | async-done | bytes 10485776 | tf_op jit(solution)/shard_map/all_gather | solution.py:629
  120.0 32.0 %feed_front.1 = (f32[2048,1024]{1,0:T(8,128)}, f32[2048,128]{1,0:T(8,128)}, f32[2048,1024]{1,0:T(8,128)}, bf16[2048,2048]{1,0:T(8,128)(2,1)}) custom-call(s32[3,16]{1,0:T(4,128)} %concatenate.33.slot_ref, bf16[2048,1024]{1,0:T(8,128)(2,1)} %x_ref.9, bf16[4,1024,512]{2,1,0:T(8,128)(2,1)} %get-tuple-element.172.ctx_ref, bf16[1024]{0:T(1024)(128)(2,1)} %vec_refs_0_.2, ...), custom_call_target="tpu_custom_call" | custom-call | flops 24999999488 | bytes 30000000 | tf_op jit(solution)/shard_map/feed_front/pallas_call | solution.py:484
  152.6 2.4 collective-permute-done.21.rest_6_
  155.0 1.5 collective-permute-done.22.rest_7_
  157.4 80.4 %feed_back.1 = (bf16[2048,1024]{1,0:T(8,128)(2,1)}, bf16[4,1024,512]{2,1,0:T(8,128)(2,1)}, f32[4,4,4,512]{3,2,1,0:T(4,128)}, bf16[2048,1024]{1,0:T(8,128)(2,1)}, f32[8,1024]{1,0:T(8,128)}) custom-call(s32[3,16]{1,0:T(4,128)} %concatenate.33.slot_ref, f32[2048,1024]{1,0:T(8,128)} %get-tuple-element.182.normal_ref, f32[2048,128]{1,0:T(8,128)} %get-tuple-element.183.inv_ref, ...), custom_call_target="tpu_custom_call" | custom-call | flops 74999996416 | bytes 40000000 | tf_op jit(solution)/shard_map/feed_back/pallas_call | solution.py:504
  237.9 63.9 %attend_back.1 = (bf16[2048,1024]{1,0:T(8,128)(2,1)}, f32[2,1024]{1,0:T(2,128)}) custom-call(s32[4]{0:T(128)} %dynamic_slice.7.fill_ref, s32[3,16]{1,0:T(4,128)} %concatenate.33.slot_ref, bf16[2,4,1024,512]{3,2,1,0:T(8,128)(2,1)} %get-tuple-element.191.qk_ref, bf16[2,2048,1024]{2,1,0:T(8,128)(2,1)} %get-tuple-element.192.kv_ref, ...), custom_call_target="tpu_custom_call" | custom-call | flops 49999998976 | bytes 30000000 | tf_op jit(solution)/shard_map/attend_back/pallas_call | solution.py:439
  303.9 1.3 collective-permute-start.26
  306.1 1.3 collective-permute-start.24
  307.4 1.3 bitcast_reduce_fusion
  310.0 2.0 collective-permute-start.29
  312.0 2.4 collective-permute-start.27
  (102 shorter events, 17.9 us)
Async XLA Ops:
  7.2 112.8 %all-gather.5.cloned.1.call-start = ((), (), s32[]{:S(2)}) async-start(), calls=%async_computation | async-start | bytes 10813440 | tf_op jit(solution)/shard_map/all_gather | solution.py:629
  8.2 6.7 %collective-permute-start = (bf16[1,3,64,256]{3,2,1,0:T(8,128)(2,1)S(1)}, bf16[1,3,64,256]{3,2,1,0:T(8,128)(2,1)S(1)}, u32[]{:S(2)}, u32[]{:S(2)}) collective-permute-start(bf16[1,3,64,256]{3,2,1,0:T(8,128)(2,1)S(1)} %get-tuple-element.221), channel_id=1, source_target_pairs={{0,8},{1,17},{2,10},{3,19},{4,12},{5,21},{6,14},{7,23},{8,0},{9,25... | collective-permute-start | bytes 294920 | tf_op jit(solution)/shard_map/ppermute | solution.py:549
  15.0 6.1 %collective-permute-start.2 = (bf16[1,3,64,256]{3,2,1,0:T(8,128)(2,1)S(1)}, bf16[1,3,64,256]{3,2,1,0:T(8,128)(2,1)S(1)}, u32[]{:S(2)}, u32[]{:S(2)}) collective-permute-start(bf16[1,3,64,256]{3,2,1,0:T(8,128)(2,1)S(1)} %get-tuple-element.116), channel_id=1, source_target_pairs={{0,8},{1,17},{2,10},{3,19},{4,12},{5,21},{6,14},{7,23},{8,0},{9,25... | collective-permute-start | bytes 294920 | tf_op jit(solution)/shard_map/ppermute | solution.py:549
  16.9 7.5 %collective-permute-start.1 = (bf16[2,3,64,256]{3,2,1,0:T(8,128)(2,1)S(1)}, bf16[2,3,64,256]{3,2,1,0:T(8,128)(2,1)S(1)}, u32[]{:S(2)}, u32[]{:S(2)}) collective-permute-start(bf16[2,3,64,256]{3,2,1,0:T(8,128)(2,1)S(1)} %pad_maximum_fusion.2), channel_id=1, source_target_pairs={{0,16},{1,9},{2,18},{3,11},{4,20},{5,13},{6,22},{7,15},{8,24},{9,1... | collective-permute-start | bytes 589832 | tf_op jit(solution)/shard_map/ppermute | solution.py:549
  24.5 283.0 %all-gather.7.cloned.1.call-start = ((), (), s32[]{:S(2)}) async-start(), calls=%async_computation.1 | async-start | bytes 1081344 | tf_op jit(solution)/shard_map/all_gather | solution.py:694
  24.5 7.7 %collective-permute-start.5 = (bf16[2,512]{1,0:T(2,128)(2,1)}, bf16[2,512]{1,0:T(2,128)(2,1)S(1)}, u32[]{:S(2)}, u32[]{:S(2)}) collective-permute-start(bf16[2,512]{1,0:T(2,128)(2,1)} %b_ref.1), channel_id=1, source_target_pairs={{0,1},{1,0},{2,3},{3,2},{4,5},{5,4},{6,7},{7,6},{8,9},{9,8},{10,11... | collective-permute-start | bytes 6152 | tf_op jit(solution)/shard_map/ppermute | solution.py:557
  24.7 7.5 %collective-permute-start.6 = (bf16[2048]{0:T(1024)(128)(2,1)}, bf16[2048]{0:T(1024)(128)(2,1)S(1)}, u32[]{:S(2)}, u32[]{:S(2)}) collective-permute-start(bf16[2048]{0:T(1024)(128)(2,1)} %bi_refs_0_.1), channel_id=1, source_target_pairs={{0,1},{1,0},{2,3},{3,2},{4,5},{5,4},{6,7},{7,6},{8,9},{9,8},{10,11... | collective-permute-start | bytes 12296 | tf_op jit(solution)/shard_map/ppermute | solution.py:557
  25.2 9.1 %collective-permute-start.3 = (bf16[4,3,64,256]{3,2,1,0:T(8,128)(2,1)S(1)}, bf16[4,3,64,256]{3,2,1,0:T(8,128)(2,1)S(1)}, u32[]{:S(2)}, u32[]{:S(2)}) collective-permute-start(bf16[4,3,64,256]{3,2,1,0:T(8,128)(2,1)S(1)} %constant_dynamic-update-slice_fusion), channel_id=1, source_target_pairs={{0,4},{1,3},{2,6},{3,1},{4,0},{5,7},{6,2},{7,5},{8,12},{9,11},{10,... | collective-permute-start | bytes 1179656 | tf_op jit(solution)/shard_map/ppermute | solution.py:549
  26.8 7.5 %collective-permute-start.4 = (bf16[2,3,64,256]{3,2,1,0:T(8,128)(2,1)S(1)}, bf16[2,3,64,256]{3,2,1,0:T(8,128)(2,1)S(1)}, u32[]{:S(2)}, u32[]{:S(2)}) collective-permute-start(bf16[2,3,64,256]{3,2,1,0:T(8,128)(2,1)S(1)} %constant_dynamic-update-slice_fusion.2), channel_id=1, source_target_pairs={{0,16},{1,9},{2,18},{3,11},{4,20},{5,13},{6,22},{7,15},{8,24},{9,1... | collective-permute-start | bytes 589832 | tf_op jit(solution)/shard_map/ppermute | solution.py:549
  34.3 4.3 %collective-permute-start.8 = (bf16[8,3,64,256]{3,2,1,0:T(8,128)(2,1)S(1)}, bf16[8,3,64,256]{3,2,1,0:T(8,128)(2,1)S(1)}, u32[]{:S(2)}, u32[]{:S(2)}) collective-permute-start(bf16[8,3,64,256]{3,2,1,0:T(8,128)(2,1)S(1)} %constant_dynamic-update-slice_fusion.4.rest_0_), channel_id=1, source_target_pairs={{0,1},{1,0},{2,3},{3,2},{4,5},{5,4},{6,7},{7,6},{8,9},{9,8},{10,11... | collective-permute-start | bytes 2359304 | tf_op jit(solution)/shard_map/ppermute | solution.py:557
  34.4 13.1 %collective-permute-start.7 = (bf16[8,3,64,256]{3,2,1,0:T(8,128)(2,1)S(1)}, bf16[8,3,64,256]{3,2,1,0:T(8,128)(2,1)S(1)}, u32[]{:S(2)}, u32[]{:S(2)}) collective-permute-start(bf16[8,3,64,256]{3,2,1,0:T(8,128)(2,1)S(1)} %constant_dynamic-update-slice_fusion.4.rest_0_), channel_id=1, source_target_pairs={{0,2},{1,5},{2,0},{3,7},{4,6},{5,1},{6,4},{7,3},{8,10},{9,13},{10,... | collective-permute-start | bytes 2359304 | tf_op jit(solution)/shard_map/ppermute | solution.py:549
  47.5 17.3 %collective-permute-start.11 = (bf16[1,64,2048]{2,1,0:T(8,128)(2,1)S(1)}, bf16[1,64,2048]{2,1,0:T(8,128)(2,1)S(1)}, u32[]{:S(2)}, u32[]{:S(2)}) collective-permute-start(bf16[1,64,2048]{2,1,0:T(8,128)(2,1)S(1)} %maximum_bitcast_fusion), channel_id=1, source_target_pairs={{0,8},{1,17},{2,10},{3,19},{4,12},{5,21},{6,14},{7,23},{8,0},{9,25... | collective-permute-start | bytes 786440 | tf_op jit(solution)/shard_map/ppermute | solution.py:549
  49.0 15.8 %collective-permute-start.10 = (bf16[4,3,64,256]{3,2,1,0:T(8,128)(2,1)S(1)}, bf16[4,3,64,256]{3,2,1,0:T(8,128)(2,1)S(1)}, u32[]{:S(2)}, u32[]{:S(2)}) collective-permute-start(bf16[4,3,64,256]{3,2,1,0:T(8,128)(2,1)S(1)} %pad_maximum_fusion), channel_id=1, source_target_pairs={{0,4},{1,3},{2,6},{3,1},{4,0},{5,7},{6,2},{7,5},{8,12},{9,11},{10,... | collective-permute-start | bytes 1179656 | tf_op jit(solution)/shard_map/ppermute | solution.py:549
  50.5 14.3 %collective-permute-start.9 = (bf16[8,3,64,256]{3,2,1,0:T(8,128)(2,1)S(1)}, bf16[8,3,64,256]{3,2,1,0:T(8,128)(2,1)}, u32[]{:S(2)}, u32[]{:S(2)}) collective-permute-start(bf16[8,3,64,256]{3,2,1,0:T(8,128)(2,1)S(1)} %collective-permute-done.7.rest_1_), channel_id=1, source_target_pairs={{0,1},{1,0},{2,3},{3,2},{4,5},{5,4},{6,7},{7,6},{8,9},{9,8},{10,11... | collective-permute-start | bytes 2359304 | tf_op jit(solution)/shard_map/ppermute | solution.py:557
  64.9 16.9 %collective-permute-start.13 = (bf16[8,3,64,256]{3,2,1,0:T(8,128)(2,1)S(1)}, bf16[8,3,64,256]{3,2,1,0:T(8,128)(2,1)S(1)}, u32[]{:S(2)}, u32[]{:S(2)}) collective-permute-start(bf16[8,3,64,256]{3,2,1,0:T(8,128)(2,1)S(1)} %constant_dynamic-update-slice_fusion.6.rest_0_.rest_4_), channel_id=1, source_target_pairs={{0,2},{1,5},{2,0},{3,7},{4,6},{5,1},{6,4},{7,3},{8,10},{9,13},{10,... | collective-permute-start | bytes 2359304 | tf_op jit(solution)/shard_map/ppermute | solution.py:549
  65.6 16.2 %collective-permute-start.12 = (bf16[8,3,64,256]{3,2,1,0:T(8,128)(2,1)S(1)}, bf16[8,3,64,256]{3,2,1,0:T(8,128)(2,1)}, u32[]{:S(2)}, u32[]{:S(2)}) collective-permute-start(bf16[8,3,64,256]{3,2,1,0:T(8,128)(2,1)S(1)} %constant_dynamic-update-slice_fusion.6.rest_0_.rest_4_), channel_id=1, source_target_pairs={{0,1},{1,0},{2,3},{3,2},{4,5},{5,4},{6,7},{7,6},{8,9},{9,8},{10,11... | collective-permute-start | bytes 2359304 | tf_op jit(solution)/shard_map/ppermute | solution.py:557
  65.6 30.9 %collective-permute-start.15 = (bf16[2,64,2048]{2,1,0:T(8,128)(2,1)S(1)}, bf16[2,64,2048]{2,1,0:T(8,128)(2,1)S(1)}, u32[]{:S(2)}, u32[]{:S(2)}) collective-permute-start(bf16[2,64,2048]{2,1,0:T(8,128)(2,1)S(1)} %constant_dynamic-update-slice_fusion.8), channel_id=1, source_target_pairs={{0,16},{1,9},{2,18},{3,11},{4,20},{5,13},{6,22},{7,15},{8,24},{9,1... | collective-permute-start | bytes 1572872 | tf_op jit(solution)/shard_map/ppermute | solution.py:549
  81.8 14.7 %collective-permute-start.14 = (bf16[8,3,64,256]{3,2,1,0:T(8,128)(2,1)S(1)}, bf16[8,3,64,256]{3,2,1,0:T(8,128)(2,1)S(1)}, u32[]{:S(2)}, u32[]{:S(2)}) collective-permute-start(bf16[8,3,64,256]{3,2,1,0:T(8,128)(2,1)S(1)} %collective-permute-done.13.rest_1_.rest_5_), channel_id=1, source_target_pairs={{0,1},{1,0},{2,3},{3,2},{4,5},{5,4},{6,7},{7,6},{8,9},{9,8},{10,11... | collective-permute-start | bytes 2359304 | tf_op jit(solution)/shard_map/ppermute | solution.py:557
  97.5 15.5 %collective-permute-start.16 = (bf16[4,64,2048]{2,1,0:T(8,128)(2,1)S(1)}, bf16[4,64,2048]{2,1,0:T(8,128)(2,1)S(1)}, u32[]{:S(2)}, u32[]{:S(2)}) collective-permute-start(bf16[4,64,2048]{2,1,0:T(8,128)(2,1)S(1)} %constant_dynamic-update-slice_fusion.10.rest_0_), channel_id=1, source_target_pairs={{0,4},{1,3},{2,6},{3,1},{4,0},{5,7},{6,2},{7,5},{8,12},{9,11},{10,... | collective-permute-start | bytes 3145736 | tf_op jit(solution)/shard_map/ppermute | solution.py:549
  113.0 39.0 %collective-permute-start.19 = (bf16[4,64,2048]{2,1,0:T(8,128)(2,1)S(1)}, bf16[4,64,2048]{2,1,0:T(8,128)(2,1)}, u32[]{:S(2)}, u32[]{:S(2)}) collective-permute-start(bf16[4,64,2048]{2,1,0:T(8,128)(2,1)S(1)} %constant_dynamic-update-slice_fusion.10.rest_0_), channel_id=1, source_target_pairs={{0,2},{1,5},{2,0},{3,7},{4,6},{5,1},{6,4},{7,3},{8,10},{9,13},{10,... | collective-permute-start | bytes 3145736 | tf_op jit(solution)/shard_map/ppermute | solution.py:549
  114.4 37.6 %collective-permute-start.17 = (bf16[4,64,2048]{2,1,0:T(8,128)(2,1)S(1)}, bf16[4,64,2048]{2,1,0:T(8,128)(2,1)}, u32[]{:S(2)}, u32[]{:S(2)}) collective-permute-start(bf16[4,64,2048]{2,1,0:T(8,128)(2,1)S(1)} %constant_dynamic-update-slice_fusion.10.rest_0_), channel_id=1, source_target_pairs={{0,1},{1,0},{2,3},{3,2},{4,5},{5,4},{6,7},{7,6},{8,9},{9,8},{10,11... | collective-permute-start | bytes 3145736 | tf_op jit(solution)/shard_map/ppermute | solution.py:557
  114.4 37.6 %collective-permute-start.20 = (bf16[4,64,2048]{2,1,0:T(8,128)(2,1)S(1)}, bf16[4,64,2048]{2,1,0:T(8,128)(2,1)}, u32[]{:S(2)}, u32[]{:S(2)}) collective-permute-start(bf16[4,64,2048]{2,1,0:T(8,128)(2,1)S(1)} %collective-permute-done.16.rest_1_), channel_id=1, source_target_pairs={{0,2},{1,5},{2,0},{3,7},{4,6},{5,1},{6,4},{7,3},{8,10},{9,13},{10,... | collective-permute-start | bytes 3145736 | tf_op jit(solution)/shard_map/ppermute | solution.py:549
  115.1 36.9 %collective-permute-start.18 = (bf16[4,64,2048]{2,1,0:T(8,128)(2,1)S(1)}, bf16[4,64,2048]{2,1,0:T(8,128)(2,1)}, u32[]{:S(2)}, u32[]{:S(2)}) collective-permute-start(bf16[4,64,2048]{2,1,0:T(8,128)(2,1)S(1)} %collective-permute-done.16.rest_1_), channel_id=1, source_target_pairs={{0,1},{1,0},{2,3},{3,2},{4,5},{5,4},{6,7},{7,6},{8,9},{9,8},{10,11... | collective-permute-start | bytes 3145736 | tf_op jit(solution)/shard_map/ppermute | solution.py:557
  152.0 2.9 collective-permute-start.21
  152.3 4.1 %collective-permute-start.22 = (bf16[4,64,2048]{2,1,0:T(8,128)(2,1)}, bf16[4,64,2048]{2,1,0:T(8,128)(2,1)S(1)}, u32[]{:S(2)}, u32[]{:S(2)}) collective-permute-start(bf16[4,64,2048]{2,1,0:T(8,128)(2,1)} %collective-permute-done.20.rest_3_), channel_id=1, source_target_pairs={{0,1},{1,0},{2,3},{3,2},{4,5},{5,4},{6,7},{7,6},{8,9},{9,8},{10,11... | collective-permute-start | bytes 3145736 | tf_op jit(solution)/shard_map/ppermute | solution.py:557
  301.8 1.4 collective-permute-start.23
  303.9 6.0 %collective-permute-start.26 = (f32[2,1024]{1,0:T(2,128)S(1)}, f32[2,1024]{1,0:T(2,128)S(1)}, u32[]{:S(2)}, u32[]{:S(2)}) collective-permute-start(f32[2,1024]{1,0:T(2,128)S(1)} %add.94), channel_id=1, source_target_pairs={{0,6},{2,4},{4,2},{6,0},{8,14},{10,12},{12,10},{14,8},{16,22},{18,... | collective-permute-start | bytes 24584 | tf_op jit(solution)/shard_map/ppermute | solution.py:582
  305.3 4.7 %collective-permute-start.25 = (f32[2,1024]{1,0:T(2,128)S(1)}, f32[2,1024]{1,0:T(2,128)S(1)}, u32[]{:S(2)}, u32[]{:S(2)}) collective-permute-start(f32[2,1024]{1,0:T(2,128)S(1)} %add.94), channel_id=1, source_target_pairs={{0,4},{2,6},{4,0},{6,2},{8,12},{10,14},{12,8},{14,10},{16,20},{18,... | collective-permute-start | bytes 24584 | tf_op jit(solution)/shard_map/ppermute | solution.py:582
  306.1 3.9 %collective-permute-start.24 = (f32[2,1024]{1,0:T(2,128)S(1)}, f32[2,1024]{1,0:T(2,128)S(1)}, u32[]{:S(2)}, u32[]{:S(2)}) collective-permute-start(f32[2,1024]{1,0:T(2,128)S(1)} %add.94), channel_id=1, source_target_pairs={{0,2},{2,0},{4,6},{6,4},{8,10},{10,8},{12,14},{14,12},{16,18},{18,... | collective-permute-start | bytes 24584 | tf_op jit(solution)/shard_map/ppermute | solution.py:582
  310.0 5.5 %collective-permute-start.29 = (f32[2,1024]{1,0:T(2,128)S(1)}, f32[2,1024]{1,0:T(2,128)S(1)}, u32[]{:S(2)}, u32[]{:S(2)}) collective-permute-start(f32[2,1024]{1,0:T(2,128)S(1)} %add_add_fusion.1), channel_id=1, source_target_pairs={{0,24},{2,26},{4,28},{6,30},{8,16},{10,18},{12,20},{14,22},{16,8},... | collective-permute-start | bytes 24584 | tf_op jit(solution)/shard_map/ppermute | solution.py:582
  312.0 4.5 %collective-permute-start.28 = (f32[2,1024]{1,0:T(2,128)S(1)}, f32[2,1024]{1,0:T(2,128)S(1)}, u32[]{:S(2)}, u32[]{:S(2)}) collective-permute-start(f32[2,1024]{1,0:T(2,128)S(1)} %add_add_fusion.1), channel_id=1, source_target_pairs={{0,16},{2,18},{4,20},{6,22},{8,24},{10,26},{12,28},{14,30},{16,0},... | collective-permute-start | bytes 24584 | tf_op jit(solution)/shard_map/ppermute | solution.py:582
  312.0 4.5 %collective-permute-start.27 = (f32[2,1024]{1,0:T(2,128)S(1)}, f32[2,1024]{1,0:T(2,128)S(1)}, u32[]{:S(2)}, u32[]{:S(2)}) collective-permute-start(f32[2,1024]{1,0:T(2,128)S(1)} %add_add_fusion.1), channel_id=1, source_target_pairs={{0,8},{2,10},{4,12},{6,14},{8,0},{10,2},{12,4},{14,6},{16,24},{18,... | collective-permute-start | bytes 24584 | tf_op jit(solution)/shard_map/ppermute | solution.py:582
  (14 other events, 285.2 us)
Sparse Core Ops, SparseCore 0:
  24.6 95.3 all-gather.4
  238.0 51.7 all-gather.6

commit v7 on v6

--- a/solution.py
+++ b/solution.py
@@ -125,7 +125,8 @@
     x = x_ref[...]
     weight = [set_weight(w_ref, slot_ref, other, i) for i in range(3)]
     columns = slice(half * WIDE, (half + 1) * WIDE)
-    b_q, b_v = wide(b_ref[0:1, columns]), wide(b_ref[1:2, columns])
+    biases = wide(b_ref[...])[:, columns]
+    b_q, b_v = biases[0:1], biases[1:2]
     bias = mask_bias(segc_ref[0], segr_ref[0], fill_ref[pl.program_id(0)])
     q = low(mul(x, weight[0]) + b_q)
     k = low(mul(x, weight[1]))
@@ -247,7 +248,7 @@
 def piece_bias(b_refs, piece):
     late, other, start, size = piece
     begin = FIRST * late + start
-    return wide(b_refs[other][begin : begin + size]).reshape(1, size)
+    return wide(b_refs[other][...]).reshape(1, FF // 2)[:, begin : begin + size]
 
 
 def out_columns(first_ref, slot_ref, group):
@@ -575,7 +576,7 @@
     return jnp.concatenate([ordered, jnp.full((1, n), core, jnp.int32)], 0)
 
 
-def sum_over_rows(values, n, beside):
+def sum_over_rows(values, n, beside, steps):
     bits = n.bit_length() - 1
 
     def got(distance):
@@ -583,9 +584,15 @@
 
     for bit in range(0, bits - 1, 2):
         near, far, both = [got(j << bit) for j in (1, 2, 3)]
+        if steps:
+            beside = steps[0](beside)
+            steps = steps[1:]
         near, far, both, beside = together(near, far, both, beside)
         values = (values + near) + (far + both)
-    return values + got(1 << (bits - 1)) if bits % 2 else values, beside
+    values = values + got(1 << (bits - 1)) if bits % 2 else values
+    for step in steps:
+        beside = step(beside)
+    return values, beside
 
 
 def shards(
@@ -691,14 +698,20 @@
     layer_out, context_grad, delta, sum_one, grads = feed_back(
         slots, front, cotangent, context, first, late_own + late_far + late_others, vectors, b_in
     )
-    sums = jnp.sum(lax.all_gather(grads, ("rows", "tp"), axis=0), 0)
-    sums = [sums[0], sums[1], sums[4:].reshape(-1), sums[2], sums[3]]
+    grads = lax.all_gather(grads, ("rows", "tp"), axis=0)
+
+    def summed(grads):
+        return jnp.sum(grads, 0)
+
+    def taken_apart(sums):
+        return sums[0], sums[1], sums[4:].reshape(-1), sums[2], sums[3]
+
     a_set = [a, a_got, a_other, a_other_got]
     b_set = [b, b_got, b_other, b_other_got]
     tokens_grad, qv_grads = attend_back(
         qk, kv, context_grad, delta, lse, *small, a_set + b_set, sum_one
     )
-    qv, sums = sum_over_rows(qv_grads + swap_cores(qv_grads), n, sums)
+    qv, sums = sum_over_rows(qv_grads + swap_cores(qv_grads), n, grads, (summed, taken_apart))
     return (layer_out, tokens_grad, qv, *sums)
 
 

time: 325 us -> 324 us (level)
  transfers between devices with their start and end apart: 32 -> 32, of which waited for: 10 -> 11; matrix products, arithmetic and copies ran while one was open for 3% -> 3% of each run, Pallas kernels for 47% -> 47%
where the time goes in v7:
time: 324 us
  Pallas kernels  232 us (72%)
  starting transfers between devices  34.9 us (11%)
  waiting for transfers between devices  28.3 us (9%)
  between operations  14.5 us (4%)
  local copies, waits for them, and re-layouts  10.1 us (3%)
  other arithmetic  4.3 us (1%)
    pallas_call x1, Pallas kernels, feed_back(): pl.pallas_call(partial(back_kernel, len(late)), grid=(count // TILE,), in...  80.4 us
    pallas_call x1, Pallas kernels, attend_back(): pl.pallas_call(partial(attend_back_kernel, len(weights)), grid=(rows, GRO...  63.9 us
    pallas_call x4, Pallas kernels, attend(): pl.pallas_call(partial(attend_kernel, step, len(pieces)), grid=(rows,), i...  55.3 us
    pallas_call x1, Pallas kernels, feed_front(): pl.pallas_call(front_kernel, grid=(count // FRONT_TILE,), in_specs=[SCALA...  32 us
    ppermute x13, starting transfers between devices, partner(): return lax.ppermute(block, ('rows', 'tp'), pairs)  24.7 us
    ppermute x13, waiting for transfers between devices, partner(): return lax.ppermute(block, ('rows', 'tp'), pairs)  16.8 us
    ppermute x6, starting transfers between devices, got(): return lax.ppermute(values, 'rows', [(i, i ^ distance) for i in range(n)])  7.94 us
  transfers between devices with their start and end apart: 32, of which 11 were waited for; matrix products, arithmetic and copies ran while one was open for 3% of the time, Pallas kernels for 47%

profile of v7, /device:TPU:0, one launch (start us, length us, event | category | flops | bytes accessed | tf_op | source)
XLA Modules:
  0.0 323.6 jit_solution(264673272686787008)
XLA Ops:
  8.2 3.1 collective-permute-start
  12.4 2.5 collective-permute-done
  15.0 2.0 collective-permute-start.2
  16.9 2.6 collective-permute-start.1
  19.5 1.6 pad_maximum_fusion.1
  21.1 3.4 %collective-permute-done.1 = bf16[2,3,64,256]{3,2,1,0:T(8,128)(2,1)S(1)} collective-permute-done((bf16[2,3,64,256]{3,2,1,0:T(8,128)(2,1)S(1)}, bf16[2,3,64,256]{3,2,1,0:T(8,128)(2,1)S(1)}, u32[]{:S(2)}, u32[]{:S(2)}) %collective-permute-start.1) | collective-permute-done | bytes 196640 | tf_op jit(solution)/shard_map/ppermute | solution.py:550
  25.2 1.6 collective-permute-start.3
  26.8 2.9 collective-permute-start.4
  32.2 2.0 collective-permute-done.4
  34.4 2.8 collective-permute-start.7
  37.3 1.4 copy.39.segc_ref
  38.7 8.8 %collective-permute-done.7.rest_1_ = bf16[8,3,64,256]{3,2,1,0:T(8,128)(2,1)S(1)} collective-permute-done((bf16[8,3,64,256]{3,2,1,0:T(8,128)(2,1)S(1)}, bf16[8,3,64,256]{3,2,1,0:T(8,128)(2,1)S(1)}, u32[]{:S(2)}, u32[]{:S(2)}) %collective-permute-start.7) | collective-permute-done | bytes 786464 | tf_op jit(solution)/shard_map/ppermute | solution.py:550
  47.5 1.5 collective-permute-start.11
  49.0 1.5 collective-permute-start.10
  50.8 13.9 %attend.4 = (bf16[2,4,1024,512]{3,2,1,0:T(8,128)(2,1)}, bf16[2,2048,1024]{2,1,0:T(8,128)(2,1)}, bf16[4,1024,512]{2,1,0:T(8,128)(2,1)}, f32[4,4,4,512]{3,2,1,0:T(4,128)}) custom-call(s32[4]{0:T(128)} %dynamic_slice.7.fill_ref, s32[3,16]{1,0:T(4,128)} %concatenate.33.slot_ref, bf16[2048,1024]{1,0:T(8,128)(2,1)} %x_ref.9, s32[4,512,1]{2,1,0:T(8,128)} %copy.39.segc_ref, ...), custom_call_target="tpu_custom_call" | custom-call | flops 15000000512 | bytes 10000000 | tf_op jit(solution)/shard_map/attend/pallas_call | solution.py:403
  65.6 2.3 collective-permute-start.15
  67.9 13.8 %attend.5 = (bf16[2,4,1024,512]{3,2,1,0:T(8,128)(2,1)}, bf16[2,2048,1024]{2,1,0:T(8,128)(2,1)}, bf16[4,1024,512]{2,1,0:T(8,128)(2,1)}, f32[4,4,4,512]{3,2,1,0:T(4,128)}) custom-call(s32[4]{0:T(128)} %dynamic_slice.7.fill_ref, s32[3,16]{1,0:T(4,128)} %concatenate.33.slot_ref, ...), custom_call_target="tpu_custom_call", output_to_operand_aliasing={{0}: (8, {}), {1}: (9, {}), {2}: (10, {}), {3}: (11, {})} | custom-call | flops 15000000512 | bytes 10000000 | tf_op jit(solution)/shard_map/attend/pallas_call | solution.py:403
  82.7 13.8 %attend.6 = (bf16[2,4,1024,512]{3,2,1,0:T(8,128)(2,1)}, bf16[2,2048,1024]{2,1,0:T(8,128)(2,1)}, bf16[4,1024,512]{2,1,0:T(8,128)(2,1)}, f32[4,4,4,512]{3,2,1,0:T(4,128)}) custom-call(s32[4]{0:T(128)} %dynamic_slice.7.fill_ref, s32[3,16]{1,0:T(4,128)} %concatenate.33.slot_ref, ...), custom_call_target="tpu_custom_call", output_to_operand_aliasing={{0}: (8, {}), {1}: (9, {}), {2}: (10, {}), {3}: (11, {})} | custom-call | flops 15000000512 | bytes 10000000 | tf_op jit(solution)/shard_map/attend/pallas_call | solution.py:403
  97.5 1.7 collective-permute-start.16
  99.2 13.8 %attend.7 = (bf16[2,4,1024,512]{3,2,1,0:T(8,128)(2,1)}, bf16[2,2048,1024]{2,1,0:T(8,128)(2,1)}, bf16[4,1024,512]{2,1,0:T(8,128)(2,1)}, f32[4,4,4,512]{3,2,1,0:T(4,128)}) custom-call(s32[4]{0:T(128)} %dynamic_slice.7.fill_ref, s32[3,16]{1,0:T(4,128)} %concatenate.33.slot_ref, ...), custom_call_target="tpu_custom_call", output_to_operand_aliasing={{0}: (8, {}), {1}: (9, {}), {2}: (10, {}), {3}: (11, {})} | custom-call | flops 15000000512 | bytes 10000000 | tf_op jit(solution)/shard_map/attend/pallas_call | solution.py:403
  113.0 1.3 collective-permute-start.19
  115.2 4.7 %all-gather.5.cloned.1.call-done = bf16[2048,2560]{1,0:T(8,128)(2,1)} async-done(((bf16[64,2560]{1,0:T(8,128)(2,1)}), bf16[2048,2560]{1,0:T(8,128)(2,1)}) %all-gather.5.cloned.1.call-update) | async-done | bytes 10485776 | tf_op jit(solution)/shard_map/all_gather | solution.py:636
  120.0 32.0 %feed_front.1 = (f32[2048,1024]{1,0:T(8,128)}, f32[2048,128]{1,0:T(8,128)}, f32[2048,1024]{1,0:T(8,128)}, bf16[2048,2048]{1,0:T(8,128)(2,1)}) custom-call(s32[3,16]{1,0:T(4,128)} %concatenate.33.slot_ref, bf16[2048,1024]{1,0:T(8,128)(2,1)} %x_ref.9, bf16[4,1024,512]{2,1,0:T(8,128)(2,1)} %get-tuple-element.168.ctx_ref, bf16[1024]{0:T(1024)(128)(2,1)} %vec_refs_0_.2, ...), custom_call_target="tpu_custom_call" | custom-call | flops 24999999488 | bytes 30000000 | tf_op jit(solution)/shard_map/feed_front/pallas_call | solution.py:485
  152.6 2.4 collective-permute-done.21.rest_6_
  155.0 1.5 collective-permute-done.22.rest_7_
  157.4 80.4 %feed_back.1 = (bf16[2048,1024]{1,0:T(8,128)(2,1)}, bf16[4,1024,512]{2,1,0:T(8,128)(2,1)}, f32[4,4,4,512]{3,2,1,0:T(4,128)}, bf16[2048,1024]{1,0:T(8,128)(2,1)}, f32[8,1024]{1,0:T(8,128)}) custom-call(s32[3,16]{1,0:T(4,128)} %concatenate.33.slot_ref, f32[2048,1024]{1,0:T(8,128)} %get-tuple-element.178.normal_ref, f32[2048,128]{1,0:T(8,128)} %get-tuple-element.179.inv_ref, ...), custom_call_target="tpu_custom_call" | custom-call | flops 74999996416 | bytes 40000000 | tf_op jit(solution)/shard_map/feed_back/pallas_call | solution.py:505
  237.9 63.9 %attend_back.1 = (bf16[2048,1024]{1,0:T(8,128)(2,1)}, f32[2,1024]{1,0:T(2,128)}) custom-call(s32[4]{0:T(128)} %dynamic_slice.7.fill_ref, s32[3,16]{1,0:T(4,128)} %concatenate.33.slot_ref, bf16[2,4,1024,512]{3,2,1,0:T(8,128)(2,1)} %get-tuple-element.187.qk_ref, bf16[2,2048,1024]{2,1,0:T(8,128)(2,1)} %get-tuple-element.188.kv_ref, ...), custom_call_target="tpu_custom_call" | custom-call | flops 49999998976 | bytes 30000000 | tf_op jit(solution)/shard_map/attend_back/pallas_call | solution.py:440
  303.9 1.3 collective-permute-start.26
  306.1 1.3 collective-permute-start.24
  307.4 1.3 bitcast_reduce_fusion
  309.8 1.9 collective-permute-start.29
  311.6 2.6 collective-permute-start.27
  (102 shorter events, 17.5 us)
Async XLA Ops:
  7.2 112.8 %all-gather.5.cloned.1.call-start = ((), (), s32[]{:S(2)}) async-start(), calls=%async_computation | async-start | bytes 10813440 | tf_op jit(solution)/shard_map/all_gather | solution.py:636
  8.2 6.7 %collective-permute-start = (bf16[1,3,64,256]{3,2,1,0:T(8,128)(2,1)S(1)}, bf16[1,3,64,256]{3,2,1,0:T(8,128)(2,1)S(1)}, u32[]{:S(2)}, u32[]{:S(2)}) collective-permute-start(bf16[1,3,64,256]{3,2,1,0:T(8,128)(2,1)S(1)} %get-tuple-element.213), channel_id=1, source_target_pairs={{0,8},{1,17},{2,10},{3,19},{4,12},{5,21},{6,14},{7,23},{8,0},{9,25... | collective-permute-start | bytes 294920 | tf_op jit(solution)/shard_map/ppermute | solution.py:550
  15.0 6.1 %collective-permute-start.2 = (bf16[1,3,64,256]{3,2,1,0:T(8,128)(2,1)S(1)}, bf16[1,3,64,256]{3,2,1,0:T(8,128)(2,1)S(1)}, u32[]{:S(2)}, u32[]{:S(2)}) collective-permute-start(bf16[1,3,64,256]{3,2,1,0:T(8,128)(2,1)S(1)} %get-tuple-element.112), channel_id=1, source_target_pairs={{0,8},{1,17},{2,10},{3,19},{4,12},{5,21},{6,14},{7,23},{8,0},{9,25... | collective-permute-start | bytes 294920 | tf_op jit(solution)/shard_map/ppermute | solution.py:550
  16.9 7.5 %collective-permute-start.1 = (bf16[2,3,64,256]{3,2,1,0:T(8,128)(2,1)S(1)}, bf16[2,3,64,256]{3,2,1,0:T(8,128)(2,1)S(1)}, u32[]{:S(2)}, u32[]{:S(2)}) collective-permute-start(bf16[2,3,64,256]{3,2,1,0:T(8,128)(2,1)S(1)} %pad_maximum_fusion.2), channel_id=1, source_target_pairs={{0,16},{1,9},{2,18},{3,11},{4,20},{5,13},{6,22},{7,15},{8,24},{9,1... | collective-permute-start | bytes 589832 | tf_op jit(solution)/shard_map/ppermute | solution.py:550
  24.5 283.0 %all-gather.7.cloned.1.call-start = ((), (), s32[]{:S(2)}) async-start(), calls=%async_computation.1 | async-start | bytes 1081344 | tf_op jit(solution)/shard_map/all_gather | solution.py:701
  24.5 7.7 %collective-permute-start.5 = (bf16[2,512]{1,0:T(2,128)(2,1)}, bf16[2,512]{1,0:T(2,128)(2,1)S(1)}, u32[]{:S(2)}, u32[]{:S(2)}) collective-permute-start(bf16[2,512]{1,0:T(2,128)(2,1)} %b_ref.1), channel_id=1, source_target_pairs={{0,1},{1,0},{2,3},{3,2},{4,5},{5,4},{6,7},{7,6},{8,9},{9,8},{10,11... | collective-permute-start | bytes 6152 | tf_op jit(solution)/shard_map/ppermute | solution.py:558
  24.7 7.5 %collective-permute-start.6 = (bf16[2048]{0:T(1024)(128)(2,1)}, bf16[2048]{0:T(1024)(128)(2,1)S(1)}, u32[]{:S(2)}, u32[]{:S(2)}) collective-permute-start(bf16[2048]{0:T(1024)(128)(2,1)} %bi_refs_0_.1), channel_id=1, source_target_pairs={{0,1},{1,0},{2,3},{3,2},{4,5},{5,4},{6,7},{7,6},{8,9},{9,8},{10,11... | collective-permute-start | bytes 12296 | tf_op jit(solution)/shard_map/ppermute | solution.py:558
  25.2 9.1 %collective-permute-start.3 = (bf16[4,3,64,256]{3,2,1,0:T(8,128)(2,1)S(1)}, bf16[4,3,64,256]{3,2,1,0:T(8,128)(2,1)S(1)}, u32[]{:S(2)}, u32[]{:S(2)}) collective-permute-start(bf16[4,3,64,256]{3,2,1,0:T(8,128)(2,1)S(1)} %constant_dynamic-update-slice_fusion), channel_id=1, source_target_pairs={{0,4},{1,3},{2,6},{3,1},{4,0},{5,7},{6,2},{7,5},{8,12},{9,11},{10,... | collective-permute-start | bytes 1179656 | tf_op jit(solution)/shard_map/ppermute | solution.py:550
  26.8 7.5 %collective-permute-start.4 = (bf16[2,3,64,256]{3,2,1,0:T(8,128)(2,1)S(1)}, bf16[2,3,64,256]{3,2,1,0:T(8,128)(2,1)S(1)}, u32[]{:S(2)}, u32[]{:S(2)}) collective-permute-start(bf16[2,3,64,256]{3,2,1,0:T(8,128)(2,1)S(1)} %constant_dynamic-update-slice_fusion.2), channel_id=1, source_target_pairs={{0,16},{1,9},{2,18},{3,11},{4,20},{5,13},{6,22},{7,15},{8,24},{9,1... | collective-permute-start | bytes 589832 | tf_op jit(solution)/shard_map/ppermute | solution.py:550
  34.3 4.3 %collective-permute-start.8 = (bf16[8,3,64,256]{3,2,1,0:T(8,128)(2,1)S(1)}, bf16[8,3,64,256]{3,2,1,0:T(8,128)(2,1)S(1)}, u32[]{:S(2)}, u32[]{:S(2)}) collective-permute-start(bf16[8,3,64,256]{3,2,1,0:T(8,128)(2,1)S(1)} %constant_dynamic-update-slice_fusion.4.rest_0_), channel_id=1, source_target_pairs={{0,1},{1,0},{2,3},{3,2},{4,5},{5,4},{6,7},{7,6},{8,9},{9,8},{10,11... | collective-permute-start | bytes 2359304 | tf_op jit(solution)/shard_map/ppermute | solution.py:558
  34.4 13.1 %collective-permute-start.7 = (bf16[8,3,64,256]{3,2,1,0:T(8,128)(2,1)S(1)}, bf16[8,3,64,256]{3,2,1,0:T(8,128)(2,1)S(1)}, u32[]{:S(2)}, u32[]{:S(2)}) collective-permute-start(bf16[8,3,64,256]{3,2,1,0:T(8,128)(2,1)S(1)} %constant_dynamic-update-slice_fusion.4.rest_0_), channel_id=1, source_target_pairs={{0,2},{1,5},{2,0},{3,7},{4,6},{5,1},{6,4},{7,3},{8,10},{9,13},{10,... | collective-permute-start | bytes 2359304 | tf_op jit(solution)/shard_map/ppermute | solution.py:550
  47.5 17.3 %collective-permute-start.11 = (bf16[1,64,2048]{2,1,0:T(8,128)(2,1)S(1)}, bf16[1,64,2048]{2,1,0:T(8,128)(2,1)S(1)}, u32[]{:S(2)}, u32[]{:S(2)}) collective-permute-start(bf16[1,64,2048]{2,1,0:T(8,128)(2,1)S(1)} %maximum_bitcast_fusion), channel_id=1, source_target_pairs={{0,8},{1,17},{2,10},{3,19},{4,12},{5,21},{6,14},{7,23},{8,0},{9,25... | collective-permute-start | bytes 786440 | tf_op jit(solution)/shard_map/ppermute | solution.py:550
  49.0 15.8 %collective-permute-start.10 = (bf16[4,3,64,256]{3,2,1,0:T(8,128)(2,1)S(1)}, bf16[4,3,64,256]{3,2,1,0:T(8,128)(2,1)S(1)}, u32[]{:S(2)}, u32[]{:S(2)}) collective-permute-start(bf16[4,3,64,256]{3,2,1,0:T(8,128)(2,1)S(1)} %pad_maximum_fusion), channel_id=1, source_target_pairs={{0,4},{1,3},{2,6},{3,1},{4,0},{5,7},{6,2},{7,5},{8,12},{9,11},{10,... | collective-permute-start | bytes 1179656 | tf_op jit(solution)/shard_map/ppermute | solution.py:550
  50.5 14.3 %collective-permute-start.9 = (bf16[8,3,64,256]{3,2,1,0:T(8,128)(2,1)S(1)}, bf16[8,3,64,256]{3,2,1,0:T(8,128)(2,1)}, u32[]{:S(2)}, u32[]{:S(2)}) collective-permute-start(bf16[8,3,64,256]{3,2,1,0:T(8,128)(2,1)S(1)} %collective-permute-done.7.rest_1_), channel_id=1, source_target_pairs={{0,1},{1,0},{2,3},{3,2},{4,5},{5,4},{6,7},{7,6},{8,9},{9,8},{10,11... | collective-permute-start | bytes 2359304 | tf_op jit(solution)/shard_map/ppermute | solution.py:558
  64.9 16.9 %collective-permute-start.13 = (bf16[8,3,64,256]{3,2,1,0:T(8,128)(2,1)S(1)}, bf16[8,3,64,256]{3,2,1,0:T(8,128)(2,1)S(1)}, u32[]{:S(2)}, u32[]{:S(2)}) collective-permute-start(bf16[8,3,64,256]{3,2,1,0:T(8,128)(2,1)S(1)} %constant_dynamic-update-slice_fusion.6.rest_0_.rest_4_), channel_id=1, source_target_pairs={{0,2},{1,5},{2,0},{3,7},{4,6},{5,1},{6,4},{7,3},{8,10},{9,13},{10,... | collective-permute-start | bytes 2359304 | tf_op jit(solution)/shard_map/ppermute | solution.py:550
  65.6 16.2 %collective-permute-start.12 = (bf16[8,3,64,256]{3,2,1,0:T(8,128)(2,1)S(1)}, bf16[8,3,64,256]{3,2,1,0:T(8,128)(2,1)}, u32[]{:S(2)}, u32[]{:S(2)}) collective-permute-start(bf16[8,3,64,256]{3,2,1,0:T(8,128)(2,1)S(1)} %constant_dynamic-update-slice_fusion.6.rest_0_.rest_4_), channel_id=1, source_target_pairs={{0,1},{1,0},{2,3},{3,2},{4,5},{5,4},{6,7},{7,6},{8,9},{9,8},{10,11... | collective-permute-start | bytes 2359304 | tf_op jit(solution)/shard_map/ppermute | solution.py:558
  65.6 30.9 %collective-permute-start.15 = (bf16[2,64,2048]{2,1,0:T(8,128)(2,1)S(1)}, bf16[2,64,2048]{2,1,0:T(8,128)(2,1)S(1)}, u32[]{:S(2)}, u32[]{:S(2)}) collective-permute-start(bf16[2,64,2048]{2,1,0:T(8,128)(2,1)S(1)} %constant_dynamic-update-slice_fusion.8), channel_id=1, source_target_pairs={{0,16},{1,9},{2,18},{3,11},{4,20},{5,13},{6,22},{7,15},{8,24},{9,1... | collective-permute-start | bytes 1572872 | tf_op jit(solution)/shard_map/ppermute | solution.py:550
  81.8 14.7 %collective-permute-start.14 = (bf16[8,3,64,256]{3,2,1,0:T(8,128)(2,1)S(1)}, bf16[8,3,64,256]{3,2,1,0:T(8,128)(2,1)S(1)}, u32[]{:S(2)}, u32[]{:S(2)}) collective-permute-start(bf16[8,3,64,256]{3,2,1,0:T(8,128)(2,1)S(1)} %collective-permute-done.13.rest_1_.rest_5_), channel_id=1, source_target_pairs={{0,1},{1,0},{2,3},{3,2},{4,5},{5,4},{6,7},{7,6},{8,9},{9,8},{10,11... | collective-permute-start | bytes 2359304 | tf_op jit(solution)/shard_map/ppermute | solution.py:558
  97.5 15.5 %collective-permute-start.16 = (bf16[4,64,2048]{2,1,0:T(8,128)(2,1)S(1)}, bf16[4,64,2048]{2,1,0:T(8,128)(2,1)S(1)}, u32[]{:S(2)}, u32[]{:S(2)}) collective-permute-start(bf16[4,64,2048]{2,1,0:T(8,128)(2,1)S(1)} %constant_dynamic-update-slice_fusion.10.rest_0_), channel_id=1, source_target_pairs={{0,4},{1,3},{2,6},{3,1},{4,0},{5,7},{6,2},{7,5},{8,12},{9,11},{10,... | collective-permute-start | bytes 3145736 | tf_op jit(solution)/shard_map/ppermute | solution.py:550
  113.0 39.0 %collective-permute-start.19 = (bf16[4,64,2048]{2,1,0:T(8,128)(2,1)S(1)}, bf16[4,64,2048]{2,1,0:T(8,128)(2,1)}, u32[]{:S(2)}, u32[]{:S(2)}) collective-permute-start(bf16[4,64,2048]{2,1,0:T(8,128)(2,1)S(1)} %constant_dynamic-update-slice_fusion.10.rest_0_), channel_id=1, source_target_pairs={{0,2},{1,5},{2,0},{3,7},{4,6},{5,1},{6,4},{7,3},{8,10},{9,13},{10,... | collective-permute-start | bytes 3145736 | tf_op jit(solution)/shard_map/ppermute | solution.py:550
  114.4 37.6 %collective-permute-start.17 = (bf16[4,64,2048]{2,1,0:T(8,128)(2,1)S(1)}, bf16[4,64,2048]{2,1,0:T(8,128)(2,1)}, u32[]{:S(2)}, u32[]{:S(2)}) collective-permute-start(bf16[4,64,2048]{2,1,0:T(8,128)(2,1)S(1)} %constant_dynamic-update-slice_fusion.10.rest_0_), channel_id=1, source_target_pairs={{0,1},{1,0},{2,3},{3,2},{4,5},{5,4},{6,7},{7,6},{8,9},{9,8},{10,11... | collective-permute-start | bytes 3145736 | tf_op jit(solution)/shard_map/ppermute | solution.py:558
  114.4 37.6 %collective-permute-start.20 = (bf16[4,64,2048]{2,1,0:T(8,128)(2,1)S(1)}, bf16[4,64,2048]{2,1,0:T(8,128)(2,1)}, u32[]{:S(2)}, u32[]{:S(2)}) collective-permute-start(bf16[4,64,2048]{2,1,0:T(8,128)(2,1)S(1)} %collective-permute-done.16.rest_1_), channel_id=1, source_target_pairs={{0,2},{1,5},{2,0},{3,7},{4,6},{5,1},{6,4},{7,3},{8,10},{9,13},{10,... | collective-permute-start | bytes 3145736 | tf_op jit(solution)/shard_map/ppermute | solution.py:550
  115.1 36.9 %collective-permute-start.18 = (bf16[4,64,2048]{2,1,0:T(8,128)(2,1)S(1)}, bf16[4,64,2048]{2,1,0:T(8,128)(2,1)}, u32[]{:S(2)}, u32[]{:S(2)}) collective-permute-start(bf16[4,64,2048]{2,1,0:T(8,128)(2,1)S(1)} %collective-permute-done.16.rest_1_), channel_id=1, source_target_pairs={{0,1},{1,0},{2,3},{3,2},{4,5},{5,4},{6,7},{7,6},{8,9},{9,8},{10,11... | collective-permute-start | bytes 3145736 | tf_op jit(solution)/shard_map/ppermute | solution.py:558
  152.0 2.9 collective-permute-start.21
  152.3 4.1 %collective-permute-start.22 = (bf16[4,64,2048]{2,1,0:T(8,128)(2,1)}, bf16[4,64,2048]{2,1,0:T(8,128)(2,1)S(1)}, u32[]{:S(2)}, u32[]{:S(2)}) collective-permute-start(bf16[4,64,2048]{2,1,0:T(8,128)(2,1)} %collective-permute-done.20.rest_3_), channel_id=1, source_target_pairs={{0,1},{1,0},{2,3},{3,2},{4,5},{5,4},{6,7},{7,6},{8,9},{9,8},{10,11... | collective-permute-start | bytes 3145736 | tf_op jit(solution)/shard_map/ppermute | solution.py:558
  301.8 1.4 collective-permute-start.23
  303.9 4.8 %collective-permute-start.26 = (f32[2,1024]{1,0:T(2,128)S(1)}, f32[2,1024]{1,0:T(2,128)S(1)}, u32[]{:S(2)}, u32[]{:S(2)}) collective-permute-start(f32[2,1024]{1,0:T(2,128)S(1)} %add.94), channel_id=1, source_target_pairs={{0,6},{2,4},{4,2},{6,0},{8,14},{10,12},{12,10},{14,8},{16,22},{18,... | collective-permute-start | bytes 24584 | tf_op jit(solution)/shard_map/ppermute | solution.py:583
  305.3 3.7 %collective-permute-start.25 = (f32[2,1024]{1,0:T(2,128)S(1)}, f32[2,1024]{1,0:T(2,128)S(1)}, u32[]{:S(2)}, u32[]{:S(2)}) collective-permute-start(f32[2,1024]{1,0:T(2,128)S(1)} %add.94), channel_id=1, source_target_pairs={{0,4},{2,6},{4,0},{6,2},{8,12},{10,14},{12,8},{14,10},{16,20},{18,... | collective-permute-start | bytes 24584 | tf_op jit(solution)/shard_map/ppermute | solution.py:583
  306.1 3.7 %collective-permute-start.24 = (f32[2,1024]{1,0:T(2,128)S(1)}, f32[2,1024]{1,0:T(2,128)S(1)}, u32[]{:S(2)}, u32[]{:S(2)}) collective-permute-start(f32[2,1024]{1,0:T(2,128)S(1)} %add.94), channel_id=1, source_target_pairs={{0,2},{2,0},{4,6},{6,4},{8,10},{10,8},{12,14},{14,12},{16,18},{18,... | collective-permute-start | bytes 24584 | tf_op jit(solution)/shard_map/ppermute | solution.py:583
  309.8 5.7 %collective-permute-start.29 = (f32[2,1024]{1,0:T(2,128)S(1)}, f32[2,1024]{1,0:T(2,128)S(1)}, u32[]{:S(2)}, u32[]{:S(2)}) collective-permute-start(f32[2,1024]{1,0:T(2,128)S(1)} %add_add_fusion.1), channel_id=1, source_target_pairs={{0,24},{2,26},{4,28},{6,30},{8,16},{10,18},{12,20},{14,22},{16,8},... | collective-permute-start | bytes 24584 | tf_op jit(solution)/shard_map/ppermute | solution.py:583
  311.6 4.5 %collective-permute-start.28 = (f32[2,1024]{1,0:T(2,128)S(1)}, f32[2,1024]{1,0:T(2,128)S(1)}, u32[]{:S(2)}, u32[]{:S(2)}) collective-permute-start(f32[2,1024]{1,0:T(2,128)S(1)} %add_add_fusion.1), channel_id=1, source_target_pairs={{0,16},{2,18},{4,20},{6,22},{8,24},{10,26},{12,28},{14,30},{16,0},... | collective-permute-start | bytes 24584 | tf_op jit(solution)/shard_map/ppermute | solution.py:583
  311.6 4.5 %collective-permute-start.27 = (f32[2,1024]{1,0:T(2,128)S(1)}, f32[2,1024]{1,0:T(2,128)S(1)}, u32[]{:S(2)}, u32[]{:S(2)}) collective-permute-start(f32[2,1024]{1,0:T(2,128)S(1)} %add_add_fusion.1), channel_id=1, source_target_pairs={{0,8},{2,10},{4,12},{6,14},{8,0},{10,2},{12,4},{14,6},{16,24},{18,... | collective-permute-start | bytes 24584 | tf_op jit(solution)/shard_map/ppermute | solution.py:583
  (14 other events, 284.8 us)
Sparse Core Ops, SparseCore 0:
  24.6 95.3 all-gather.4
  238.0 51.7 all-gather.6

commit v8 on v7

--- a/solution.py
+++ b/solution.py
@@ -116,13 +116,24 @@
 
 def attend_kernel(step, count, fill_ref, slot_ref, x_ref, segc_ref, segr_ref, b_ref, *rest):
     other, half = step % 2, step // 2
-    qk_ref, kv_ref, ctx_ref, lse_ref, w_ref, sem = rest[-6:]
+    qk_ref, kv_ref, ctx_ref, lse_ref, w_ref, sem, block_ref, block_sem = rest[-8:]
+    row = pl.program_id(0)
+
+    def block_copy(r):
+        return pltpu.make_async_copy(x_ref.at[pl.ds(r * SLOTS, SLOTS)], block_ref.at[r % 2], block_sem.at[r % 2])
 
     @pl.when(pl.program_id(0) == 0)
     def _():
+        block_copy(row).start()
         wait_all(fetch(rest[:count], w_ref, sem))
 
-    x = x_ref[...]
+    block_copy(row).wait()
+
+    @pl.when(row + 1 < pl.num_programs(0))
+    def _():
+        block_copy(row + 1).start()
+
+    x = block_ref[row % 2]
     weight = [set_weight(w_ref, slot_ref, other, i) for i in range(3)]
     columns = slice(half * WIDE, (half + 1) * WIDE)
     biases = wide(b_ref[...])[:, columns]
@@ -406,7 +417,7 @@
         in_specs=[
             SCALARS,
             SCALARS,
-            pl.BlockSpec((SLOTS, D), lambda r: (r, 0)),
+            ANYWHERE,
             pl.BlockSpec((1, SLOTS, 1), lambda r: (r, 0, 0)),
             pl.BlockSpec((1, 1, SLOTS), lambda r: (r, 0, 0)),
             whole(bias),
@@ -427,6 +438,8 @@
         scratch_shapes=[
             pltpu.VMEM((sum(w.shape[0] for w in pieces),) + pieces[0].shape[1:], jnp.bfloat16),
             pltpu.SemaphoreType.DMA((len(pieces),)),
+            pltpu.VMEM((2, SLOTS, D), jnp.bfloat16),
+            pltpu.SemaphoreType.DMA((2,)),
         ],
         input_output_aliases={6 + len(pieces) + i: i for i in range(len(earlier))},
         compiler_params=params(1),

time: 324 us -> 324 us (level)
  no operation moved by 1% of the time
where the time goes in v8:
time: 324 us
  Pallas kernels  231 us (71%)
  starting transfers between devices  34.6 us (11%)
  waiting for transfers between devices  29.3 us (9%)
  between operations  14.5 us (4%)
  local copies, waits for them, and re-layouts  10.1 us (3%)
  other arithmetic  4.3 us (1%)
    pallas_call x1, Pallas kernels, feed_back(): pl.pallas_call(partial(back_kernel, len(late)), grid=(count // TILE,), in...  80.4 us
    pallas_call x1, Pallas kernels, attend_back(): pl.pallas_call(partial(attend_back_kernel, len(weights)), grid=(rows, GRO...  63.9 us
    pallas_call x4, Pallas kernels, attend(): pl.pallas_call(partial(attend_kernel, step, len(pieces)), grid=(rows,), i...  54.8 us
    pallas_call x1, Pallas kernels, feed_front(): pl.pallas_call(front_kernel, grid=(count // FRONT_TILE,), in_specs=[SCALA...  32 us
    ppermute x13, starting transfers between devices, partner(): return lax.ppermute(block, ('rows', 'tp'), pairs)  24.3 us
    ppermute x13, waiting for transfers between devices, partner(): return lax.ppermute(block, ('rows', 'tp'), pairs)  17.6 us
    ppermute x6, starting transfers between devices, got(): return lax.ppermute(values, 'rows', [(i, i ^ distance) for i in range(n)])  7.94 us
  transfers between devices with their start and end apart: 32, of which 11 were waited for; matrix products, arithmetic and copies ran while one was open for 3% of the time, Pallas kernels for 47%

profile of v8, /device:TPU:0, one launch (start us, length us, event | category | flops | bytes accessed | tf_op | source)
XLA Modules:
  0.0 323.9 jit_solution(17659082848175405606)
XLA Ops:
  8.2 3.1 collective-permute-start
  12.4 2.5 collective-permute-done
  15.0 2.0 collective-permute-start.2
  16.9 2.6 collective-permute-start.1
  19.5 1.6 pad_maximum_fusion.1
  21.1 3.4 %collective-permute-done.1 = bf16[2,3,64,256]{3,2,1,0:T(8,128)(2,1)S(1)} collective-permute-done((bf16[2,3,64,256]{3,2,1,0:T(8,128)(2,1)S(1)}, bf16[2,3,64,256]{3,2,1,0:T(8,128)(2,1)S(1)}, u32[]{:S(2)}, u32[]{:S(2)}) %collective-permute-start.1) | collective-permute-done | bytes 196640 | tf_op jit(solution)/shard_map/ppermute | solution.py:563
  25.2 1.6 collective-permute-start.3
  26.8 2.9 collective-permute-start.4
  29.8 1.2 dynamic_slice.7.fill_ref
  32.2 2.0 collective-permute-done.4
  34.4 2.8 collective-permute-start.7
  37.3 1.4 copy.39.segc_ref
  38.7 8.8 %collective-permute-done.7.rest_1_ = bf16[8,3,64,256]{3,2,1,0:T(8,128)(2,1)S(1)} collective-permute-done((bf16[8,3,64,256]{3,2,1,0:T(8,128)(2,1)S(1)}, bf16[8,3,64,256]{3,2,1,0:T(8,128)(2,1)S(1)}, u32[]{:S(2)}, u32[]{:S(2)}) %collective-permute-start.7) | collective-permute-done | bytes 786464 | tf_op jit(solution)/shard_map/ppermute | solution.py:563
  47.5 1.5 collective-permute-start.11
  49.0 1.5 collective-permute-start.10
  50.8 13.9 %attend.4 = (bf16[2,4,1024,512]{3,2,1,0:T(8,128)(2,1)}, bf16[2,2048,1024]{2,1,0:T(8,128)(2,1)}, bf16[4,1024,512]{2,1,0:T(8,128)(2,1)}, f32[4,4,4,512]{3,2,1,0:T(4,128)}) custom-call(s32[4]{0:T(128)} %dynamic_slice.7.fill_ref, s32[3,16]{1,0:T(4,128)} %concatenate.33.slot_ref, bf16[2048,1024]{1,0:T(8,128)(2,1)} %x_ref.9, s32[4,512,1]{2,1,0:T(8,128)} %copy.39.segc_ref, ...), custom_call_target="tpu_custom_call" | custom-call | flops 15000000512 | bytes 10000000 | tf_op jit(solution)/shard_map/attend/pallas_call | solution.py:414
  65.4 2.3 collective-permute-start.15
  67.7 13.6 %attend.5 = (bf16[2,4,1024,512]{3,2,1,0:T(8,128)(2,1)}, bf16[2,2048,1024]{2,1,0:T(8,128)(2,1)}, bf16[4,1024,512]{2,1,0:T(8,128)(2,1)}, f32[4,4,4,512]{3,2,1,0:T(4,128)}) custom-call(s32[4]{0:T(128)} %dynamic_slice.7.fill_ref, s32[3,16]{1,0:T(4,128)} %concatenate.33.slot_ref, ...), custom_call_target="tpu_custom_call", output_to_operand_aliasing={{0}: (8, {}), {1}: (9, {}), {2}: (10, {}), {3}: (11, {})} | custom-call | flops 15000000512 | bytes 10000000 | tf_op jit(solution)/shard_map/attend/pallas_call | solution.py:414
  82.3 13.7 %attend.6 = (bf16[2,4,1024,512]{3,2,1,0:T(8,128)(2,1)}, bf16[2,2048,1024]{2,1,0:T(8,128)(2,1)}, bf16[4,1024,512]{2,1,0:T(8,128)(2,1)}, f32[4,4,4,512]{3,2,1,0:T(4,128)}) custom-call(s32[4]{0:T(128)} %dynamic_slice.7.fill_ref, s32[3,16]{1,0:T(4,128)} %concatenate.33.slot_ref, ...), custom_call_target="tpu_custom_call", output_to_operand_aliasing={{0}: (8, {}), {1}: (9, {}), {2}: (10, {}), {3}: (11, {})} | custom-call | flops 15000000512 | bytes 10000000 | tf_op jit(solution)/shard_map/attend/pallas_call | solution.py:414
  97.0 1.6 collective-permute-start.16
  98.5 13.6 %attend.7 = (bf16[2,4,1024,512]{3,2,1,0:T(8,128)(2,1)}, bf16[2,2048,1024]{2,1,0:T(8,128)(2,1)}, bf16[4,1024,512]{2,1,0:T(8,128)(2,1)}, f32[4,4,4,512]{3,2,1,0:T(4,128)}) custom-call(s32[4]{0:T(128)} %dynamic_slice.7.fill_ref, s32[3,16]{1,0:T(4,128)} %concatenate.33.slot_ref, ...), custom_call_target="tpu_custom_call", output_to_operand_aliasing={{0}: (8, {}), {1}: (9, {}), {2}: (10, {}), {3}: (11, {})} | custom-call | flops 15000000512 | bytes 10000000 | tf_op jit(solution)/shard_map/attend/pallas_call | solution.py:414
  113.0 1.5 collective-permute-start.19
  115.3 5.0 %all-gather.5.cloned.1.call-done = bf16[2048,2560]{1,0:T(8,128)(2,1)} async-done(((bf16[64,2560]{1,0:T(8,128)(2,1)}), bf16[2048,2560]{1,0:T(8,128)(2,1)}) %all-gather.5.cloned.1.call-update) | async-done | bytes 10485776 | tf_op jit(solution)/shard_map/all_gather | solution.py:649
  120.3 32.0 %feed_front.1 = (f32[2048,1024]{1,0:T(8,128)}, f32[2048,128]{1,0:T(8,128)}, f32[2048,1024]{1,0:T(8,128)}, bf16[2048,2048]{1,0:T(8,128)(2,1)}) custom-call(s32[3,16]{1,0:T(4,128)} %concatenate.33.slot_ref, bf16[2048,1024]{1,0:T(8,128)(2,1)} %x_ref.9, bf16[4,1024,512]{2,1,0:T(8,128)(2,1)} %get-tuple-element.168.ctx_ref, bf16[1024]{0:T(1024)(128)(2,1)} %vec_refs_0_.2, ...), custom_call_target="tpu_custom_call" | custom-call | flops 24999999488 | bytes 30000000 | tf_op jit(solution)/shard_map/feed_front/pallas_call | solution.py:498
  153.0 2.4 collective-permute-done.21.rest_6_
  155.3 1.5 collective-permute-done.22.rest_7_
  157.8 80.4 %feed_back.1 = (bf16[2048,1024]{1,0:T(8,128)(2,1)}, bf16[4,1024,512]{2,1,0:T(8,128)(2,1)}, f32[4,4,4,512]{3,2,1,0:T(4,128)}, bf16[2048,1024]{1,0:T(8,128)(2,1)}, f32[8,1024]{1,0:T(8,128)}) custom-call(s32[3,16]{1,0:T(4,128)} %concatenate.33.slot_ref, f32[2048,1024]{1,0:T(8,128)} %get-tuple-element.178.normal_ref, f32[2048,128]{1,0:T(8,128)} %get-tuple-element.179.inv_ref, ...), custom_call_target="tpu_custom_call" | custom-call | flops 74999996416 | bytes 40000000 | tf_op jit(solution)/shard_map/feed_back/pallas_call | solution.py:518
  238.3 63.9 %attend_back.1 = (bf16[2048,1024]{1,0:T(8,128)(2,1)}, f32[2,1024]{1,0:T(2,128)}) custom-call(s32[4]{0:T(128)} %dynamic_slice.7.fill_ref, s32[3,16]{1,0:T(4,128)} %concatenate.33.slot_ref, bf16[2,4,1024,512]{3,2,1,0:T(8,128)(2,1)} %get-tuple-element.187.qk_ref, bf16[2,2048,1024]{2,1,0:T(8,128)(2,1)} %get-tuple-element.188.kv_ref, ...), custom_call_target="tpu_custom_call" | custom-call | flops 49999998976 | bytes 30000000 | tf_op jit(solution)/shard_map/attend_back/pallas_call | solution.py:453
  306.4 1.4 collective-permute-start.24
  307.8 1.3 bitcast_reduce_fusion
  310.0 1.9 collective-permute-start.29
  312.3 2.2 collective-permute-start.27
  (102 shorter events, 18.4 us)
Async XLA Ops:
  7.2 113.1 %all-gather.5.cloned.1.call-start = ((), (), s32[]{:S(2)}) async-start(), calls=%async_computation | async-start | bytes 10813440 | tf_op jit(solution)/shard_map/all_gather | solution.py:649
  8.2 6.7 %collective-permute-start = (bf16[1,3,64,256]{3,2,1,0:T(8,128)(2,1)S(1)}, bf16[1,3,64,256]{3,2,1,0:T(8,128)(2,1)S(1)}, u32[]{:S(2)}, u32[]{:S(2)}) collective-permute-start(bf16[1,3,64,256]{3,2,1,0:T(8,128)(2,1)S(1)} %get-tuple-element.213), channel_id=1, source_target_pairs={{0,8},{1,17},{2,10},{3,19},{4,12},{5,21},{6,14},{7,23},{8,0},{9,25... | collective-permute-start | bytes 294920 | tf_op jit(solution)/shard_map/ppermute | solution.py:563
  15.0 6.1 %collective-permute-start.2 = (bf16[1,3,64,256]{3,2,1,0:T(8,128)(2,1)S(1)}, bf16[1,3,64,256]{3,2,1,0:T(8,128)(2,1)S(1)}, u32[]{:S(2)}, u32[]{:S(2)}) collective-permute-start(bf16[1,3,64,256]{3,2,1,0:T(8,128)(2,1)S(1)} %get-tuple-element.112), channel_id=1, source_target_pairs={{0,8},{1,17},{2,10},{3,19},{4,12},{5,21},{6,14},{7,23},{8,0},{9,25... | collective-permute-start | bytes 294920 | tf_op jit(solution)/shard_map/ppermute | solution.py:563
  16.9 7.5 %collective-permute-start.1 = (bf16[2,3,64,256]{3,2,1,0:T(8,128)(2,1)S(1)}, bf16[2,3,64,256]{3,2,1,0:T(8,128)(2,1)S(1)}, u32[]{:S(2)}, u32[]{:S(2)}) collective-permute-start(bf16[2,3,64,256]{3,2,1,0:T(8,128)(2,1)S(1)} %pad_maximum_fusion.2), channel_id=1, source_target_pairs={{0,16},{1,9},{2,18},{3,11},{4,20},{5,13},{6,22},{7,15},{8,24},{9,1... | collective-permute-start | bytes 589832 | tf_op jit(solution)/shard_map/ppermute | solution.py:563
  24.5 283.3 %all-gather.7.cloned.1.call-start = ((), (), s32[]{:S(2)}) async-start(), calls=%async_computation.1 | async-start | bytes 1081344 | tf_op jit(solution)/shard_map/all_gather | solution.py:714
  24.5 7.7 %collective-permute-start.5 = (bf16[2,512]{1,0:T(2,128)(2,1)}, bf16[2,512]{1,0:T(2,128)(2,1)S(1)}, u32[]{:S(2)}, u32[]{:S(2)}) collective-permute-start(bf16[2,512]{1,0:T(2,128)(2,1)} %b_ref.1), channel_id=1, source_target_pairs={{0,1},{1,0},{2,3},{3,2},{4,5},{5,4},{6,7},{7,6},{8,9},{9,8},{10,11... | collective-permute-start | bytes 6152 | tf_op jit(solution)/shard_map/ppermute | solution.py:571
  24.7 7.5 %collective-permute-start.6 = (bf16[2048]{0:T(1024)(128)(2,1)}, bf16[2048]{0:T(1024)(128)(2,1)S(1)}, u32[]{:S(2)}, u32[]{:S(2)}) collective-permute-start(bf16[2048]{0:T(1024)(128)(2,1)} %bi_refs_0_.1), channel_id=1, source_target_pairs={{0,1},{1,0},{2,3},{3,2},{4,5},{5,4},{6,7},{7,6},{8,9},{9,8},{10,11... | collective-permute-start | bytes 12296 | tf_op jit(solution)/shard_map/ppermute | solution.py:571
  25.2 9.1 %collective-permute-start.3 = (bf16[4,3,64,256]{3,2,1,0:T(8,128)(2,1)S(1)}, bf16[4,3,64,256]{3,2,1,0:T(8,128)(2,1)S(1)}, u32[]{:S(2)}, u32[]{:S(2)}) collective-permute-start(bf16[4,3,64,256]{3,2,1,0:T(8,128)(2,1)S(1)} %constant_dynamic-update-slice_fusion), channel_id=1, source_target_pairs={{0,4},{1,3},{2,6},{3,1},{4,0},{5,7},{6,2},{7,5},{8,12},{9,11},{10,... | collective-permute-start | bytes 1179656 | tf_op jit(solution)/shard_map/ppermute | solution.py:563
  26.8 7.5 %collective-permute-start.4 = (bf16[2,3,64,256]{3,2,1,0:T(8,128)(2,1)S(1)}, bf16[2,3,64,256]{3,2,1,0:T(8,128)(2,1)S(1)}, u32[]{:S(2)}, u32[]{:S(2)}) collective-permute-start(bf16[2,3,64,256]{3,2,1,0:T(8,128)(2,1)S(1)} %constant_dynamic-update-slice_fusion.2), channel_id=1, source_target_pairs={{0,16},{1,9},{2,18},{3,11},{4,20},{5,13},{6,22},{7,15},{8,24},{9,1... | collective-permute-start | bytes 589832 | tf_op jit(solution)/shard_map/ppermute | solution.py:563
  34.3 4.3 %collective-permute-start.8 = (bf16[8,3,64,256]{3,2,1,0:T(8,128)(2,1)S(1)}, bf16[8,3,64,256]{3,2,1,0:T(8,128)(2,1)S(1)}, u32[]{:S(2)}, u32[]{:S(2)}) collective-permute-start(bf16[8,3,64,256]{3,2,1,0:T(8,128)(2,1)S(1)} %constant_dynamic-update-slice_fusion.4.rest_0_), channel_id=1, source_target_pairs={{0,1},{1,0},{2,3},{3,2},{4,5},{5,4},{6,7},{7,6},{8,9},{9,8},{10,11... | collective-permute-start | bytes 2359304 | tf_op jit(solution)/shard_map/ppermute | solution.py:571
  34.4 13.1 %collective-permute-start.7 = (bf16[8,3,64,256]{3,2,1,0:T(8,128)(2,1)S(1)}, bf16[8,3,64,256]{3,2,1,0:T(8,128)(2,1)S(1)}, u32[]{:S(2)}, u32[]{:S(2)}) collective-permute-start(bf16[8,3,64,256]{3,2,1,0:T(8,128)(2,1)S(1)} %constant_dynamic-update-slice_fusion.4.rest_0_), channel_id=1, source_target_pairs={{0,2},{1,5},{2,0},{3,7},{4,6},{5,1},{6,4},{7,3},{8,10},{9,13},{10,... | collective-permute-start | bytes 2359304 | tf_op jit(solution)/shard_map/ppermute | solution.py:563
  47.5 17.3 %collective-permute-start.11 = (bf16[1,64,2048]{2,1,0:T(8,128)(2,1)S(1)}, bf16[1,64,2048]{2,1,0:T(8,128)(2,1)S(1)}, u32[]{:S(2)}, u32[]{:S(2)}) collective-permute-start(bf16[1,64,2048]{2,1,0:T(8,128)(2,1)S(1)} %maximum_bitcast_fusion), channel_id=1, source_target_pairs={{0,8},{1,17},{2,10},{3,19},{4,12},{5,21},{6,14},{7,23},{8,0},{9,25... | collective-permute-start | bytes 786440 | tf_op jit(solution)/shard_map/ppermute | solution.py:563
  49.0 15.8 %collective-permute-start.10 = (bf16[4,3,64,256]{3,2,1,0:T(8,128)(2,1)S(1)}, bf16[4,3,64,256]{3,2,1,0:T(8,128)(2,1)S(1)}, u32[]{:S(2)}, u32[]{:S(2)}) collective-permute-start(bf16[4,3,64,256]{3,2,1,0:T(8,128)(2,1)S(1)} %pad_maximum_fusion), channel_id=1, source_target_pairs={{0,4},{1,3},{2,6},{3,1},{4,0},{5,7},{6,2},{7,5},{8,12},{9,11},{10,... | collective-permute-start | bytes 1179656 | tf_op jit(solution)/shard_map/ppermute | solution.py:563
  50.5 14.3 %collective-permute-start.9 = (bf16[8,3,64,256]{3,2,1,0:T(8,128)(2,1)S(1)}, bf16[8,3,64,256]{3,2,1,0:T(8,128)(2,1)}, u32[]{:S(2)}, u32[]{:S(2)}) collective-permute-start(bf16[8,3,64,256]{3,2,1,0:T(8,128)(2,1)S(1)} %collective-permute-done.7.rest_1_), channel_id=1, source_target_pairs={{0,1},{1,0},{2,3},{3,2},{4,5},{5,4},{6,7},{7,6},{8,9},{9,8},{10,11... | collective-permute-start | bytes 2359304 | tf_op jit(solution)/shard_map/ppermute | solution.py:571
  64.9 16.5 %collective-permute-start.13 = (bf16[8,3,64,256]{3,2,1,0:T(8,128)(2,1)S(1)}, bf16[8,3,64,256]{3,2,1,0:T(8,128)(2,1)S(1)}, u32[]{:S(2)}, u32[]{:S(2)}) collective-permute-start(bf16[8,3,64,256]{3,2,1,0:T(8,128)(2,1)S(1)} %constant_dynamic-update-slice_fusion.6.rest_0_.rest_4_), channel_id=1, source_target_pairs={{0,2},{1,5},{2,0},{3,7},{4,6},{5,1},{6,4},{7,3},{8,10},{9,13},{10,... | collective-permute-start | bytes 2359304 | tf_op jit(solution)/shard_map/ppermute | solution.py:563
  65.4 16.0 %collective-permute-start.12 = (bf16[8,3,64,256]{3,2,1,0:T(8,128)(2,1)S(1)}, bf16[8,3,64,256]{3,2,1,0:T(8,128)(2,1)}, u32[]{:S(2)}, u32[]{:S(2)}) collective-permute-start(bf16[8,3,64,256]{3,2,1,0:T(8,128)(2,1)S(1)} %constant_dynamic-update-slice_fusion.6.rest_0_.rest_4_), channel_id=1, source_target_pairs={{0,1},{1,0},{2,3},{3,2},{4,5},{5,4},{6,7},{7,6},{8,9},{9,8},{10,11... | collective-permute-start | bytes 2359304 | tf_op jit(solution)/shard_map/ppermute | solution.py:571
  65.4 30.5 %collective-permute-start.15 = (bf16[2,64,2048]{2,1,0:T(8,128)(2,1)S(1)}, bf16[2,64,2048]{2,1,0:T(8,128)(2,1)S(1)}, u32[]{:S(2)}, u32[]{:S(2)}) collective-permute-start(bf16[2,64,2048]{2,1,0:T(8,128)(2,1)S(1)} %constant_dynamic-update-slice_fusion.8), channel_id=1, source_target_pairs={{0,16},{1,9},{2,18},{3,11},{4,20},{5,13},{6,22},{7,15},{8,24},{9,1... | collective-permute-start | bytes 1572872 | tf_op jit(solution)/shard_map/ppermute | solution.py:563
  81.4 14.6 %collective-permute-start.14 = (bf16[8,3,64,256]{3,2,1,0:T(8,128)(2,1)S(1)}, bf16[8,3,64,256]{3,2,1,0:T(8,128)(2,1)S(1)}, u32[]{:S(2)}, u32[]{:S(2)}) collective-permute-start(bf16[8,3,64,256]{3,2,1,0:T(8,128)(2,1)S(1)} %collective-permute-done.13.rest_1_.rest_5_), channel_id=1, source_target_pairs={{0,1},{1,0},{2,3},{3,2},{4,5},{5,4},{6,7},{7,6},{8,9},{9,8},{10,11... | collective-permute-start | bytes 2359304 | tf_op jit(solution)/shard_map/ppermute | solution.py:571
  97.0 16.1 %collective-permute-start.16 = (bf16[4,64,2048]{2,1,0:T(8,128)(2,1)S(1)}, bf16[4,64,2048]{2,1,0:T(8,128)(2,1)S(1)}, u32[]{:S(2)}, u32[]{:S(2)}) collective-permute-start(bf16[4,64,2048]{2,1,0:T(8,128)(2,1)S(1)} %constant_dynamic-update-slice_fusion.10.rest_0_), channel_id=1, source_target_pairs={{0,4},{1,3},{2,6},{3,1},{4,0},{5,7},{6,2},{7,5},{8,12},{9,11},{10,... | collective-permute-start | bytes 3145736 | tf_op jit(solution)/shard_map/ppermute | solution.py:563
  113.0 39.3 %collective-permute-start.19 = (bf16[4,64,2048]{2,1,0:T(8,128)(2,1)S(1)}, bf16[4,64,2048]{2,1,0:T(8,128)(2,1)}, u32[]{:S(2)}, u32[]{:S(2)}) collective-permute-start(bf16[4,64,2048]{2,1,0:T(8,128)(2,1)S(1)} %constant_dynamic-update-slice_fusion.10.rest_0_), channel_id=1, source_target_pairs={{0,2},{1,5},{2,0},{3,7},{4,6},{5,1},{6,4},{7,3},{8,10},{9,13},{10,... | collective-permute-start | bytes 3145736 | tf_op jit(solution)/shard_map/ppermute | solution.py:563
  114.5 37.8 %collective-permute-start.17 = (bf16[4,64,2048]{2,1,0:T(8,128)(2,1)S(1)}, bf16[4,64,2048]{2,1,0:T(8,128)(2,1)}, u32[]{:S(2)}, u32[]{:S(2)}) collective-permute-start(bf16[4,64,2048]{2,1,0:T(8,128)(2,1)S(1)} %constant_dynamic-update-slice_fusion.10.rest_0_), channel_id=1, source_target_pairs={{0,1},{1,0},{2,3},{3,2},{4,5},{5,4},{6,7},{7,6},{8,9},{9,8},{10,11... | collective-permute-start | bytes 3145736 | tf_op jit(solution)/shard_map/ppermute | solution.py:571
  114.6 37.8 %collective-permute-start.20 = (bf16[4,64,2048]{2,1,0:T(8,128)(2,1)S(1)}, bf16[4,64,2048]{2,1,0:T(8,128)(2,1)}, u32[]{:S(2)}, u32[]{:S(2)}) collective-permute-start(bf16[4,64,2048]{2,1,0:T(8,128)(2,1)S(1)} %collective-permute-done.16.rest_1_), channel_id=1, source_target_pairs={{0,2},{1,5},{2,0},{3,7},{4,6},{5,1},{6,4},{7,3},{8,10},{9,13},{10,... | collective-permute-start | bytes 3145736 | tf_op jit(solution)/shard_map/ppermute | solution.py:563
  115.2 37.2 %collective-permute-start.18 = (bf16[4,64,2048]{2,1,0:T(8,128)(2,1)S(1)}, bf16[4,64,2048]{2,1,0:T(8,128)(2,1)}, u32[]{:S(2)}, u32[]{:S(2)}) collective-permute-start(bf16[4,64,2048]{2,1,0:T(8,128)(2,1)S(1)} %collective-permute-done.16.rest_1_), channel_id=1, source_target_pairs={{0,1},{1,0},{2,3},{3,2},{4,5},{5,4},{6,7},{7,6},{8,9},{9,8},{10,11... | collective-permute-start | bytes 3145736 | tf_op jit(solution)/shard_map/ppermute | solution.py:571
  152.4 2.9 collective-permute-start.21
  152.7 4.1 %collective-permute-start.22 = (bf16[4,64,2048]{2,1,0:T(8,128)(2,1)}, bf16[4,64,2048]{2,1,0:T(8,128)(2,1)S(1)}, u32[]{:S(2)}, u32[]{:S(2)}) collective-permute-start(bf16[4,64,2048]{2,1,0:T(8,128)(2,1)} %collective-permute-done.20.rest_3_), channel_id=1, source_target_pairs={{0,1},{1,0},{2,3},{3,2},{4,5},{5,4},{6,7},{7,6},{8,9},{9,8},{10,11... | collective-permute-start | bytes 3145736 | tf_op jit(solution)/shard_map/ppermute | solution.py:571
  302.1 1.4 collective-permute-start.23
  304.3 4.8 %collective-permute-start.26 = (f32[2,1024]{1,0:T(2,128)S(1)}, f32[2,1024]{1,0:T(2,128)S(1)}, u32[]{:S(2)}, u32[]{:S(2)}) collective-permute-start(f32[2,1024]{1,0:T(2,128)S(1)} %add.94), channel_id=1, source_target_pairs={{0,6},{2,4},{4,2},{6,0},{8,14},{10,12},{12,10},{14,8},{16,22},{18,... | collective-permute-start | bytes 24584 | tf_op jit(solution)/shard_map/ppermute | solution.py:596
  305.3 3.8 %collective-permute-start.25 = (f32[2,1024]{1,0:T(2,128)S(1)}, f32[2,1024]{1,0:T(2,128)S(1)}, u32[]{:S(2)}, u32[]{:S(2)}) collective-permute-start(f32[2,1024]{1,0:T(2,128)S(1)} %add.94), channel_id=1, source_target_pairs={{0,4},{2,6},{4,0},{6,2},{8,12},{10,14},{12,8},{14,10},{16,20},{18,... | collective-permute-start | bytes 24584 | tf_op jit(solution)/shard_map/ppermute | solution.py:596
  306.4 3.7 %collective-permute-start.24 = (f32[2,1024]{1,0:T(2,128)S(1)}, f32[2,1024]{1,0:T(2,128)S(1)}, u32[]{:S(2)}, u32[]{:S(2)}) collective-permute-start(f32[2,1024]{1,0:T(2,128)S(1)} %add.94), channel_id=1, source_target_pairs={{0,2},{2,0},{4,6},{6,4},{8,10},{10,8},{12,14},{14,12},{16,18},{18,... | collective-permute-start | bytes 24584 | tf_op jit(solution)/shard_map/ppermute | solution.py:596
  310.0 5.7 %collective-permute-start.29 = (f32[2,1024]{1,0:T(2,128)S(1)}, f32[2,1024]{1,0:T(2,128)S(1)}, u32[]{:S(2)}, u32[]{:S(2)}) collective-permute-start(f32[2,1024]{1,0:T(2,128)S(1)} %add_add_fusion.1), channel_id=1, source_target_pairs={{0,24},{2,26},{4,28},{6,30},{8,16},{10,18},{12,20},{14,22},{16,8},... | collective-permute-start | bytes 24584 | tf_op jit(solution)/shard_map/ppermute | solution.py:596
  311.9 4.5 %collective-permute-start.28 = (f32[2,1024]{1,0:T(2,128)S(1)}, f32[2,1024]{1,0:T(2,128)S(1)}, u32[]{:S(2)}, u32[]{:S(2)}) collective-permute-start(f32[2,1024]{1,0:T(2,128)S(1)} %add_add_fusion.1), channel_id=1, source_target_pairs={{0,16},{2,18},{4,20},{6,22},{8,24},{10,26},{12,28},{14,30},{16,0},... | collective-permute-start | bytes 24584 | tf_op jit(solution)/shard_map/ppermute | solution.py:596
  312.3 4.1 %collective-permute-start.27 = (f32[2,1024]{1,0:T(2,128)S(1)}, f32[2,1024]{1,0:T(2,128)S(1)}, u32[]{:S(2)}, u32[]{:S(2)}) collective-permute-start(f32[2,1024]{1,0:T(2,128)S(1)} %add_add_fusion.1), channel_id=1, source_target_pairs={{0,8},{2,10},{4,12},{6,14},{8,0},{10,2},{12,4},{14,6},{16,24},{18,... | collective-permute-start | bytes 24584 | tf_op jit(solution)/shard_map/ppermute | solution.py:596
  (14 other events, 285.3 us)
Sparse Core Ops, SparseCore 0:
  24.6 95.6 all-gather.4
  238.4 52.5 all-gather.6
